TPU v7x, 32 devices: a whole 2x2x4 slice. The times are simulated.
32 devices in a mesh: tm: 4 (over x, core), rep: 8 (over z, y).
Axes of the slice: x: 2, y: 2, z: 4, core: 2. Of those that a mesh axis runs over, the one named last changes fastest.
Arguments:
- samples: bfloat16 [8, 2048, 512], P('rep', 'tm'), may hold values from -5 to 5
- grad_out: bfloat16 [8, 2048, 512], P('rep', 'tm'), may hold values from -4 to 4
- w_conv: bfloat16 [1024, 1024], replicated, may hold values from -0.1875 to 0.1875
- w_res: bfloat16 [512, 512], replicated, may hold values from -0.25 to 0.25
- lengths: int32 [8], P('rep'), may hold values from 512 to 2048
Outputs:
- grad_in: bfloat16 [8, 2048, 512], P('rep', 'tm')
- grad_conv: float32 [1024, 1024], P('tm', 'rep')
- grad_res: float32 [512, 512], P('tm', 'rep')
All inputs are finite; a program needn't handle non-finite values.
Results may differ from a plain program's by a relative error of at most 0.015.
Values may be sent and summed in bfloat16 or wider, within the bound.
No kernel may reach another device: no remote copies, remote signals or barrier semaphores. Data moves between devices by JAX's collectives and lax.ppermute only.
A program may use at most 64 MiB of HBM per device.

v0:
```python
import jax
import jax.numpy as jnp
from jax import lax
from jax.sharding import PartitionSpec as P

DILATION_STEP = 256


def passed_along(array, axis, by):
    length = lax.axis_size(axis)
    pairs = [(i, i + by) for i in range(length) if 0 <= i + by < length]
    return lax.ppermute(array, axis, pairs)


def gate_backward(inputs, cotangent, in_length, w_conv, w_res):
    channel_count = w_res.shape[0]
    pre_act = jnp.dot(inputs, w_conv, preferred_element_type=jnp.float32)
    tanh_f = jnp.tanh(pre_act[:, :channel_count])
    sig_g = jax.nn.sigmoid(pre_act[:, channel_count:])
    gated = (in_length * tanh_f * sig_g).astype(jnp.bfloat16)
    gated_grad = in_length * jnp.dot(cotangent, w_res.T, preferred_element_type=jnp.float32)
    pre_grad = jnp.concatenate(
        [gated_grad * sig_g * (1.0 - tanh_f * tanh_f), gated_grad * tanh_f * sig_g * (1.0 - sig_g)],
        1,
    ).astype(jnp.bfloat16)
    return (gated, pre_grad)


def body(samples, grad_out, w_conv, w_res, lengths):
    sequence_rows = samples[0]
    cotangent = grad_out[0]
    seq_len = lengths[0]
    count_of_rows = sequence_rows.shape[0]
    channel_count = sequence_rows.shape[1]
    start_row = lax.axis_index("tm") * count_of_rows
    trailing_rows = sequence_rows[count_of_rows - DILATION_STEP :]
    arrived_gradient = passed_along(trailing_rows, "tm", 1)
    prior_samples = jnp.concatenate(
        [arrived_gradient, sequence_rows[: count_of_rows - DILATION_STEP]], 0
    )
    inputs = jnp.concatenate([prior_samples, sequence_rows], 1)
    in_length = (start_row + jnp.arange(count_of_rows) < seq_len).astype(jnp.float32)[:, None]
    gated, pre_grad = gate_backward(inputs, cotangent, in_length, w_conv, w_res)
    input_gradient = jnp.dot(pre_grad, w_conv.T, preferred_element_type=jnp.float32)
    incoming_gradient = passed_along(input_gradient[:DILATION_STEP, :channel_count], "tm", -1)
    delayed_gradient = jnp.concatenate(
        [input_gradient[DILATION_STEP:, :channel_count], incoming_gradient], 0
    )
    grad_rows = (
        cotangent.astype(jnp.float32) + input_gradient[:, channel_count:] + delayed_gradient
    ).astype(jnp.bfloat16)
    term_conv = jnp.einsum("tk,tn->kn", inputs, pre_grad, preferred_element_type=jnp.float32)
    term_res = jnp.einsum("tk,tn->kn", gated, cotangent, preferred_element_type=jnp.float32)
    part_conv, part_res = (
        lax.psum_scatter(
            term_conv.astype(jnp.bfloat16), "tm", scatter_dimension=0, tiled=True
        ).astype(jnp.float32),
        lax.psum_scatter(
            term_res.astype(jnp.bfloat16), "tm", scatter_dimension=0, tiled=True
        ).astype(jnp.float32),
    )
    sum_conv, sum_res = (
        lax.psum_scatter(part_conv, "rep", scatter_dimension=1, tiled=True),
        lax.psum_scatter(part_res, "rep", scatter_dimension=1, tiled=True),
    )
    all_tokens = count_of_rows * lax.axis_size("tm") * lax.axis_size("rep")
    grad_scale = float(all_tokens) ** (-0.5)
    return (grad_rows[None], sum_conv * grad_scale, sum_res * grad_scale)


def solution(mesh):
    return jax.shard_map(
        body,
        mesh=mesh,
        in_specs=(P("rep", "tm", None), P("rep", "tm", None), P(), P(), P("rep")),
        out_specs=(P("rep", "tm", None), P("tm", "rep"), P("tm", "rep")),
        check_vma=False,
    )
```

profile of v0, /device:TPU:0, one launch (start us, length us, event | category | flops | bytes accessed | tf_op | source)
XLA Modules:
  0.0 219.0 jit_solution(11050107515772439727)
XLA Ops:
  7.2 0.0 copy-start
  7.2 0.0 reduce-scatter.11.cloned.1.call-start
  7.2 1.2 slice_bitcast_fusion.1
  8.4 2.4 %collective-permute-start = (bf16[256,512]{1,0:T(8,128)(2,1)S(1)}, bf16[256,512]{1,0:T(8,128)(2,1)S(1)}, u32[]{:S(2)}, u32[]{:S(2)}) collective-permute-start(bf16[256,512]{1,0:T(8,128)(2,1)S(1)} %get-tuple-element.13), channel_id=1, source_target_pairs={{0,8},{8,16},{16,24},{1,9},{9,17},{17,25},{2,10},{10,18},{18,26},{... | collective-permute-start | bytes 786440 | tf_op jit(solution)/shard_map/ppermute | solution.py:12
  11.5 0.5 collective-permute-done
  11.9 0.0 copy-start.3
  11.9 0.0 copy-done
  11.9 0.0 copy-start.2
  11.9 2.5 %fusion.10 = f32[512,1024]{0,1:T(8,128)S(1)} fusion(bf16[1024,1024]{1,0:T(8,128)(2,1)S(1)} %copy-done, bf16[512,512]{1,0:T(8,128)(2,1)} %bitcast.23, bf16[256,512]{1,0:T(8,128)(2,1)S(1)} %get-tuple-element.14, bf16[256,512]{1,0:T(8,128)(2,1)S(1)} %collective-permute-done), kind=kOutput, calls=%fused_computation.21 | convolution fusion | flops 1076887552 | bytes 5242880 | tf_op jit(solution)/shard_map/dot_general | solution.py:17
  14.4 0.0 copy-done.3
  14.4 0.0 copy-start.8
  14.4 1.3 copy-done.8
  15.8 0.0 copy-done.2
  15.8 1.4 convolution_convert_fusion.1
  17.2 0.0 reduce-scatter.11.cloned.1.call-update
  17.2 0.0 copy-start.1
  17.2 0.0 reduce-scatter.7.cloned.1.call-start
  17.3 0.0 copy-start.4
  17.3 2.6 %multiply_convert_fusion.2 = (bf16[512,512]{0,1:T(8,128)(2,1)S(1)}, bf16[512,512]{0,1:T(8,128)(2,1)S(1)}) fusion(f32[512,1024]{0,1:T(8,128)} %copy-done.8, bf16[512,512]{1,0:T(8,128)(2,1)} %param.8, bf16[1,512,512]{2,1,0:T(8,128)(2,1)S(1)} %copy-done.2, f32[512]{0:T(512)S(1)} %fusion.11), kind=kOutput, calls=%fused_computation.15 | convolution fusion | flops 272105472 | bytes 4196352 | tf_op jit(solution)/shard_map/dot_general | solution.py:21
  19.9 0.0 copy-start.5
  19.9 0.0 copy-start.7
  19.9 0.8 copy-done.5
  20.7 0.2 copy-done.7
  20.8 0.0 copy-done.1
  20.8 0.0 copy-done.4
  20.8 2.6 %convolution_convert_fusion = bf16[1024,1024]{1,0:T(8,128)(2,1)} fusion(bf16[512,512]{0,1:T(8,128)(2,1)S(1)} %get-tuple-element.10, bf16[512,512]{0,1:T(8,128)(2,1)S(1)} %get-tuple-element.9, bf16[512,512]{1,0:T(8,128)(2,1)S(1)} %bitcast.24, bf16[256,512]{1,0:T(8,128)(2,1)S(1)} %get-tuple-element.14, bf16[256,512]{1,0:T(8,128)(2,1)S(1)} %copy-done.4), kind=kOutput, calls=%fused_computation | convolution fusion | flops 1080033280 | bytes 4194304 | tf_op jit(solution)/shard_map/tk,tn->kn/dot_general | solution.py:52
  23.5 0.0 reduce-scatter.7.cloned.1.call-update
  23.5 0.0 copy-start.6
  23.5 0.0 reduce-scatter.13.cloned.1.call-start
  23.6 22.3 %reduce-scatter.11.cloned.1.call-done = bf16[128,512]{1,0:T(8,128)(2,1)} async-done(((bf16[512,512]{1,0:T(8,128)(2,1)}), bf16[128,512]{1,0:T(8,128)(2,1)}) %reduce-scatter.11.cloned.1.call-update) | async-done | bytes 131088 | tf_op jit(solution)/shard_map/reduce_scatter | solution.py:58
  45.9 1.7 copy.15
  47.6 0.0 reduce-scatter.13.cloned.1.call-update
  47.6 0.0 reduce-scatter.9.cloned.1.call-start
  47.7 32.3 %reduce-scatter.7.cloned.1.call-done = bf16[256,1024]{1,0:T(8,128)(2,1)} async-done(((bf16[1024,1024]{1,0:T(8,128)(2,1)}), bf16[256,1024]{1,0:T(8,128)(2,1)}) %reduce-scatter.7.cloned.1.call-update) | async-done | bytes 524304 | tf_op jit(solution)/shard_map/reduce_scatter | solution.py:55
  80.0 2.1 convert_element_type.33
  82.1 0.0 reduce-scatter.9.cloned.1.call-update
  82.2 0.0 copy-done.6
  82.2 2.3 %fusion.5 = f32[512,1024]{1,0:T(8,128)S(1)} fusion(bf16[1024,1024]{1,0:T(8,128)(2,1)S(1)} %copy-done, bf16[512,512]{0,1:T(8,128)(2,1)} %copy-done.7, bf16[512,512]{0,1:T(8,128)(2,1)S(1)} %copy-done.6), kind=kOutput, calls=%fused_computation.16 | convolution fusion | flops 1075838976 | bytes 5242880 | tf_op jit(solution)/shard_map/dot_general | solution.py:44
  84.5 0.1 fusion.16
  84.6 1.3 collective-permute-start.1
  85.9 2.5 %collective-permute-done.1 = f32[256,512]{1,0:T(8,128)S(1)} collective-permute-done((f32[256,512]{1,0:T(8,128)S(1)}, f32[256,512]{1,0:T(8,128)S(1)}, u32[]{:S(2)}, u32[]{:S(2)}) %collective-permute-start.1) | collective-permute-done | bytes 524320 | tf_op jit(solution)/shard_map/ppermute | solution.py:12
  88.4 1.1 fusion.6
  89.5 55.1 %reduce-scatter.13.cloned.1.call-done = f32[64,128]{1,0:T(8,128)} async-done(((f32[512,128]{1,0:T(8,128)}), f32[64,128]{1,0:T(8,128)}) %reduce-scatter.13.cloned.1.call-update) | async-done | bytes 32784
  144.6 0.8 copy.16
  145.5 0.7 copy.13
  146.2 64.7 %reduce-scatter.9.cloned.1.call-done = f32[256,128]{1,0:T(8,128)} async-done(((f32[256,1024]{1,0:T(8,128)}), f32[256,128]{1,0:T(8,128)}) %reduce-scatter.9.cloned.1.call-update) | async-done | bytes 131088 | tf_op jit(solution)/shard_map/reduce_scatter | solution.py:63
  210.9 1.6 broadcast_multiply_fusion
  (2 shorter events, 0.0 us)
Async XLA Ops:
  7.2 4.8 %copy-start = (bf16[1024,1024]{1,0:T(8,128)(2,1)S(1)}, bf16[1024,1024]{1,0:T(8,128)(2,1)}, u32[]{:S(2)}) copy-start(bf16[1024,1024]{1,0:T(8,128)(2,1)} %param.7) | copy-start | bytes 6291460
  7.2 38.7 %reduce-scatter.11.cloned.1.call-start = ((), (), s32[]{:S(2)}) async-start(), calls=%async_computation.6 | async-start | bytes 655360 | tf_op jit(solution)/shard_map/reduce_scatter | solution.py:58
  8.4 3.5 %collective-permute-start = (bf16[256,512]{1,0:T(8,128)(2,1)S(1)}, bf16[256,512]{1,0:T(8,128)(2,1)S(1)}, u32[]{:S(2)}, u32[]{:S(2)}) collective-permute-start(bf16[256,512]{1,0:T(8,128)(2,1)S(1)} %get-tuple-element.13), channel_id=1, source_target_pairs={{0,8},{8,16},{16,24},{1,9},{9,17},{17,25},{2,10},{10,18},{18,26},{... | collective-permute-start | bytes 786440 | tf_op jit(solution)/shard_map/ppermute | solution.py:12
  11.9 2.5 %copy-start.3 = (bf16[256,512]{1,0:T(8,128)(2,1)}, bf16[256,512]{1,0:T(8,128)(2,1)S(1)}, u32[]{:S(2)}) copy-start(bf16[256,512]{1,0:T(8,128)(2,1)S(1)} %collective-permute-done) | copy-start | bytes 786436
  11.9 3.8 %copy-start.2 = (bf16[1,512,512]{2,1,0:T(8,128)(2,1)S(1)}, bf16[1,512,512]{2,1,0:T(8,128)(2,1)}, u32[]{:S(2)}) copy-start(bf16[1,512,512]{2,1,0:T(8,128)(2,1)} %param.6) | copy-start | bytes 1572868
  14.4 1.3 copy-start.8
  17.2 3.7 %copy-start.1 = (bf16[1,512,512]{2,1,0:T(8,128)(2,1)S(1)}, bf16[1,512,512]{2,1,0:T(8,128)(2,1)}, u32[]{:S(2)}) copy-start(bf16[1,512,512]{2,1,0:T(8,128)(2,1)} %param.5) | copy-start | bytes 1572868
  17.2 62.8 %reduce-scatter.7.cloned.1.call-start = ((), (), s32[]{:S(2)}) async-start(), calls=%async_computation.4 | async-start | bytes 2621440 | tf_op jit(solution)/shard_map/reduce_scatter | solution.py:55
  17.3 3.6 %copy-start.4 = (bf16[256,512]{1,0:T(8,128)(2,1)S(1)}, bf16[256,512]{1,0:T(8,128)(2,1)}, u32[]{:S(2)}) copy-start(bf16[256,512]{1,0:T(8,128)(2,1)} %copy-done.3) | copy-start | bytes 786436
  19.9 0.8 copy-start.5
  19.9 1.0 copy-start.7
  23.5 58.6 %copy-start.6 = (bf16[512,512]{0,1:T(8,128)(2,1)S(1)}, bf16[512,512]{0,1:T(8,128)(2,1)}, u32[]{:S(2)}) copy-start(bf16[512,512]{0,1:T(8,128)(2,1)} %copy-done.5) | copy-start | bytes 1572868
  23.5 121.1 %reduce-scatter.13.cloned.1.call-start = ((), (), s32[]{:S(2)}) async-start(), calls=%async_computation.7 | async-start | bytes 294912
  47.6 163.3 %reduce-scatter.9.cloned.1.call-start = ((), (), s32[]{:S(2)}) async-start(), calls=%async_computation.5 | async-start | bytes 1179648 | tf_op jit(solution)/shard_map/reduce_scatter | solution.py:63
  84.6 3.8 %collective-permute-start.1 = (f32[256,512]{1,0:T(8,128)S(1)}, f32[256,512]{1,0:T(8,128)S(1)}, u32[]{:S(2)}, u32[]{:S(2)}) collective-permute-start(f32[256,512]{1,0:T(8,128)S(1)} %get-tuple-element.12), channel_id=1, source_target_pairs={{8,0},{16,8},{24,16},{9,1},{17,9},{25,17},{10,2},{18,10},{26,18},{... | collective-permute-start | bytes 1572872 | tf_op jit(solution)/shard_map/ppermute | solution.py:12
Sparse Core Ops, SparseCore 0:
  17.3 28.5 reduce-scatter.10
  48.6 31.3 reduce-scatter.6
  83.3 61.2 reduce-scatter.12
  147.9 62.9 reduce-scatter.8
where the time goes:
time: 219 us
  waiting for transfers between devices  177 us (81%)
  between operations  14.6 us (7%)
  matrix products  11.4 us (5%)
  local copies, waits for them, and re-layouts  6.86 us (3%)
  other arithmetic  4.83 us (2%)
  starting transfers between devices  3.83 us (2%)
    reduce_scatter x1, waiting for transfers between devices, body(): lax.psum_scatter(part_conv, 'rep', scatter_dimension=1, tiled=True)  64.7 us
    unnamed x5, waiting for transfers between devices  55.1 us
    reduce_scatter x1, waiting for transfers between devices, body(): lax.psum_scatter(term_conv.astype(jnp.bfloat16), 'tm', scatter_dimension=...  32.3 us
    reduce_scatter x1, waiting for transfers between devices, body(): lax.psum_scatter(term_res.astype(jnp.bfloat16), 'tm', scatter_dimension=0...  22.3 us
    unnamed x21, local copies, waits for them, and re-layouts  5.56 us
  transfers between devices with their start and end apart: 6, of which 6 were waited for; matrix products, arithmetic and copies ran while one was open for 6% of the time, Pallas kernels for 0%

commit v1 on v0

v1 whole, which is shorter than its diff:
```python
import functools

import jax
import jax.numpy as jnp
from jax import lax
from jax.experimental import pallas as pl
from jax.experimental.pallas import tpu as pltpu
from jax.sharding import PartitionSpec as P

DILATION_STEP = 256
VMEM_GRANT = 32 * 1024 * 1024
F32, BF16 = jnp.float32, jnp.bfloat16


def dot(left, right):
    return jnp.dot(left, right, preferred_element_type=F32)


def dot_nt(left, right):
    return lax.dot_general(left, right, (((1,), (1,)), ((), ())), preferred_element_type=F32)


def gates(pre_act, gated_grad, in_length):
    channels = pre_act.shape[1] // 2
    tanh_f = jnp.tanh(pre_act[:, :channels])
    sig_g = 0.5 + 0.5 * jnp.tanh(0.5 * pre_act[:, channels:])
    both = tanh_f * sig_g
    gated = (in_length * both).astype(BF16)
    pre_f = (gated_grad * (sig_g * (1.0 - tanh_f * tanh_f))).astype(BF16)
    pre_g = (gated_grad * (both * (1.0 - sig_g))).astype(BF16)
    return gated, pre_f, pre_g


def length_mask(lengths_ref, first_row, rows, total_rows):
    start = lax.axis_index("tm") * total_rows + first_row
    at = start + lax.broadcasted_iota(jnp.int32, (rows, 1), 0)
    return (at < lengths_ref[0]).astype(F32)


def local_kernel(lengths_ref, x_ref, c_ref, wc_ref, wr_ref, xt_ref, ct_ref, cur_ref, gg_ref, pg_ref, ga_ref):
    rows, channels = x_ref.shape
    step = DILATION_STEP
    gated_grad = dot_nt(c_ref[...], wr_ref[...])
    gg_ref[...] = gated_grad[:step] * length_mask(lengths_ref, 0, step, rows)
    cur = dot(x_ref[...], wc_ref[channels:, :])
    cur_ref[...] = cur[:step]
    pre_act = cur[step:] + dot(x_ref[: rows - step, :], wc_ref[:channels, :])
    mask = length_mask(lengths_ref, step, rows - step, rows)
    gated, pre_f, pre_g = gates(pre_act, gated_grad[step:] * mask, mask)
    ga_ref[...] = gated
    pg_ref[:, :channels] = pre_f
    pg_ref[:, channels:] = pre_g
    xt_ref[...] = x_ref[...].T.reshape(xt_ref.shape)
    ct_ref[...] = c_ref[...].T


def block_products(parity, xt_ref, ht_ref, ct_ref, pg_ref, gb_ref, out_ref):
    halves, reps, height, lanes = out_ref.shape
    blocks, h, rows = xt_ref.shape
    back = ht_ref.shape[2]
    columns = pg_ref.shape[1]
    per_tap = blocks // 2
    earlier = [
        jnp.concatenate([ht_ref[2 * i + parity], xt_ref[2 * i + parity][:, : rows - back]], 1)
        for i in range(per_tap)
    ]
    current = [xt_ref[2 * i + parity] for i in range(per_tap)]
    left = jnp.concatenate(earlier + current, 0)
    wide = min(256, columns)
    for j in range(0, columns, wide):
        term = dot(left, pg_ref[:, j : j + wide]).astype(BF16)
        for t in range(halves):
            for k in range(0, wide, lanes):
                out_ref[t, (j + k) // lanes, :h, :] = term[t * h : (t + 1) * h, k : k + lanes]
    right = jnp.concatenate([gb_ref[2 * t + parity] for t in range(halves)], 1)
    term = dot(ct_ref[...], right).astype(BF16)
    low = height - h
    for t in range(halves):
        for r in range(reps):
            out_ref[t, r, h:, :] = term[r * low : (r + 1) * low, t * lanes : (t + 1) * lanes]


def partner_kernel(
    lengths_ref, halo_ref, wc_ref, xt_ref, ct_ref, cur_ref, gg_ref, pgh_ref, gah_ref,
    pg_ref, gb_ref, ht_ref, out_ref,
):
    step, channels = halo_ref.shape
    rows = pg_ref.shape[0]
    lanes = gb_ref.shape[2]
    pre_act = cur_ref[...] + dot(halo_ref[...], wc_ref[:channels, :])
    mask = length_mask(lengths_ref, 0, step, rows)
    gated, pre_f, pre_g = gates(pre_act, gg_ref[...], mask)
    pg_ref[:step, :channels] = pre_f
    pg_ref[:step, channels:] = pre_g
    pg_ref[step:, :] = pgh_ref[...]
    for t in range(gb_ref.shape[0]):
        gb_ref[t, :step, :] = gated[:, t * lanes : (t + 1) * lanes]
        gb_ref[t, step:, :] = gah_ref[:, t * lanes : (t + 1) * lanes]
    ht_ref[...] = halo_ref[...].T.reshape(ht_ref.shape)
    parity = 1 - lax.rem(lax.axis_index("tm"), 2)
    block_products(parity, xt_ref, ht_ref, ct_ref, pg_ref, gb_ref, out_ref)


def own_kernel(xt_ref, ht_ref, ct_ref, pg_ref, gb_ref, out_ref):
    parity = lax.rem(lax.axis_index("tm"), 2)
    block_products(parity, xt_ref, ht_ref, ct_ref, pg_ref, gb_ref, out_ref)


def input_kernel(pg_ref, wc_ref, c_ref, lo_ref, hi_ref, back_ref):
    step = DILATION_STEP
    rows, channels = c_ref.shape
    current = dot_nt(pg_ref[...], wc_ref[channels:, :]) + c_ref[...].astype(F32)
    earlier = dot_nt(pg_ref[...], wc_ref[:channels, :])
    back_ref[...] = earlier[:step].astype(BF16)
    lo_ref[...] = (current[: rows - step] + earlier[step:]).astype(BF16)
    hi_ref[...] = current[rows - step :]


def split_kernel(count_x, count_z, got_ref, kept_ref, *outs):
    halves, reps, height, lanes = got_ref.shape
    x = lax.axis_index("tm") // 2
    rep = lax.axis_index("rep")
    z, y = rep // 2, lax.rem(rep, 2)
    wide = outs[0].shape[1]
    for d in range(2 * count_x):
        to_x, to_y = x ^ (d // 2), y ^ (d % 2)
        for to_z in range(count_z):
            r = 2 * to_z + to_y
            part = got_ref[to_x, r, :wide, :].astype(F32) + kept_ref[to_x, r, :wide, :].astype(F32)
            outs[d][to_z] = part.astype(BF16)
    if wide == height:
        return
    for d in range(count_z):
        to_z = z ^ d
        for to_x in range(count_x):
            for to_y in range(2):
                r = 2 * to_z + to_y
                part = got_ref[to_x, r, wide:, :].astype(F32) + kept_ref[to_x, r, wide:, :].astype(F32)
                outs[2 * count_x + d][2 * to_x + to_y] = part.astype(BF16)


def total_of(refs, index):
    total = refs[0][index].astype(F32)
    for ref in refs[1:]:
        total = total + ref[index].astype(F32)
    return total


def plane_kernel(count_x, count_z, *refs):
    parts, outs = refs[: 2 * count_x], refs[2 * count_x :]
    z = lax.axis_index("rep") // 2
    for d in range(count_z):
        outs[d][...] = total_of(parts, z ^ d).astype(BF16)


def line_kernel(count_x, count_z, *refs):
    parts, outs = refs[:count_z], refs[count_z:]
    x = lax.axis_index("tm") // 2
    y = lax.rem(lax.axis_index("rep"), 2)
    for d in range(2 * count_x):
        outs[d][...] = total_of(parts, 2 * (x ^ (d // 2)) + (y ^ (d % 2))).astype(BF16)


def final_kernel(scale, count_first, *refs):
    first, second, (conv_ref, res_ref) = refs[:count_first], refs[count_first:-2], refs[-2:]
    total = total_of(first, ...)
    if second:
        total = jnp.concatenate([total, total_of(second, ...)], 0)
    total = total * scale
    height = conv_ref.shape[0]
    conv_ref[...] = total[:height]
    res_ref[...] = total[height:]


def call(kernel, out_shapes, flops, *args, name):
    specs = [
        pl.BlockSpec(memory_space=pltpu.SMEM) if a.dtype == jnp.int32 else pl.BlockSpec(memory_space=pltpu.VMEM)
        for a in args
    ]
    out_shape = [jax.ShapeDtypeStruct(shape, kind) for shape, kind in out_shapes]
    moved = sum(a.size * a.dtype.itemsize for a in list(args) + out_shape)
    return pl.pallas_call(
        kernel,
        out_shape=out_shape,
        in_specs=specs,
        out_specs=[pl.BlockSpec(memory_space=pltpu.VMEM)] * len(out_shape),
        cost_estimate=pl.CostEstimate(flops=int(flops), bytes_accessed=int(moved), transcendentals=0),
        compiler_params=pltpu.CompilerParams(vmem_limit_bytes=VMEM_GRANT),
        name=name,
    )(*args)


def body(samples, grad_out, w_conv, w_res, lengths):
    x, cot = samples[0], grad_out[0]
    rows, channels = x.shape
    step = DILATION_STEP
    tms, reps = lax.axis_size("tm"), lax.axis_size("rep")
    halves, count_z = tms // 2, reps // 2
    h, low = 2 * channels // tms, channels // reps
    lanes = channels // tms
    height = h + low
    devices = tms * reps

    def swap(array, mask):
        return lax.ppermute(array, ("tm", "rep"), [(i, i ^ mask) for i in range(devices)])

    halo = lax.ppermute(x[rows - step :], "tm", [(i, i + 1) for i in range(tms - 1)])
    xt, ct, cur, gg, pgh, gah = call(
        local_kernel,
        [
            ((tms // 2, h, rows), BF16), ((channels, rows), BF16), ((step, 2 * channels), F32),
            ((step, channels), F32), ((rows - step, 2 * channels), BF16), ((rows - step, channels), BF16),
        ],
        2 * rows * channels * channels * 4,
        lengths, x, cot, w_conv, w_res, name="local",
    )
    term = ((halves, reps, height, lanes), BF16)
    pg, gb, ht, theirs = call(
        partner_kernel,
        [((rows, 2 * channels), BF16), ((tms, rows, lanes), BF16), ((tms // 2, h, step), BF16), term],
        2 * rows * channels * channels * 4,
        lengths, halo, w_conv, xt, ct, cur, gg, pgh, gah, name="partner",
    )
    got = swap(theirs, reps)
    (mine,) = call(own_kernel, [term], 2 * rows * channels * channels * 3, xt, ht, ct, pg, gb, name="own")

    narrow = (height * 6 // 17) // 16 * 16
    wide = height - narrow
    plane = ((count_z, wide, lanes), BF16)
    line = ((2 * halves, narrow, lanes), BF16)
    parts = call(
        functools.partial(split_kernel, halves, count_z),
        [plane] * (2 * halves) + [line] * count_z,
        term[0][0] * reps * height * lanes,
        got, mine, name="split",
    )
    plane_masks = [(d // 2) * 2 * reps + d % 2 for d in range(2 * halves)]
    line_masks = [2 * d for d in range(count_z)]
    planes = [swap(p, m) if m else p for p, m in zip(parts[: 2 * halves], plane_masks)]
    lines = [swap(p, m) if m else p for p, m in zip(parts[2 * halves :], line_masks)]
    lo, hi, back = call(
        input_kernel,
        [((rows - step, channels), BF16), ((step, channels), F32), ((step, channels), BF16)],
        2 * rows * channels * channels * 4,
        pg, w_conv, cot, name="input",
    )
    parts = call(
        functools.partial(plane_kernel, halves, count_z),
        [(plane[0][1:], BF16)] * count_z, height * lanes * 16, *planes, name="plane",
    )
    firsts = [swap(p, m) if m else p for p, m in zip(parts, line_masks)]
    parts = call(
        functools.partial(line_kernel, halves, count_z),
        [(line[0][1:], BF16)] * (2 * halves), height * lanes * 16, *lines, name="line",
    )
    seconds = [swap(p, m) if m else p for p, m in zip(parts, plane_masks)]
    back = lax.ppermute(back, "tm", [(i + 1, i) for i in range(tms - 1)])
    grad_rows = jnp.concatenate([lo, (hi + back.astype(F32)).astype(BF16)], 0)
    scale = float(rows * devices) ** (-0.5)
    conv, res = call(
        functools.partial(final_kernel, scale, count_z),
        [((h, lanes), F32), ((low, lanes), F32)], height * lanes * 8, *firsts, *seconds, name="final",
    )
    return grad_rows[None], conv, res.T


def solution(mesh):
    return jax.shard_map(
        body,
        mesh=mesh,
        in_specs=(P("rep", "tm", None), P("rep", "tm", None), P(), P(), P("rep")),
        out_specs=(P("rep", "tm", None), P("tm", "rep"), P("tm", "rep")),
        check_vma=False,
    )
```

time: 219 us -> 51.2 us (0.23)
  waiting for transfers between devices: 177 us -> 11.7 us
  starting transfers between devices: 3.83 us -> 24.7 us
  between operations: 14.6 us -> 1.4 us
  matrix products: 11.4 us -> 0 us
  Pallas kernels: 0 us -> 6.34 us
  other arithmetic: 4.83 us -> 0.9 us
    reduce_scatter x3 -> x0, waiting for transfers between devices: 119 us -> none  [the longest x1 64.7 us: body(): lax.psum_scatter(part_conv, 'rep', scatter_dimension=1, tiled=True)]
    unnamed x5 -> x0, waiting for transfers between devices: 55.1 us -> none
    ppermute x2 -> x15, starting transfers between devices: 3.66 us -> 24.7 us  [the longest x13 21 us: swap(): lax.ppermute(array, ('tm', 'rep'), [(i, i ^ mask) for i in range(devices)])]
    dot_general x5 -> x0, matrix products: 11.4 us -> none  [the longest x1 2.65 us: body(): jnp.einsum('tk,tn->kn', inputs, pre_grad, preferred_element_type=jnp.floa...]
    ppermute x2 -> x15, waiting for transfers between devices: 2.97 us -> 11.7 us  [the longest x13 11.7 us: swap(): lax.ppermute(array, ('tm', 'rep'), [(i, i ^ mask) for i in range(devices)])]
    pallas_call x0 -> x8, Pallas kernels: none -> 6.34 us  [call(): pl.pallas_call(kernel, out_shape=out_shape, in_specs=specs, out_specs=[pl...]
    unnamed x21 -> x12, local copies, waits for them, and re-layouts: 5.56 us -> 4.81 us
  transfers between devices with their start and end apart: 6 -> 15, of which waited for: 6 -> 3; matrix products, arithmetic and copies ran while one was open for 6% -> 2% of each run, Pallas kernels for 0% -> 8%
where the time goes in v1:
time: 51.2 us; the launch traced here: 50.8 us
  starting transfers between devices  24.7 us (48%)
  waiting for transfers between devices  11.7 us (23%)
  Pallas kernels  6.34 us (12%)
  local copies, waits for them, and re-layouts  5.78 us (11%)
  between operations  1.4 us (3%)
  other arithmetic  0.9 us (2%)
    ppermute x13, starting transfers between devices, swap(): lax.ppermute(array, ('tm', 'rep'), [(i, i ^ mask) for i in range(devices)])  21 us
    ppermute x13, waiting for transfers between devices, swap(): lax.ppermute(array, ('tm', 'rep'), [(i, i ^ mask) for i in range(devices)])  11.7 us
    pallas_call x8, Pallas kernels, call(): pl.pallas_call(kernel, out_shape=out_shape, in_specs=specs, out_specs=[pl...  6.34 us
    unnamed x12, local copies, waits for them, and re-layouts  4.81 us
    ppermute x1, starting transfers between devices, body(): lax.ppermute(x[rows - step:], 'tm', [(i, i + 1) for i in range(tms - 1)])  2.37 us
    ppermute x1, starting transfers between devices, body(): back = lax.ppermute(back, 'tm', [(i + 1, i) for i in range(tms - 1)])  1.29 us
  transfers between devices with their start and end apart: 15, of which 3 were waited for; matrix products, arithmetic and copies ran while one was open for 2% of the time, Pallas kernels for 8%

profile of v1, /device:TPU:0, one launch (start us, length us, event | category | flops | bytes accessed | tf_op | source)
XLA Modules:
  0.0 50.8 jit_solution(12474808502235040318)
XLA Ops:
  0.6 1.0 %slice_bitcast_fusion = bf16[256,512]{1,0:T(8,128)(2,1)S(1)} fusion(bf16[1,512,512]{2,1,0:T(8,128)(2,1)} %param.5), kind=kLoop, calls=%fused_computation.2 | loop fusion | bytes 524288 | tf_op jit(solution)/shard_map/slice | solution.py:207
  1.6 2.4 %collective-permute-start = (bf16[256,512]{1,0:T(8,128)(2,1)S(1)}, bf16[256,512]{1,0:T(8,128)(2,1)S(1)}, u32[]{:S(2)}, u32[]{:S(2)}) collective-permute-start(bf16[256,512]{1,0:T(8,128)(2,1)S(1)} %slice_bitcast_fusion), channel_id=1, source_target_pairs={{0,8},{8,16},{16,24},{1,9},{9,17},{17,25},{2,10},{10,18},{18,26},{... | collective-permute-start | bytes 786440 | tf_op jit(solution)/shard_map/ppermute | solution.py:207
  4.6 0.0 copy-start
  4.6 1.6 %copy-done = bf16[1024,1024]{1,0:T(8,128)(2,1)S(1)} copy-done((bf16[1024,1024]{1,0:T(8,128)(2,1)S(1)}, bf16[1024,1024]{1,0:T(8,128)(2,1)}, u32[]{:S(2)}) %copy-start) | copy-done | bytes 2097176
  6.2 0.0 copy-start.2
  6.2 1.0 %copy-done.2 = bf16[1,512,512]{2,1,0:T(8,128)(2,1)S(1)} copy-done((bf16[1,512,512]{2,1,0:T(8,128)(2,1)S(1)}, bf16[1,512,512]{2,1,0:T(8,128)(2,1)}, u32[]{:S(2)}) %copy-start.2) | copy-done | bytes 524312
  7.3 0.0 copy-start.3
  7.3 1.0 %copy-done.3 = bf16[512,512]{1,0:T(8,128)(2,1)S(1)} copy-done((bf16[512,512]{1,0:T(8,128)(2,1)S(1)}, bf16[512,512]{1,0:T(8,128)(2,1)}, u32[]{:S(2)}) %copy-start.3) | copy-done | bytes 524312
  8.3 0.0 copy-start.4
  8.3 1.0 %copy-done.4 = bf16[1,512,512]{2,1,0:T(8,128)(2,1)S(1)} copy-done((bf16[1,512,512]{2,1,0:T(8,128)(2,1)S(1)}, bf16[1,512,512]{2,1,0:T(8,128)(2,1)}, u32[]{:S(2)}) %copy-start.4) | copy-done | bytes 524312
  9.4 0.0 copy-start.1
  9.4 1.5 %local.1 = (bf16[2,256,512]{2,1,0:T(8,128)(2,1)S(1)}, bf16[512,512]{1,0:T(8,128)(2,1)S(1)}, f32[256,1024]{1,0:T(8,128)S(1)}, f32[256,512]{1,0:T(8,128)S(1)}, bf1...) custom-call(s32[1]{0:T(128)S(6)} %copy.8.lengths_ref, bf16[512,512]{1,0:T(8,128)(2,1)S(1)} %bitcast.7, ...), custom_call_target="tpu_custom_call" | custom-call | flops 1073741824 | bytes 7077892 | tf_op jit(solution)/shard_map/local/pallas_call | solution.py:182
  10.8 0.0 collective-permute-done.halo_ref
  10.9 0.1 copy-done.1
  10.9 0.0 copy-start.5
  10.9 1.5 %partner.1 = (bf16[512,1024]{1,0:T(8,128)(2,1)S(1)}, bf16[4,512,128]{2,1,0:T(8,128)(2,1)S(1)}, bf16[2,256,256]{2,1,0:T(8,128)(2,1)S(1)}, bf16[2,8,320,128]{3,2,1,0:T(8,128)(2,1)S(1)}) custom-call(s32[1]{0:T(128)S(6)} %copy.8.lengths_ref, bf16[256,512]{1,0:T(8,128)(2,1)S(1)} %collective-permute-done.halo_ref, bf16[1024,1024]{1,0:T(8,128)(2,1)S(1)} %copy-done.1, ...), custom_call_target="tpu_custom_call" | custom-call | flops 1073741824 | bytes 8912900 | tf_op jit(solution)/shard_map/partner/pallas_call | solution.py:182
  12.5 2.7 %collective-permute-start.2 = (bf16[2,8,320,128]{3,2,1,0:T(8,128)(2,1)S(1)}, bf16[2,8,320,128]{3,2,1,0:T(8,128)(2,1)S(1)}, u32[]{:S(2)}, u32[]{:S(2)}) collective-permute-start(bf16[2,8,320,128]{3,2,1,0:T(8,128)(2,1)S(1)} %get-tuple-element.44), channel_id=1, source_target_pairs={{0,8},{1,9},{2,10},{3,11},{4,12},{5,13},{6,14},{7,15},{8,0},{9,1},... | collective-permute-start | bytes 3932168 | tf_op jit(solution)/shard_map/ppermute | solution.py:205
  15.2 0.0 copy-done.5
  15.2 1.3 %input.1 = (bf16[256,512]{1,0:T(8,128)(2,1)S(1)}, f32[256,512]{1,0:T(8,128)S(1)}, bf16[256,512]{1,0:T(8,128)(2,1)S(1)}) custom-call(bf16[512,1024]{1,0:T(8,128)(2,1)S(1)} %get-tuple-element.40.pg_ref, bf16[1024,1024]{1,0:T(8,128)(2,1)S(1)} %copy-done.1, bf16[512,512]{1,0:T(8,128)(2,1)S(1)} %bitcast.9), custom_call_target="tpu_custom_call" | custom-call | flops 1073741824 | bytes 4718592 | tf_op jit(solution)/shard_map/input/pallas_call | solution.py:182
  16.4 1.3 %collective-permute-start.1 = (bf16[256,512]{1,0:T(8,128)(2,1)S(1)}, bf16[256,512]{1,0:T(8,128)(2,1)S(1)}, u32[]{:S(2)}, u32[]{:S(2)}) collective-permute-start(bf16[256,512]{1,0:T(8,128)(2,1)S(1)} %get-tuple-element.43), channel_id=1, source_target_pairs={{8,0},{16,8},{24,16},{9,1},{17,9},{25,17},{10,2},{18,10},{26,18},{... | collective-permute-start | bytes 786440 | tf_op jit(solution)/shard_map/ppermute | solution.py:257
  17.7 0.8 %own.1.kept_ref = bf16[2,8,320,128]{3,2,1,0:T(8,128)(2,1)S(1)} custom-call(bf16[2,256,512]{2,1,0:T(8,128)(2,1)S(1)} %get-tuple-element.34.xt_ref, bf16[2,256,256]{2,1,0:T(8,128)(2,1)S(1)} %get-tuple-element.45.ht_ref, bf16[512,512]{1,0:T(8,128)(2,1)S(1)} %get-tuple-element.35.ct_ref, bf16[512,1024]{1,0:T(8,128)(2,1)S(1)} %get-tuple-element.40.pg_ref, ...), custom_call_target="tpu_custom_call" | custom-call | flops 805306368 | bytes 4194304 | tf_op jit(solution)/shard_map/own/pallas_call | solution.py:182
  18.6 0.0 collective-permute-done.2.got_ref
  18.6 0.3 split.1
  18.9 1.6 %collective-permute-start.9 = (bf16[4,112,128]{2,1,0:T(8,128)(2,1)S(1)}, bf16[4,112,128]{2,1,0:T(8,128)(2,1)S(1)}, u32[]{:S(2)}, u32[]{:S(2)}) collective-permute-start(bf16[4,112,128]{2,1,0:T(8,128)(2,1)S(1)} %get-tuple-element.56), channel_id=1, source_target_pairs={{0,2},{1,3},{2,0},{3,1},{4,6},{5,7},{6,4},{7,5},{8,10},{9,11},{10,... | collective-permute-start | bytes 344072 | tf_op jit(solution)/shard_map/ppermute | solution.py:205
  20.6 2.6 %collective-permute-start.10 = (bf16[4,112,128]{2,1,0:T(8,128)(2,1)S(1)}, bf16[4,112,128]{2,1,0:T(8,128)(2,1)S(1)}, u32[]{:S(2)}, u32[]{:S(2)}) collective-permute-start(bf16[4,112,128]{2,1,0:T(8,128)(2,1)S(1)} %get-tuple-element.57), channel_id=1, source_target_pairs={{0,4},{1,5},{2,6},{3,7},{4,0},{5,1},{6,2},{7,3},{8,12},{9,13},{10,... | collective-permute-start | bytes 344072 | tf_op jit(solution)/shard_map/ppermute | solution.py:205
  23.2 0.2 collective-permute-start.11
  23.4 1.5 %collective-permute-start.3 = (bf16[4,208,128]{2,1,0:T(8,128)(2,1)S(1)}, bf16[4,208,128]{2,1,0:T(8,128)(2,1)S(1)}, u32[]{:S(2)}, u32[]{:S(2)}) collective-permute-start(bf16[4,208,128]{2,1,0:T(8,128)(2,1)S(1)} %get-tuple-element.48), channel_id=1, source_target_pairs={{0,1},{1,0},{2,3},{3,2},{4,5},{5,4},{6,7},{7,6},{8,9},{9,8},{10,11... | collective-permute-start | bytes 638984 | tf_op jit(solution)/shard_map/ppermute | solution.py:205
  24.9 0.0 collective-permute-done.9.refs_1_
  24.9 2.4 %collective-permute-start.4 = (bf16[4,208,128]{2,1,0:T(8,128)(2,1)S(1)}, bf16[4,208,128]{2,1,0:T(8,128)(2,1)S(1)}, u32[]{:S(2)}, u32[]{:S(2)}) collective-permute-start(bf16[4,208,128]{2,1,0:T(8,128)(2,1)S(1)} %get-tuple-element.49), channel_id=1, source_target_pairs={{0,16},{1,17},{2,18},{3,19},{4,20},{5,21},{6,22},{7,23},{8,24},{9,... | collective-permute-start | bytes 638984 | tf_op jit(solution)/shard_map/ppermute | solution.py:205
  27.3 5.2 %collective-permute-done.10.refs_2_ = bf16[4,112,128]{2,1,0:T(8,128)(2,1)S(1)} collective-permute-done((bf16[4,112,128]{2,1,0:T(8,128)(2,1)S(1)}, bf16[4,112,128]{2,1,0:T(8,128)(2,1)S(1)}, u32[]{:S(2)}, u32[]{:S(2)}) %collective-permute-start.10) | collective-permute-done | bytes 114720 | tf_op jit(solution)/shard_map/ppermute | solution.py:205
  32.5 2.0 %collective-permute-start.5 = (bf16[4,208,128]{2,1,0:T(8,128)(2,1)S(1)}, bf16[4,208,128]{2,1,0:T(8,128)(2,1)S(1)}, u32[]{:S(2)}, u32[]{:S(2)}) collective-permute-start(bf16[4,208,128]{2,1,0:T(8,128)(2,1)S(1)} %get-tuple-element.50), channel_id=1, source_target_pairs={{0,17},{1,16},{2,19},{3,18},{4,21},{5,20},{6,23},{7,22},{8,25},{9,... | collective-permute-start | bytes 638984 | tf_op jit(solution)/shard_map/ppermute | solution.py:205
  34.5 0.0 collective-permute-done.11.refs_3_
  34.5 0.1 line.1
  34.5 0.6 %collective-permute-start.12 = (bf16[112,128]{1,0:T(8,128)(2,1)S(1)}, bf16[112,128]{1,0:T(8,128)(2,1)S(1)}, u32[]{:S(2)}, u32[]{:S(2)}) collective-permute-start(bf16[112,128]{1,0:T(8,128)(2,1)S(1)} %get-tuple-element.60), channel_id=1, source_target_pairs={{0,1},{1,0},{2,3},{3,2},{4,5},{5,4},{6,7},{7,6},{8,9},{9,8},{10,11... | collective-permute-start | bytes 86024 | tf_op jit(solution)/shard_map/ppermute | solution.py:205
  35.1 0.0 collective-permute-done.1
  35.1 0.1 add_convert_fusion
  35.2 1.0 %collective-permute-start.13 = (bf16[112,128]{1,0:T(8,128)(2,1)S(1)}, bf16[112,128]{1,0:T(8,128)(2,1)S(1)}, u32[]{:S(2)}, u32[]{:S(2)}) collective-permute-start(bf16[112,128]{1,0:T(8,128)(2,1)S(1)} %get-tuple-element.61), channel_id=1, source_target_pairs={{0,16},{1,17},{2,18},{3,19},{4,20},{5,21},{6,22},{7,23},{8,24},{9,... | collective-permute-start | bytes 86024 | tf_op jit(solution)/shard_map/ppermute | solution.py:205
  36.2 0.0 collective-permute-done.3.refs_1_
  36.2 2.0 %collective-permute-start.14 = (bf16[112,128]{1,0:T(8,128)(2,1)S(1)}, bf16[112,128]{1,0:T(8,128)(2,1)S(1)}, u32[]{:S(2)}, u32[]{:S(2)}) collective-permute-start(bf16[112,128]{1,0:T(8,128)(2,1)S(1)} %get-tuple-element.62), channel_id=1, source_target_pairs={{0,17},{1,16},{2,19},{3,18},{4,21},{5,20},{6,23},{7,22},{8,25},{9,... | collective-permute-start | bytes 86024 | tf_op jit(solution)/shard_map/ppermute | solution.py:205
  38.2 0.0 collective-permute-done.4.refs_2_
  38.2 2.8 %collective-permute-done.5.refs_3_ = bf16[4,208,128]{2,1,0:T(8,128)(2,1)S(1)} collective-permute-done((bf16[4,208,128]{2,1,0:T(8,128)(2,1)S(1)}, bf16[4,208,128]{2,1,0:T(8,128)(2,1)S(1)}, u32[]{:S(2)}, u32[]{:S(2)}) %collective-permute-start.5) | collective-permute-done | bytes 213024 | tf_op jit(solution)/shard_map/ppermute | solution.py:205
  41.0 0.1 plane.1
  41.1 0.1 collective-permute-start.6
  41.2 3.0 %collective-permute-start.7 = (bf16[208,128]{1,0:T(8,128)(2,1)S(1)}, bf16[208,128]{1,0:T(8,128)(2,1)S(1)}, u32[]{:S(2)}, u32[]{:S(2)}) collective-permute-start(bf16[208,128]{1,0:T(8,128)(2,1)S(1)} %get-tuple-element.53), channel_id=1, source_target_pairs={{0,4},{1,5},{2,6},{3,7},{4,0},{5,1},{6,2},{7,3},{8,12},{9,13},{10,... | collective-permute-start | bytes 159752 | tf_op jit(solution)/shard_map/ppermute | solution.py:205
  44.2 0.0 collective-permute-done.12.refs_5_
  44.2 1.3 %collective-permute-start.8 = (bf16[208,128]{1,0:T(8,128)(2,1)S(1)}, bf16[208,128]{1,0:T(8,128)(2,1)S(1)}, u32[]{:S(2)}, u32[]{:S(2)}) collective-permute-start(bf16[208,128]{1,0:T(8,128)(2,1)S(1)} %get-tuple-element.54), channel_id=1, source_target_pairs={{0,6},{1,7},{2,4},{3,5},{4,2},{5,3},{6,0},{7,1},{8,14},{9,15},{10,... | collective-permute-start | bytes 159752 | tf_op jit(solution)/shard_map/ppermute | solution.py:205
  45.6 0.8 %maximum_bitcast_fusion = bf16[1,512,512]{2,1,0:T(8,128)(2,1)} fusion(bf16[256,512]{1,0:T(8,128)(2,1)S(1)} %add_convert_fusion, bf16[256,512]{1,0:T(8,128)(2,1)S(1)} %get-tuple-element.41), kind=kLoop, calls=%fused_computation | loop fusion | flops 1048576 | bytes 1048576 | tf_op jit(solution)/shard_map/broadcast_in_dim | solution.py:264
  46.4 0.0 collective-permute-done.13.refs_6_
  46.4 0.0 collective-permute-done.14.refs_7_
  46.4 0.0 collective-permute-done.6.refs_1_
  46.4 0.0 collective-permute-done.7.refs_2_
  46.4 3.7 %collective-permute-done.8.refs_3_ = bf16[208,128]{1,0:T(8,128)(2,1)S(1)} collective-permute-done((bf16[208,128]{1,0:T(8,128)(2,1)S(1)}, bf16[208,128]{1,0:T(8,128)(2,1)S(1)}, u32[]{:S(2)}, u32[]{:S(2)}) %collective-permute-start.8) | collective-permute-done | bytes 53280 | tf_op jit(solution)/shard_map/ppermute | solution.py:205
  50.1 0.7 %final.1 = (f32[256,128]{1,0:T(8,128)}, f32[64,128]{1,0:T(8,128)}) custom-call(bf16[208,128]{1,0:T(8,128)(2,1)S(1)} %get-tuple-element.51.refs_0_, bf16[208,128]{1,0:T(8,128)(2,1)S(1)} %collective-permute-done.6.refs_1_, bf16[208,128]{1,0:T(8,128)(2,1)S(1)} %collective-permute-done.7.refs_2_, bf16[208,128]{1,0:T(8,128)(2,1)S(1)} %collective-permute-done.8.refs_3_, ...), custom_call_target="tpu_custom_call" | custom-call | flops 327680 | bytes 491520 | tf_op jit(solution)/shard_map/final/pallas_call | solution.py:182
Async XLA Ops:
  1.6 9.2 %collective-permute-start = (bf16[256,512]{1,0:T(8,128)(2,1)S(1)}, bf16[256,512]{1,0:T(8,128)(2,1)S(1)}, u32[]{:S(2)}, u32[]{:S(2)}) collective-permute-start(bf16[256,512]{1,0:T(8,128)(2,1)S(1)} %slice_bitcast_fusion), channel_id=1, source_target_pairs={{0,8},{8,16},{16,24},{1,9},{9,17},{17,25},{2,10},{10,18},{18,26},{... | collective-permute-start | bytes 786440 | tf_op jit(solution)/shard_map/ppermute | solution.py:207
  4.6 1.6 %copy-start = (bf16[1024,1024]{1,0:T(8,128)(2,1)S(1)}, bf16[1024,1024]{1,0:T(8,128)(2,1)}, u32[]{:S(2)}) copy-start(bf16[1024,1024]{1,0:T(8,128)(2,1)} %wc_ref.5) | copy-start | bytes 6291460
  6.2 1.0 %copy-start.2 = (bf16[1,512,512]{2,1,0:T(8,128)(2,1)S(1)}, bf16[1,512,512]{2,1,0:T(8,128)(2,1)}, u32[]{:S(2)}) copy-start(bf16[1,512,512]{2,1,0:T(8,128)(2,1)} %param.5) | copy-start | bytes 1572868
  7.3 1.0 %copy-start.3 = (bf16[512,512]{1,0:T(8,128)(2,1)S(1)}, bf16[512,512]{1,0:T(8,128)(2,1)}, u32[]{:S(2)}) copy-start(bf16[512,512]{1,0:T(8,128)(2,1)} %wr_ref.1) | copy-start | bytes 1572868
  8.3 1.0 %copy-start.4 = (bf16[1,512,512]{2,1,0:T(8,128)(2,1)S(1)}, bf16[1,512,512]{2,1,0:T(8,128)(2,1)}, u32[]{:S(2)}) copy-start(bf16[1,512,512]{2,1,0:T(8,128)(2,1)} %param.6) | copy-start | bytes 1572868
  9.4 1.6 %copy-start.1 = (bf16[1024,1024]{1,0:T(8,128)(2,1)S(1)}, bf16[1024,1024]{1,0:T(8,128)(2,1)}, u32[]{:S(2)}) copy-start(bf16[1024,1024]{1,0:T(8,128)(2,1)} %wc_ref.5) | copy-start | bytes 6291460
  10.9 4.2 %copy-start.5 = (bf16[1,512,512]{2,1,0:T(8,128)(2,1)S(1)}, bf16[1,512,512]{2,1,0:T(8,128)(2,1)}, u32[]{:S(2)}) copy-start(bf16[1,512,512]{2,1,0:T(8,128)(2,1)} %param.6) | copy-start | bytes 1572868
  12.5 6.1 %collective-permute-start.2 = (bf16[2,8,320,128]{3,2,1,0:T(8,128)(2,1)S(1)}, bf16[2,8,320,128]{3,2,1,0:T(8,128)(2,1)S(1)}, u32[]{:S(2)}, u32[]{:S(2)}) collective-permute-start(bf16[2,8,320,128]{3,2,1,0:T(8,128)(2,1)S(1)} %get-tuple-element.44), channel_id=1, source_target_pairs={{0,8},{1,9},{2,10},{3,11},{4,12},{5,13},{6,14},{7,15},{8,0},{9,1},... | collective-permute-start | bytes 3932168 | tf_op jit(solution)/shard_map/ppermute | solution.py:205
  16.4 18.7 %collective-permute-start.1 = (bf16[256,512]{1,0:T(8,128)(2,1)S(1)}, bf16[256,512]{1,0:T(8,128)(2,1)S(1)}, u32[]{:S(2)}, u32[]{:S(2)}) collective-permute-start(bf16[256,512]{1,0:T(8,128)(2,1)S(1)} %get-tuple-element.43), channel_id=1, source_target_pairs={{8,0},{16,8},{24,16},{9,1},{17,9},{25,17},{10,2},{18,10},{26,18},{... | collective-permute-start | bytes 786440 | tf_op jit(solution)/shard_map/ppermute | solution.py:257
  18.9 6.0 %collective-permute-start.9 = (bf16[4,112,128]{2,1,0:T(8,128)(2,1)S(1)}, bf16[4,112,128]{2,1,0:T(8,128)(2,1)S(1)}, u32[]{:S(2)}, u32[]{:S(2)}) collective-permute-start(bf16[4,112,128]{2,1,0:T(8,128)(2,1)S(1)} %get-tuple-element.56), channel_id=1, source_target_pairs={{0,2},{1,3},{2,0},{3,1},{4,6},{5,7},{6,4},{7,5},{8,10},{9,11},{10,... | collective-permute-start | bytes 344072 | tf_op jit(solution)/shard_map/ppermute | solution.py:205
  20.6 11.9 %collective-permute-start.10 = (bf16[4,112,128]{2,1,0:T(8,128)(2,1)S(1)}, bf16[4,112,128]{2,1,0:T(8,128)(2,1)S(1)}, u32[]{:S(2)}, u32[]{:S(2)}) collective-permute-start(bf16[4,112,128]{2,1,0:T(8,128)(2,1)S(1)} %get-tuple-element.57), channel_id=1, source_target_pairs={{0,4},{1,5},{2,6},{3,7},{4,0},{5,1},{6,2},{7,3},{8,12},{9,13},{10,... | collective-permute-start | bytes 344072 | tf_op jit(solution)/shard_map/ppermute | solution.py:205
  23.2 11.3 %collective-permute-start.11 = (bf16[4,112,128]{2,1,0:T(8,128)(2,1)S(1)}, bf16[4,112,128]{2,1,0:T(8,128)(2,1)S(1)}, u32[]{:S(2)}, u32[]{:S(2)}) collective-permute-start(bf16[4,112,128]{2,1,0:T(8,128)(2,1)S(1)} %get-tuple-element.58), channel_id=1, source_target_pairs={{0,6},{1,7},{2,4},{3,5},{4,2},{5,3},{6,0},{7,1},{8,14},{9,15},{10,... | collective-permute-start | bytes 344072 | tf_op jit(solution)/shard_map/ppermute | solution.py:205
  23.4 12.8 %collective-permute-start.3 = (bf16[4,208,128]{2,1,0:T(8,128)(2,1)S(1)}, bf16[4,208,128]{2,1,0:T(8,128)(2,1)S(1)}, u32[]{:S(2)}, u32[]{:S(2)}) collective-permute-start(bf16[4,208,128]{2,1,0:T(8,128)(2,1)S(1)} %get-tuple-element.48), channel_id=1, source_target_pairs={{0,1},{1,0},{2,3},{3,2},{4,5},{5,4},{6,7},{7,6},{8,9},{9,8},{10,11... | collective-permute-start | bytes 638984 | tf_op jit(solution)/shard_map/ppermute | solution.py:205
  24.9 13.3 %collective-permute-start.4 = (bf16[4,208,128]{2,1,0:T(8,128)(2,1)S(1)}, bf16[4,208,128]{2,1,0:T(8,128)(2,1)S(1)}, u32[]{:S(2)}, u32[]{:S(2)}) collective-permute-start(bf16[4,208,128]{2,1,0:T(8,128)(2,1)S(1)} %get-tuple-element.49), channel_id=1, source_target_pairs={{0,16},{1,17},{2,18},{3,19},{4,20},{5,21},{6,22},{7,23},{8,24},{9,... | collective-permute-start | bytes 638984 | tf_op jit(solution)/shard_map/ppermute | solution.py:205
  32.5 8.5 %collective-permute-start.5 = (bf16[4,208,128]{2,1,0:T(8,128)(2,1)S(1)}, bf16[4,208,128]{2,1,0:T(8,128)(2,1)S(1)}, u32[]{:S(2)}, u32[]{:S(2)}) collective-permute-start(bf16[4,208,128]{2,1,0:T(8,128)(2,1)S(1)} %get-tuple-element.50), channel_id=1, source_target_pairs={{0,17},{1,16},{2,19},{3,18},{4,21},{5,20},{6,23},{7,22},{8,25},{9,... | collective-permute-start | bytes 638984 | tf_op jit(solution)/shard_map/ppermute | solution.py:205
  34.5 9.7 %collective-permute-start.12 = (bf16[112,128]{1,0:T(8,128)(2,1)S(1)}, bf16[112,128]{1,0:T(8,128)(2,1)S(1)}, u32[]{:S(2)}, u32[]{:S(2)}) collective-permute-start(bf16[112,128]{1,0:T(8,128)(2,1)S(1)} %get-tuple-element.60), channel_id=1, source_target_pairs={{0,1},{1,0},{2,3},{3,2},{4,5},{5,4},{6,7},{7,6},{8,9},{9,8},{10,11... | collective-permute-start | bytes 86024 | tf_op jit(solution)/shard_map/ppermute | solution.py:205
  35.2 11.2 %collective-permute-start.13 = (bf16[112,128]{1,0:T(8,128)(2,1)S(1)}, bf16[112,128]{1,0:T(8,128)(2,1)S(1)}, u32[]{:S(2)}, u32[]{:S(2)}) collective-permute-start(bf16[112,128]{1,0:T(8,128)(2,1)S(1)} %get-tuple-element.61), channel_id=1, source_target_pairs={{0,16},{1,17},{2,18},{3,19},{4,20},{5,21},{6,22},{7,23},{8,24},{9,... | collective-permute-start | bytes 86024 | tf_op jit(solution)/shard_map/ppermute | solution.py:205
  36.2 10.2 %collective-permute-start.14 = (bf16[112,128]{1,0:T(8,128)(2,1)S(1)}, bf16[112,128]{1,0:T(8,128)(2,1)S(1)}, u32[]{:S(2)}, u32[]{:S(2)}) collective-permute-start(bf16[112,128]{1,0:T(8,128)(2,1)S(1)} %get-tuple-element.62), channel_id=1, source_target_pairs={{0,17},{1,16},{2,19},{3,18},{4,21},{5,20},{6,23},{7,22},{8,25},{9,... | collective-permute-start | bytes 86024 | tf_op jit(solution)/shard_map/ppermute | solution.py:205
  41.1 5.3 %collective-permute-start.6 = (bf16[208,128]{1,0:T(8,128)(2,1)S(1)}, bf16[208,128]{1,0:T(8,128)(2,1)S(1)}, u32[]{:S(2)}, u32[]{:S(2)}) collective-permute-start(bf16[208,128]{1,0:T(8,128)(2,1)S(1)} %get-tuple-element.52), channel_id=1, source_target_pairs={{0,2},{1,3},{2,0},{3,1},{4,6},{5,7},{6,4},{7,5},{8,10},{9,11},{10,... | collective-permute-start | bytes 159752 | tf_op jit(solution)/shard_map/ppermute | solution.py:205
  41.2 5.2 %collective-permute-start.7 = (bf16[208,128]{1,0:T(8,128)(2,1)S(1)}, bf16[208,128]{1,0:T(8,128)(2,1)S(1)}, u32[]{:S(2)}, u32[]{:S(2)}) collective-permute-start(bf16[208,128]{1,0:T(8,128)(2,1)S(1)} %get-tuple-element.53), channel_id=1, source_target_pairs={{0,4},{1,5},{2,6},{3,7},{4,0},{5,1},{6,2},{7,3},{8,12},{9,13},{10,... | collective-permute-start | bytes 159752 | tf_op jit(solution)/shard_map/ppermute | solution.py:205
  44.2 5.9 %collective-permute-start.8 = (bf16[208,128]{1,0:T(8,128)(2,1)S(1)}, bf16[208,128]{1,0:T(8,128)(2,1)S(1)}, u32[]{:S(2)}, u32[]{:S(2)}) collective-permute-start(bf16[208,128]{1,0:T(8,128)(2,1)S(1)} %get-tuple-element.54), channel_id=1, source_target_pairs={{0,6},{1,7},{2,4},{3,5},{4,2},{5,3},{6,0},{7,1},{8,14},{9,15},{10,... | collective-permute-start | bytes 159752 | tf_op jit(solution)/shard_map/ppermute | solution.py:205

commit v2 on v1

v2 whole, which is shorter than its diff:
```python
import functools

import jax
import jax.numpy as jnp
from jax import lax
from jax.experimental import pallas as pl
from jax.experimental.pallas import tpu as pltpu
from jax.sharding import PartitionSpec as P

DILATION_STEP = 256
VMEM_GRANT = 32 * 1024 * 1024
F32, BF16 = jnp.float32, jnp.bfloat16


def dot(left, right):
    return jnp.dot(left, right, preferred_element_type=F32)


def dot_nt(left, right):
    return lax.dot_general(left, right, (((1,), (1,)), ((), ())), preferred_element_type=F32)


def gates(pre_act, gated_grad, in_length):
    channels = pre_act.shape[1] // 2
    tanh_f = jnp.tanh(pre_act[:, :channels])
    sig_g = 0.5 + 0.5 * jnp.tanh(0.5 * pre_act[:, channels:])
    both = tanh_f * sig_g
    gated = (in_length * both).astype(BF16)
    pre_f = (gated_grad * (sig_g * (1.0 - tanh_f * tanh_f))).astype(BF16)
    pre_g = (gated_grad * (both * (1.0 - sig_g))).astype(BF16)
    return gated, pre_f, pre_g


def length_mask(lengths_ref, first_row, rows, total_rows):
    start = lax.axis_index("tm") * total_rows + first_row
    at = start + lax.broadcasted_iota(jnp.int32, (rows, 1), 0)
    return (at < lengths_ref[0]).astype(F32)


def local_kernel(
    lengths_ref, x_hbm, c_hbm, wc_hbm, wr_hbm,
    xt_ref, ct_ref, cur_ref, gg_ref, pg_ref, gb_ref, wc_ref, c_ref, x_ref, wr_ref, sems,
):
    rows, channels = x_ref.shape
    step = DILATION_STEP
    lanes = gb_ref.shape[2]
    low, high = pl.ds(0, channels), pl.ds(channels, channels)
    copies = [
        pltpu.make_async_copy(source, target, sems.at[i])
        for i, (source, target) in enumerate(
            [
                (x_hbm, x_ref), (wc_hbm.at[high], wc_ref.at[high]), (wc_hbm.at[low], wc_ref.at[low]),
                (c_hbm, c_ref), (wr_hbm, wr_ref),
            ]
        )
    ]
    for copy in copies:
        copy.start()
    copies[0].wait()
    xt_ref[...] = x_ref[...].T.reshape(xt_ref.shape)
    copies[1].wait()
    cur_ref[...] = dot(x_ref[:step, :], wc_ref[channels:, :])
    pre_act = dot(x_ref[step:, :], wc_ref[channels:, :])
    copies[2].wait()
    pre_act = pre_act + dot(x_ref[: rows - step, :], wc_ref[:channels, :])
    copies[3].wait()
    copies[4].wait()
    gated_grad = dot_nt(c_ref[...], wr_ref[...])
    gg_ref[...] = gated_grad[:step] * length_mask(lengths_ref, 0, step, rows)
    mask = length_mask(lengths_ref, step, rows - step, rows)
    gated, pre_f, pre_g = gates(pre_act, gated_grad[step:] * mask, mask)
    for t in range(gb_ref.shape[0]):
        gb_ref[t, step:, :] = gated[:, t * lanes : (t + 1) * lanes]
    pg_ref[step:, :channels] = pre_f
    pg_ref[step:, channels:] = pre_g
    ct_ref[...] = c_ref[...].T


def block_products(parity, xt_ref, ht_ref, ct_ref, pg_ref, gb_ref, out_ref):
    halves, reps, height, lanes = out_ref.shape
    blocks, h, rows = xt_ref.shape
    back = ht_ref.shape[2]
    columns = pg_ref.shape[1]
    per_tap = blocks // 2
    earlier = [
        jnp.concatenate([ht_ref[2 * i + parity], xt_ref[2 * i + parity][:, : rows - back]], 1)
        for i in range(per_tap)
    ]
    current = [xt_ref[2 * i + parity] for i in range(per_tap)]
    left = jnp.concatenate(earlier + current, 0)
    wide = min(256, columns)
    for j in range(0, columns, wide):
        term = dot(left, pg_ref[:, j : j + wide]).astype(BF16)
        for t in range(halves):
            for k in range(0, wide, lanes):
                out_ref[t, (j + k) // lanes, :h, :] = term[t * h : (t + 1) * h, k : k + lanes]
    right = jnp.concatenate([gb_ref[2 * t + parity] for t in range(halves)], 1)
    term = dot(ct_ref[...], right).astype(BF16)
    low = height - h
    for t in range(halves):
        for r in range(reps):
            out_ref[t, r, h:, :] = term[r * low : (r + 1) * low, t * lanes : (t + 1) * lanes]


def partner_kernel(
    lengths_ref, halo_ref, wc_ref, xt_ref, ct_ref, cur_ref, gg_ref, pg_in, gb_in,
    pg_ref, gb_ref, ht_ref, out_ref,
):
    step, channels = halo_ref.shape
    rows = pg_ref.shape[0]
    lanes = gb_ref.shape[2]
    halo = jnp.where(lax.axis_index("tm") > 0, halo_ref[...], jnp.zeros_like(halo_ref))
    pre_act = cur_ref[...] + dot(halo, wc_ref[:channels, :])
    mask = length_mask(lengths_ref, 0, step, rows)
    gated, pre_f, pre_g = gates(pre_act, gg_ref[...], mask)
    pg_ref[:step, :channels] = pre_f
    pg_ref[:step, channels:] = pre_g
    for t in range(gb_ref.shape[0]):
        gb_ref[t, :step, :] = gated[:, t * lanes : (t + 1) * lanes]
    ht_ref[...] = halo.T.reshape(ht_ref.shape)
    parity = 1 - lax.rem(lax.axis_index("tm"), 2)
    block_products(parity, xt_ref, ht_ref, ct_ref, pg_ref, gb_ref, out_ref)


def own_kernel(xt_ref, ht_ref, ct_ref, pg_ref, gb_ref, out_ref):
    parity = lax.rem(lax.axis_index("tm"), 2)
    block_products(parity, xt_ref, ht_ref, ct_ref, pg_ref, gb_ref, out_ref)


def back_kernel(pg_ref, wc_ref, back_ref):
    step, channels = back_ref.shape
    back_ref[...] = dot_nt(pg_ref[:step, :], wc_ref[:channels, :]).astype(BF16)


def input_kernel(pg_ref, wc_ref, c_ref, arrived_ref, out_ref):
    step = DILATION_STEP
    rows, channels = c_ref.shape
    current = dot_nt(pg_ref[...], wc_ref[channels:, :]) + c_ref[...].astype(F32)
    earlier = dot_nt(pg_ref[step:, :], wc_ref[:channels, :])
    out_ref[: rows - step, :] = (current[: rows - step] + earlier).astype(BF16)
    arrived = jnp.where(lax.axis_index("tm") < lax.axis_size("tm") - 1, arrived_ref[...].astype(F32), 0.0)
    out_ref[rows - step :, :] = (current[rows - step :] + arrived).astype(BF16)


def split_kernel(count_x, count_z, got_ref, kept_ref, *outs):
    x = lax.axis_index("tm") // 2
    rep = lax.axis_index("rep")
    y = lax.rem(rep, 2)
    for d, out in enumerate(outs):
        to_x, to_y = x ^ (d // 2), y ^ (d % 2)
        for to_z in range(count_z):
            r = 2 * to_z + to_y
            out[to_z] = (got_ref[to_x, r].astype(F32) + kept_ref[to_x, r].astype(F32)).astype(BF16)


def total_of(refs, index):
    total = refs[0][index].astype(F32)
    for ref in refs[1:]:
        total = total + ref[index].astype(F32)
    return total


def plane_kernel(count_x, count_z, *refs):
    parts, outs = refs[: 2 * count_x], refs[2 * count_x :]
    z = lax.axis_index("rep") // 2
    for d in range(count_z):
        outs[d][...] = total_of(parts, z ^ d).astype(BF16)


def final_kernel(scale, *refs):
    parts, (conv_ref, res_ref) = refs[:-2], refs[-2:]
    total = total_of(parts, ...) * scale
    height = conv_ref.shape[0]
    conv_ref[...] = total[:height]
    res_ref[...] = total[height:]


def call(kernel, out_shapes, flops, *args, name, in_hbm=(), scratch=(), aliases=None):
    def spec(index, a):
        if index in in_hbm:
            return pl.BlockSpec(memory_space=pltpu.HBM)
        return pl.BlockSpec(memory_space=pltpu.SMEM if a.dtype == jnp.int32 else pltpu.VMEM)

    args = [pltpu.with_memory_space_constraint(a, pltpu.HBM) if i in in_hbm else a for i, a in enumerate(args)]
    out_shape = [jax.ShapeDtypeStruct(shape, kind) for shape, kind in out_shapes]
    moved = sum(a.size * a.dtype.itemsize for a in list(args) + out_shape)
    return pl.pallas_call(
        kernel,
        out_shape=out_shape,
        in_specs=[spec(i, a) for i, a in enumerate(args)],
        out_specs=[pl.BlockSpec(memory_space=pltpu.VMEM)] * len(out_shape),
        scratch_shapes=list(scratch),
        input_output_aliases=aliases or {},
        cost_estimate=pl.CostEstimate(flops=int(flops), bytes_accessed=int(moved), transcendentals=0),
        compiler_params=pltpu.CompilerParams(vmem_limit_bytes=VMEM_GRANT),
        name=name,
    )(*args)


def after(array, other):
    return lax.optimization_barrier((array, other))[0]


def body(samples, grad_out, w_conv, w_res, lengths):
    x, cot = samples[0], grad_out[0]
    rows, channels = x.shape
    step = DILATION_STEP
    tms, reps = lax.axis_size("tm"), lax.axis_size("rep")
    halves, count_z = tms // 2, reps // 2
    h, low = 2 * channels // tms, channels // reps
    lanes = channels // tms
    height = h + low
    devices = tms * reps
    product = 2 * rows * channels * channels

    def swap(array, mask):
        return lax.ppermute(array, ("tm", "rep"), [(i, i ^ mask) for i in range(devices)])

    halo = lax.ppermute(x[rows - step :], "tm", [(i, (i + 1) % tms) for i in range(tms)])
    whole_pg, whole_gb = ((rows, 2 * channels), BF16), ((tms, rows, lanes), BF16)
    xt, ct, cur, gg, pg, gb, wc, c = call(
        local_kernel,
        [
            ((tms // 2, h, rows), BF16), ((channels, rows), BF16), ((step, 2 * channels), F32),
            ((step, channels), F32), whole_pg, whole_gb, (w_conv.shape, BF16), (cot.shape, BF16),
        ],
        product * 4, lengths, x, cot, w_conv, w_res, name="local", in_hbm=(1, 2, 3, 4),
        scratch=[pltpu.VMEM(x.shape, BF16), pltpu.VMEM(w_res.shape, BF16), pltpu.SemaphoreType.DMA((5,))],
    )
    term = ((halves, reps, height, lanes), BF16)
    pg, gb, ht, theirs = call(
        partner_kernel,
        [whole_pg, whole_gb, ((tms // 2, h, step), BF16), term],
        product * 4, lengths, halo, wc, xt, ct, cur, gg, pg, gb, name="partner", aliases={7: 0, 8: 1},
    )
    got = swap(theirs, reps)
    (mine,) = call(own_kernel, [term], product * 3, xt, ht, ct, pg, gb, name="own")
    pg, mine = lax.optimization_barrier((pg, mine))
    (back,) = call(back_kernel, [((step, channels), BF16)], product, pg, wc, name="back")
    arrived = lax.ppermute(back, "tm", [((i + 1) % tms, i) for i in range(tms)])

    plane = ((count_z, height, lanes), BF16)
    parts = call(
        functools.partial(split_kernel, halves, count_z),
        [plane] * (2 * halves),
        term[0][0] * reps * height * lanes,
        got, mine, name="split",
    )
    plane_masks = [(d // 2) * 2 * reps + d % 2 for d in range(2 * halves)]
    line_masks = [2 * d for d in range(count_z)]
    planes = [swap(p, m) if m else p for p, m in zip(parts[: 2 * halves], plane_masks)]
    (grad_in,) = call(
        input_kernel, [((rows, channels), BF16)], product * 4, after(pg, planes[1]), wc, c, arrived, name="input",
    )
    parts = call(
        functools.partial(plane_kernel, halves, count_z),
        [(plane[0][1:], BF16)] * count_z, height * lanes * 16, *planes, name="plane",
    )
    firsts = list(parts)
    for d in list(range(2, count_z)) + [1]:
        firsts[d] = swap(firsts[d], line_masks[d])
    scale = float(rows * devices) ** (-0.5)
    conv, res = call(
        functools.partial(final_kernel, scale),
        [((h, lanes), F32), ((low, lanes), F32)], height * lanes * 8, *firsts[2:], *firsts[:2], name="final",
    )
    return grad_in[None], conv, res.T


def solution(mesh):
    return jax.shard_map(
        body,
        mesh=mesh,
        in_specs=(P("rep", "tm", None), P("rep", "tm", None), P(), P(), P("rep")),
        out_specs=(P("rep", "tm", None), P("tm", "rep"), P("tm", "rep")),
        check_vma=False,
    )
```

time: 51.2 us -> 42.2 us (0.82)
  starting transfers between devices: 24.7 us -> 10.1 us
  waiting for transfers between devices: 11.7 us -> 20.5 us
  local copies, waits for them, and re-layouts: 5.78 us -> 0.97 us
  Pallas kernels: 6.34 us -> 9.07 us
  other arithmetic: 0.9 us -> 0 us
    ppermute x13 -> x7, starting transfers between devices: 21 us -> 8.76 us  [swap(): lax.ppermute(array, ('tm', 'rep'), [(i, i ^ mask) for i in range(devices)])]
    ppermute x13 -> x7, waiting for transfers between devices: 11.7 us -> 18.5 us  [swap(): lax.ppermute(array, ('tm', 'rep'), [(i, i ^ mask) for i in range(devices)])]
    unnamed x12 -> x0, local copies, waits for them, and re-layouts: 4.81 us -> none
    pallas_call x8, Pallas kernels: 6.34 us -> 9.07 us  [call(): pl.pallas_call(kernel, out_shape=out_shape, in_specs=[spec(i, a) for i, a...]
    ppermute x2, starting transfers between devices: 3.66 us -> 1.38 us  [the longest x1 0.87 us: body(): arrived = lax.ppermute(back, 'tm', [((i + 1) % tms, i) for i in range(tms)])]
    ppermute x2, waiting for transfers between devices: 0.01 us -> 2.05 us  [the longest x1 2.04 us: body(): lax.ppermute(x[rows - step:], 'tm', [(i, (i + 1) % tms) for i in range(tm...]
    broadcast_in_dim x1 -> x0, other arithmetic: 0.83 us -> none  [body(): return (grad_rows[None], conv, res.T)]
  transfers between devices with their start and end apart: 15 -> 9, of which waited for: 3 -> 8; matrix products, arithmetic and copies ran while one was open for 2% -> 0% of each run, Pallas kernels for 8% -> 16%
where the time goes in v2:
time: 42.2 us; the launch traced here: 42 us
  waiting for transfers between devices  20.5 us (49%)
  starting transfers between devices  10.1 us (24%)
  Pallas kernels  9.07 us (21%)
  between operations  1.33 us (3%)
  local copies, waits for them, and re-layouts  0.97 us (2%)
    ppermute x7, waiting for transfers between devices, swap(): lax.ppermute(array, ('tm', 'rep'), [(i, i ^ mask) for i in range(devices)])  18.5 us
    pallas_call x8, Pallas kernels, call(): pl.pallas_call(kernel, out_shape=out_shape, in_specs=[spec(i, a) for i, a...  9.07 us
    ppermute x7, starting transfers between devices, swap(): lax.ppermute(array, ('tm', 'rep'), [(i, i ^ mask) for i in range(devices)])  8.76 us
    ppermute x1, waiting for transfers between devices, body(): lax.ppermute(x[rows - step:], 'tm', [(i, (i + 1) % tms) for i in range(tm...  2.04 us
    slice x1, local copies, waits for them, and re-layouts, body(): x[rows - step:]  0.97 us
    ppermute x1, starting transfers between devices, body(): arrived = lax.ppermute(back, 'tm', [((i + 1) % tms, i) for i in range(tms)])  0.87 us
  transfers between devices with their start and end apart: 9, of which 8 were waited for; matrix products, arithmetic and copies ran while one was open for 0% of the time, Pallas kernels for 16%

profile of v2, /device:TPU:0, one launch (start us, length us, event | category | flops | bytes accessed | tf_op | source)
XLA Modules:
  0.0 42.0 jit_solution(16366139673965063233)
XLA Ops:
  0.6 1.0 %slice_bitcast_fusion = bf16[256,512]{1,0:T(8,128)(2,1)S(1)} fusion(bf16[1,512,512]{2,1,0:T(8,128)(2,1)} %param.5), kind=kLoop, calls=%fused_computation | loop fusion | bytes 524288 | tf_op jit(solution)/shard_map/slice | solution.py:219
  1.6 0.5 %collective-permute-start = (bf16[256,512]{1,0:T(8,128)(2,1)S(1)}, bf16[256,512]{1,0:T(8,128)(2,1)S(1)}, u32[]{:S(2)}, u32[]{:S(2)}) collective-permute-start(bf16[256,512]{1,0:T(8,128)(2,1)S(1)} %slice_bitcast_fusion), channel_id=1, source_target_pairs={{0,8},{8,16},{16,24},{24,0},{1,9},{9,17},{17,25},{25,1},{2,10},{10... | collective-permute-start | bytes 786440 | tf_op jit(solution)/shard_map/ppermute | solution.py:219
  2.8 3.3 %local.1 = (bf16[2,256,512]{2,1,0:T(8,128)(2,1)S(1)}, bf16[512,512]{1,0:T(8,128)(2,1)S(1)}, f32[256,1024]{1,0:T(8,128)S(1)}, f32[256,512]{1,0:T(8,128)S(1)}, bf1...) custom-call(s32[1]{0:T(128)S(6)} %copy.12.lengths_ref, ...), custom_call_target="tpu_custom_call" | custom-call | flops 1073741824 | bytes 10485764 | tf_op jit(solution)/shard_map/local/pallas_call | solution.py:187
  6.0 2.0 %collective-permute-done.halo_ref = bf16[256,512]{1,0:T(8,128)(2,1)S(1)} collective-permute-done((bf16[256,512]{1,0:T(8,128)(2,1)S(1)}, bf16[256,512]{1,0:T(8,128)(2,1)S(1)}, u32[]{:S(2)}, u32[]{:S(2)}) %collective-permute-start) | collective-permute-done | bytes 262176 | tf_op jit(solution)/shard_map/ppermute | solution.py:219
  8.1 1.5 %partner.1 = (bf16[512,1024]{1,0:T(8,128)(2,1)S(1)}, bf16[4,512,128]{2,1,0:T(8,128)(2,1)S(1)}, bf16[2,256,256]{2,1,0:T(8,128)(2,1)S(1)}, bf16[2,8,320,128]{3,2,1,0:T(8,128)(2,1)S(1)}) custom-call(s32[1]{0:T(128)S(6)} %copy.12.lengths_ref, bf16[256,512]{1,0:T(8,128)(2,1)S(1)} %collective-permute-done.halo_ref, ...), custom_call_target="tpu_custom_call", output_to_operand_aliasing={{0}: (7, {}), {1}: (8, {})} | custom-call | flops 1073741824 | bytes 9699332 | tf_op jit(solution)/shard_map/partner/pallas_call | solution.py:187
  9.6 0.6 %collective-permute-start.1 = (bf16[2,8,320,128]{3,2,1,0:T(8,128)(2,1)S(1)}, bf16[2,8,320,128]{3,2,1,0:T(8,128)(2,1)S(1)}, u32[]{:S(2)}, u32[]{:S(2)}) collective-permute-start(bf16[2,8,320,128]{3,2,1,0:T(8,128)(2,1)S(1)} %get-tuple-element.39), channel_id=1, source_target_pairs={{0,8},{1,9},{2,10},{3,11},{4,12},{5,13},{6,14},{7,15},{8,0},{9,1},... | collective-permute-start | bytes 3932168 | tf_op jit(solution)/shard_map/ppermute | solution.py:217
  10.2 0.8 %own.1.kept_ref = bf16[2,8,320,128]{3,2,1,0:T(8,128)(2,1)S(1)} custom-call(bf16[2,256,512]{2,1,0:T(8,128)(2,1)S(1)} %get-tuple-element.29.xt_ref, bf16[2,256,256]{2,1,0:T(8,128)(2,1)S(1)} %get-tuple-element.36.ht_ref, bf16[512,512]{1,0:T(8,128)(2,1)S(1)} %get-tuple-element.30.ct_ref, bf16[512,1024]{1,0:T(8,128)(2,1)S(1)} %get-tuple-element.42.pg_ref, ...), custom_call_target="tpu_custom_call" | custom-call | flops 805306368 | bytes 4194304 | tf_op jit(solution)/shard_map/own/pallas_call | solution.py:187
  11.1 1.8 %collective-permute-done.1.got_ref = bf16[2,8,320,128]{3,2,1,0:T(8,128)(2,1)S(1)} collective-permute-done((bf16[2,8,320,128]{3,2,1,0:T(8,128)(2,1)S(1)}, bf16[2,8,320,128]{3,2,1,0:T(8,128)(2,1)S(1)}, u32[]{:S(2)}, u32[]{:S(2)}) %collective-permute-start.1) | collective-permute-done | bytes 1310752 | tf_op jit(solution)/shard_map/ppermute | solution.py:217
  12.9 0.3 split.1
  13.2 2.2 %collective-permute-start.2 = (bf16[4,320,128]{2,1,0:T(8,128)(2,1)S(1)}, bf16[4,320,128]{2,1,0:T(8,128)(2,1)S(1)}, u32[]{:S(2)}, u32[]{:S(2)}) collective-permute-start(bf16[4,320,128]{2,1,0:T(8,128)(2,1)S(1)} %get-tuple-element.41), channel_id=1, source_target_pairs={{0,1},{1,0},{2,3},{3,2},{4,5},{5,4},{6,7},{7,6},{8,9},{9,8},{10,11... | collective-permute-start | bytes 983048 | tf_op jit(solution)/shard_map/ppermute | solution.py:217
  15.4 1.5 %collective-permute-start.4 = (bf16[4,320,128]{2,1,0:T(8,128)(2,1)S(1)}, bf16[4,320,128]{2,1,0:T(8,128)(2,1)S(1)}, u32[]{:S(2)}, u32[]{:S(2)}) collective-permute-start(bf16[4,320,128]{2,1,0:T(8,128)(2,1)S(1)} %get-tuple-element.45), channel_id=1, source_target_pairs={{0,16},{1,17},{2,18},{3,19},{4,20},{5,21},{6,22},{7,23},{8,24},{9,... | collective-permute-start | bytes 983048 | tf_op jit(solution)/shard_map/ppermute | solution.py:217
  16.9 0.1 collective-permute-start.5
  16.9 0.5 %back.1 = bf16[256,512]{1,0:T(8,128)(2,1)S(1)} custom-call(bf16[512,1024]{1,0:T(8,128)(2,1)S(1)} %get-tuple-element.42.pg_ref, bf16[1024,1024]{1,0:T(8,128)(2,1)S(1)} %get-tuple-element.28.wc_ref), custom_call_target="tpu_custom_call" | custom-call | flops 268435456 | bytes 3407872 | tf_op jit(solution)/shard_map/back/pallas_call | solution.py:187
  17.4 0.9 %collective-permute-start.3 = (bf16[256,512]{1,0:T(8,128)(2,1)S(1)}, bf16[256,512]{1,0:T(8,128)(2,1)S(1)}, u32[]{:S(2)}, u32[]{:S(2)}) collective-permute-start(bf16[256,512]{1,0:T(8,128)(2,1)S(1)} %back.1), channel_id=1, source_target_pairs={{8,0},{16,8},{24,16},{0,24},{9,1},{17,9},{25,17},{1,25},{10,2},{18... | collective-permute-start | bytes 786440 | tf_op jit(solution)/shard_map/ppermute | solution.py:240
  18.3 5.1 %collective-permute-done.2.refs_1_ = bf16[4,320,128]{2,1,0:T(8,128)(2,1)S(1)} collective-permute-done((bf16[4,320,128]{2,1,0:T(8,128)(2,1)S(1)}, bf16[4,320,128]{2,1,0:T(8,128)(2,1)S(1)}, u32[]{:S(2)}, u32[]{:S(2)}) %collective-permute-start.2) | collective-permute-done | bytes 327712 | tf_op jit(solution)/shard_map/ppermute | solution.py:217
  23.4 2.6 %collective-permute-done.4.refs_2_ = bf16[4,320,128]{2,1,0:T(8,128)(2,1)S(1)} collective-permute-done((bf16[4,320,128]{2,1,0:T(8,128)(2,1)S(1)}, bf16[4,320,128]{2,1,0:T(8,128)(2,1)S(1)}, u32[]{:S(2)}, u32[]{:S(2)}) %collective-permute-start.4) | collective-permute-done | bytes 327712 | tf_op jit(solution)/shard_map/ppermute | solution.py:217
  26.0 5.7 %collective-permute-done.5.refs_3_ = bf16[4,320,128]{2,1,0:T(8,128)(2,1)S(1)} collective-permute-done((bf16[4,320,128]{2,1,0:T(8,128)(2,1)S(1)}, bf16[4,320,128]{2,1,0:T(8,128)(2,1)S(1)}, u32[]{:S(2)}, u32[]{:S(2)}) %collective-permute-start.5) | collective-permute-done | bytes 327712 | tf_op jit(solution)/shard_map/ppermute | solution.py:217
  31.7 0.2 plane.1
  31.9 2.8 %collective-permute-start.6 = (bf16[320,128]{1,0:T(8,128)(2,1)S(1)}, bf16[320,128]{1,0:T(8,128)(2,1)S(1)}, u32[]{:S(2)}, u32[]{:S(2)}) collective-permute-start(bf16[320,128]{1,0:T(8,128)(2,1)S(1)} %get-tuple-element.47), channel_id=1, source_target_pairs={{0,4},{1,5},{2,6},{3,7},{4,0},{5,1},{6,2},{7,3},{8,12},{9,13},{10,... | collective-permute-start | bytes 245768 | tf_op jit(solution)/shard_map/ppermute | solution.py:217
  34.7 1.3 %collective-permute-start.7 = (bf16[320,128]{1,0:T(8,128)(2,1)S(1)}, bf16[320,128]{1,0:T(8,128)(2,1)S(1)}, u32[]{:S(2)}, u32[]{:S(2)}) collective-permute-start(bf16[320,128]{1,0:T(8,128)(2,1)S(1)} %get-tuple-element.48), channel_id=1, source_target_pairs={{0,6},{1,7},{2,4},{3,5},{4,2},{5,3},{6,0},{7,1},{8,14},{9,15},{10,... | collective-permute-start | bytes 245768 | tf_op jit(solution)/shard_map/ppermute | solution.py:217
  36.0 0.2 collective-permute-start.8
  36.2 0.0 collective-permute-done.3.arrived_ref
  36.2 1.8 %input.1 = bf16[512,512]{1,0:T(8,128)(2,1)} custom-call(bf16[512,1024]{1,0:T(8,128)(2,1)S(1)} %get-tuple-element.42.pg_ref, bf16[1024,1024]{1,0:T(8,128)(2,1)S(1)} %get-tuple-element.28.wc_ref, bf16[512,512]{1,0:T(8,128)(2,1)S(1)} %get-tuple-element.43.c_ref, bf16[256,512]{1,0:T(8,128)(2,1)S(1)} %collective-permute-done.3.arrived_ref), custom_call_target="tpu_custom_call" | custom-call | flops 1073741824 | bytes 4456448 | tf_op jit(solution)/shard_map/input/pallas_call | solution.py:187
  38.1 1.5 %collective-permute-done.6.refs_0_ = bf16[320,128]{1,0:T(8,128)(2,1)S(1)} collective-permute-done((bf16[320,128]{1,0:T(8,128)(2,1)S(1)}, bf16[320,128]{1,0:T(8,128)(2,1)S(1)}, u32[]{:S(2)}, u32[]{:S(2)}) %collective-permute-start.6) | collective-permute-done | bytes 81952 | tf_op jit(solution)/shard_map/ppermute | solution.py:217
  39.6 1.7 %collective-permute-done.7.refs_1_ = bf16[320,128]{1,0:T(8,128)(2,1)S(1)} collective-permute-done((bf16[320,128]{1,0:T(8,128)(2,1)S(1)}, bf16[320,128]{1,0:T(8,128)(2,1)S(1)}, u32[]{:S(2)}, u32[]{:S(2)}) %collective-permute-start.7) | collective-permute-done | bytes 81952 | tf_op jit(solution)/shard_map/ppermute | solution.py:217
  41.2 0.1 collective-permute-done.8.refs_3_
  41.3 0.7 %final.1 = (f32[256,128]{1,0:T(8,128)}, f32[64,128]{1,0:T(8,128)}) custom-call(bf16[320,128]{1,0:T(8,128)(2,1)S(1)} %collective-permute-done.6.refs_0_, bf16[320,128]{1,0:T(8,128)(2,1)S(1)} %collective-permute-done.7.refs_1_, bf16[320,128]{1,0:T(8,128)(2,1)S(1)} %get-tuple-element.49.refs_2_, bf16[320,128]{1,0:T(8,128)(2,1)S(1)} %collective-permute-done.8.refs_3_), custom_call_target="tpu_custom_call" | custom-call | flops 327680 | bytes 491520 | tf_op jit(solution)/shard_map/final/pallas_call | solution.py:187
Async XLA Ops:
  1.6 6.5 %collective-permute-start = (bf16[256,512]{1,0:T(8,128)(2,1)S(1)}, bf16[256,512]{1,0:T(8,128)(2,1)S(1)}, u32[]{:S(2)}, u32[]{:S(2)}) collective-permute-start(bf16[256,512]{1,0:T(8,128)(2,1)S(1)} %slice_bitcast_fusion), channel_id=1, source_target_pairs={{0,8},{8,16},{16,24},{24,0},{1,9},{9,17},{17,25},{25,1},{2,10},{10... | collective-permute-start | bytes 786440 | tf_op jit(solution)/shard_map/ppermute | solution.py:219
  9.6 3.3 %collective-permute-start.1 = (bf16[2,8,320,128]{3,2,1,0:T(8,128)(2,1)S(1)}, bf16[2,8,320,128]{3,2,1,0:T(8,128)(2,1)S(1)}, u32[]{:S(2)}, u32[]{:S(2)}) collective-permute-start(bf16[2,8,320,128]{3,2,1,0:T(8,128)(2,1)S(1)} %get-tuple-element.39), channel_id=1, source_target_pairs={{0,8},{1,9},{2,10},{3,11},{4,12},{5,13},{6,14},{7,15},{8,0},{9,1},... | collective-permute-start | bytes 3932168 | tf_op jit(solution)/shard_map/ppermute | solution.py:217
  13.2 10.2 %collective-permute-start.2 = (bf16[4,320,128]{2,1,0:T(8,128)(2,1)S(1)}, bf16[4,320,128]{2,1,0:T(8,128)(2,1)S(1)}, u32[]{:S(2)}, u32[]{:S(2)}) collective-permute-start(bf16[4,320,128]{2,1,0:T(8,128)(2,1)S(1)} %get-tuple-element.41), channel_id=1, source_target_pairs={{0,1},{1,0},{2,3},{3,2},{4,5},{5,4},{6,7},{7,6},{8,9},{9,8},{10,11... | collective-permute-start | bytes 983048 | tf_op jit(solution)/shard_map/ppermute | solution.py:217
  15.4 10.6 %collective-permute-start.4 = (bf16[4,320,128]{2,1,0:T(8,128)(2,1)S(1)}, bf16[4,320,128]{2,1,0:T(8,128)(2,1)S(1)}, u32[]{:S(2)}, u32[]{:S(2)}) collective-permute-start(bf16[4,320,128]{2,1,0:T(8,128)(2,1)S(1)} %get-tuple-element.45), channel_id=1, source_target_pairs={{0,16},{1,17},{2,18},{3,19},{4,20},{5,21},{6,22},{7,23},{8,24},{9,... | collective-permute-start | bytes 983048 | tf_op jit(solution)/shard_map/ppermute | solution.py:217
  16.9 14.8 %collective-permute-start.5 = (bf16[4,320,128]{2,1,0:T(8,128)(2,1)S(1)}, bf16[4,320,128]{2,1,0:T(8,128)(2,1)S(1)}, u32[]{:S(2)}, u32[]{:S(2)}) collective-permute-start(bf16[4,320,128]{2,1,0:T(8,128)(2,1)S(1)} %get-tuple-element.46), channel_id=1, source_target_pairs={{0,17},{1,16},{2,19},{3,18},{4,21},{5,20},{6,23},{7,22},{8,25},{9,... | collective-permute-start | bytes 983048 | tf_op jit(solution)/shard_map/ppermute | solution.py:217
  17.4 18.8 %collective-permute-start.3 = (bf16[256,512]{1,0:T(8,128)(2,1)S(1)}, bf16[256,512]{1,0:T(8,128)(2,1)S(1)}, u32[]{:S(2)}, u32[]{:S(2)}) collective-permute-start(bf16[256,512]{1,0:T(8,128)(2,1)S(1)} %back.1), channel_id=1, source_target_pairs={{8,0},{16,8},{24,16},{0,24},{9,1},{17,9},{25,17},{1,25},{10,2},{18... | collective-permute-start | bytes 786440 | tf_op jit(solution)/shard_map/ppermute | solution.py:240
  31.9 7.7 %collective-permute-start.6 = (bf16[320,128]{1,0:T(8,128)(2,1)S(1)}, bf16[320,128]{1,0:T(8,128)(2,1)S(1)}, u32[]{:S(2)}, u32[]{:S(2)}) collective-permute-start(bf16[320,128]{1,0:T(8,128)(2,1)S(1)} %get-tuple-element.47), channel_id=1, source_target_pairs={{0,4},{1,5},{2,6},{3,7},{4,0},{5,1},{6,2},{7,3},{8,12},{9,13},{10,... | collective-permute-start | bytes 245768 | tf_op jit(solution)/shard_map/ppermute | solution.py:217
  34.7 6.6 %collective-permute-start.7 = (bf16[320,128]{1,0:T(8,128)(2,1)S(1)}, bf16[320,128]{1,0:T(8,128)(2,1)S(1)}, u32[]{:S(2)}, u32[]{:S(2)}) collective-permute-start(bf16[320,128]{1,0:T(8,128)(2,1)S(1)} %get-tuple-element.48), channel_id=1, source_target_pairs={{0,6},{1,7},{2,4},{3,5},{4,2},{5,3},{6,0},{7,1},{8,14},{9,15},{10,... | collective-permute-start | bytes 245768 | tf_op jit(solution)/shard_map/ppermute | solution.py:217
  36.0 5.3 %collective-permute-start.8 = (bf16[320,128]{1,0:T(8,128)(2,1)S(1)}, bf16[320,128]{1,0:T(8,128)(2,1)S(1)}, u32[]{:S(2)}, u32[]{:S(2)}) collective-permute-start(bf16[320,128]{1,0:T(8,128)(2,1)S(1)} %get-tuple-element.50), channel_id=1, source_target_pairs={{0,2},{1,3},{2,0},{3,1},{4,6},{5,7},{6,4},{7,5},{8,10},{9,11},{10,... | collective-permute-start | bytes 245768 | tf_op jit(solution)/shard_map/ppermute | solution.py:217

commit v3 on v2

--- a/solution.py
+++ b/solution.py
@@ -9,6 +9,7 @@
 
 DILATION_STEP = 256
 VMEM_GRANT = 32 * 1024 * 1024
+FIRST_CHUNK = 10
 F32, BF16 = jnp.float32, jnp.bfloat16
 
 
@@ -76,34 +77,40 @@
     ct_ref[...] = c_ref[...].T
 
 
-def block_products(parity, xt_ref, ht_ref, ct_ref, pg_ref, gb_ref, out_ref):
-    halves, reps, height, lanes = out_ref.shape
+def block_products(first, parity, xt_ref, ht_ref, ct_ref, pg_ref, gb_ref, out_ref):
+    halves, reps, size, lanes = out_ref.shape
     blocks, h, rows = xt_ref.shape
     back = ht_ref.shape[2]
-    columns = pg_ref.shape[1]
-    per_tap = blocks // 2
-    earlier = [
-        jnp.concatenate([ht_ref[2 * i + parity], xt_ref[2 * i + parity][:, : rows - back]], 1)
-        for i in range(per_tap)
-    ]
-    current = [xt_ref[2 * i + parity] for i in range(per_tap)]
-    left = jnp.concatenate(earlier + current, 0)
-    wide = min(256, columns)
-    for j in range(0, columns, wide):
-        term = dot(left, pg_ref[:, j : j + wide]).astype(BF16)
+    columns, channels = pg_ref.shape[1], ct_ref.shape[0]
+    low, last = channels // reps, first + size
+    count = min(last, h) - first
+    if count > 0:
+        some = pl.ds(first, count)
+        picked = [2 * i + parity for i in range(blocks // 2)]
+        earlier = [jnp.concatenate([ht_ref[i, some], xt_ref[i, some, : rows - back]], 1) for i in picked]
+        left = jnp.concatenate(earlier + [xt_ref[i, some] for i in picked], 0)
+        wide = min(256, columns)
+        for j in range(0, columns, wide):
+            term = dot(left, pg_ref[:, j : j + wide]).astype(BF16)
+            for t in range(halves):
+                for k in range(0, wide, lanes):
+                    out_ref[t, (j + k) // lanes, :count, :] = term[t * count : (t + 1) * count, k : k + lanes]
+    count = max(count, 0)
+    if last > h:
+        skip, part = max(first, h) - h, size - count
+        right = jnp.concatenate([gb_ref[2 * t + parity] for t in range(halves)], 1)
+        if part == low:
+            left = ct_ref[...]
+        else:
+            left = jnp.concatenate([ct_ref[pl.ds(r * low + skip, part), :] for r in range(reps)], 0)
+        term = dot(left, right).astype(BF16)
         for t in range(halves):
-            for k in range(0, wide, lanes):
-                out_ref[t, (j + k) // lanes, :h, :] = term[t * h : (t + 1) * h, k : k + lanes]
-    right = jnp.concatenate([gb_ref[2 * t + parity] for t in range(halves)], 1)
-    term = dot(ct_ref[...], right).astype(BF16)
-    low = height - h
-    for t in range(halves):
-        for r in range(reps):
-            out_ref[t, r, h:, :] = term[r * low : (r + 1) * low, t * lanes : (t + 1) * lanes]
+            for r in range(reps):
+                out_ref[t, r, count:, :] = term[r * part : (r + 1) * part, t * lanes : (t + 1) * lanes]
 
 
 def partner_kernel(
-    lengths_ref, halo_ref, wc_ref, xt_ref, ct_ref, cur_ref, gg_ref, pg_in, gb_in,
+    first, lengths_ref, halo_ref, wc_ref, xt_ref, ct_ref, cur_ref, gg_ref, pg_in, gb_in,
     pg_ref, gb_ref, ht_ref, out_ref,
 ):
     step, channels = halo_ref.shape
@@ -119,12 +126,12 @@
         gb_ref[t, :step, :] = gated[:, t * lanes : (t + 1) * lanes]
     ht_ref[...] = halo.T.reshape(ht_ref.shape)
     parity = 1 - lax.rem(lax.axis_index("tm"), 2)
-    block_products(parity, xt_ref, ht_ref, ct_ref, pg_ref, gb_ref, out_ref)
-
-
-def own_kernel(xt_ref, ht_ref, ct_ref, pg_ref, gb_ref, out_ref):
-    parity = lax.rem(lax.axis_index("tm"), 2)
-    block_products(parity, xt_ref, ht_ref, ct_ref, pg_ref, gb_ref, out_ref)
+    block_products(first, parity, xt_ref, ht_ref, ct_ref, pg_ref, gb_ref, out_ref)
+
+
+def terms_kernel(first, away, xt_ref, ht_ref, ct_ref, pg_ref, gb_ref, out_ref):
+    parity = lax.rem(lax.axis_index("tm") + away, 2)
+    block_products(first, parity, xt_ref, ht_ref, ct_ref, pg_ref, gb_ref, out_ref)
 
 
 def back_kernel(pg_ref, wc_ref, back_ref):
@@ -132,44 +139,69 @@
     back_ref[...] = dot_nt(pg_ref[:step, :], wc_ref[:channels, :]).astype(BF16)
 
 
-def input_kernel(pg_ref, wc_ref, c_ref, arrived_ref, out_ref):
+def input_kernel(pg_ref, wc_ref, c_ref, lo_ref, hi_ref):
     step = DILATION_STEP
     rows, channels = c_ref.shape
     current = dot_nt(pg_ref[...], wc_ref[channels:, :]) + c_ref[...].astype(F32)
     earlier = dot_nt(pg_ref[step:, :], wc_ref[:channels, :])
-    out_ref[: rows - step, :] = (current[: rows - step] + earlier).astype(BF16)
+    lo_ref[...] = (current[: rows - step] + earlier).astype(BF16)
+    hi_ref[...] = current[rows - step :]
+
+
+def rows_kernel(lo_ref, hi_ref, arrived_ref, out_ref):
+    count = lo_ref.shape[0]
     arrived = jnp.where(lax.axis_index("tm") < lax.axis_size("tm") - 1, arrived_ref[...].astype(F32), 0.0)
-    out_ref[rows - step :, :] = (current[rows - step :] + arrived).astype(BF16)
-
-
-def split_kernel(count_x, count_z, got_ref, kept_ref, *outs):
-    x = lax.axis_index("tm") // 2
-    rep = lax.axis_index("rep")
-    y = lax.rem(rep, 2)
+    out_ref[:count, :] = lo_ref[...]
+    out_ref[count:, :] = (hi_ref[...] + arrived).astype(BF16)
+
+
+def coordinates(count_z):
+    tm, rep = lax.axis_index("tm"), lax.axis_index("rep")
+    return lax.rem(tm, 2), lax.rem(tm // 2, 2), lax.rem(rep, 2), (tm // 4) * count_z + rep // 2
+
+
+def split_kernel(count_z, got_ref, kept_ref, stay_ref, send_ref):
+    core, x, y, _ = coordinates(count_z)
+    for s, out in enumerate((stay_ref, send_ref)):
+        for j in range(out.shape[0]):
+            far, other = j // 2, j % 2
+            to_x = jnp.where(core == 0, x ^ s, other)
+            to_y = jnp.where(core == 0, other, y ^ s)
+            t, r = 2 * (far // count_z) + to_x, 2 * (far % count_z) + to_y
+            out[j] = (got_ref[t, r].astype(F32) + kept_ref[t, r].astype(F32)).astype(BF16)
+
+
+def half_kernel(count_z, got_ref, kept_ref, stay_ref, send_ref):
+    core, x, y, _ = coordinates(count_z)
+    mine = jnp.where(core == 0, y, x)
+    for s, out in enumerate((stay_ref, send_ref)):
+        for far in range(out.shape[0]):
+            j = 2 * far + (mine ^ s)
+            out[far] = (got_ref[j].astype(F32) + kept_ref[j].astype(F32)).astype(BF16)
+
+
+def far_kernel(count_z, *refs):
+    me = coordinates(count_z)[3]
+    chunks = len(refs) - far_count(refs)
+    ins, outs = refs[:chunks], refs[chunks:]
     for d, out in enumerate(outs):
-        to_x, to_y = x ^ (d // 2), y ^ (d % 2)
-        for to_z in range(count_z):
-            r = 2 * to_z + to_y
-            out[to_z] = (got_ref[to_x, r].astype(F32) + kept_ref[to_x, r].astype(F32)).astype(BF16)
-
-
-def total_of(refs, index):
-    total = refs[0][index].astype(F32)
-    for ref in refs[1:]:
-        total = total + ref[index].astype(F32)
-    return total
-
-
-def plane_kernel(count_x, count_z, *refs):
-    parts, outs = refs[: 2 * count_x], refs[2 * count_x :]
-    z = lax.axis_index("rep") // 2
-    for d in range(count_z):
-        outs[d][...] = total_of(parts, z ^ d).astype(BF16)
+        first = 0
+        for got_ref, kept_ref in zip(ins[::2], ins[1::2]):
+            last = first + got_ref.shape[1]
+            out[first:last, :] = (got_ref[me ^ d].astype(F32) + kept_ref[me ^ d].astype(F32)).astype(BF16)
+            first = last
+
+
+def far_count(refs):
+    return refs[0].shape[0]
 
 
 def final_kernel(scale, *refs):
     parts, (conv_ref, res_ref) = refs[:-2], refs[-2:]
-    total = total_of(parts, ...) * scale
+    total = parts[0][...].astype(F32)
+    for ref in parts[1:]:
+        total = total + ref[...].astype(F32)
+    total = total * scale
     height = conv_ref.shape[0]
     conv_ref[...] = total[:height]
     res_ref[...] = total[height:]
@@ -218,7 +250,7 @@
 
     halo = lax.ppermute(x[rows - step :], "tm", [(i, (i + 1) % tms) for i in range(tms)])
     whole_pg, whole_gb = ((rows, 2 * channels), BF16), ((tms, rows, lanes), BF16)
-    xt, ct, cur, gg, pg, gb, wc, c = call(
+    xt, ct, cur, gg, pg, gb, wc, c_in = call(
         local_kernel,
         [
             ((tms // 2, h, rows), BF16), ((channels, rows), BF16), ((step, 2 * channels), F32),
@@ -227,42 +259,66 @@
         product * 4, lengths, x, cot, w_conv, w_res, name="local", in_hbm=(1, 2, 3, 4),
         scratch=[pltpu.VMEM(x.shape, BF16), pltpu.VMEM(w_res.shape, BF16), pltpu.SemaphoreType.DMA((5,))],
     )
-    term = ((halves, reps, height, lanes), BF16)
+    def core_of(device):
+        return device // reps % 2
+
+    def swap_mixed(array, first_mask, second_mask):
+        return lax.ppermute(
+            array, ("tm", "rep"), [(i, i ^ (second_mask if core_of(i) else first_mask)) for i in range(devices)]
+        )
+
+    fars = halves // 2 * count_z
+    far_masks = [(d // count_z) * 4 * reps + (d % count_z) * 2 for d in range(fars)]
+    core_mask, x_mask, y_mask = reps, 2 * reps, 1
+    cut = (height * FIRST_CHUNK // 20) // 16 * 16
+    sizes, starts = [cut, height - cut], [0, cut]
+    terms = [((halves, reps, size, lanes), BF16) for size in sizes]
     pg, gb, ht, theirs = call(
-        partner_kernel,
-        [whole_pg, whole_gb, ((tms // 2, h, step), BF16), term],
-        product * 4, lengths, halo, wc, xt, ct, cur, gg, pg, gb, name="partner", aliases={7: 0, 8: 1},
-    )
-    got = swap(theirs, reps)
-    (mine,) = call(own_kernel, [term], product * 3, xt, ht, ct, pg, gb, name="own")
-    pg, mine = lax.optimization_barrier((pg, mine))
-    (back,) = call(back_kernel, [((step, channels), BF16)], product, pg, wc, name="back")
+        functools.partial(partner_kernel, starts[1]),
+        [whole_pg, whole_gb, ((tms // 2, h, step), BF16), terms[1]],
+        product * 3, lengths, halo, wc, xt, ct, cur, gg, pg, gb, name="partner", aliases={7: 0, 8: 1},
+    )
+
+    def terms_of(chunk, away):
+        (out,) = call(
+            functools.partial(terms_kernel, starts[chunk], away), [terms[chunk]], product * 2,
+            xt, ht, ct, pg, gb, name=f"terms{chunk}{away}",
+        )
+        return out
+
+    theirs = [terms_of(0, 1), theirs]
+    got = [swap(part, core_mask) for part in theirs]
+    sums = []
+    for c, size in enumerate(sizes):
+        stay, send = call(
+            functools.partial(split_kernel, count_z), [((2 * fars, size, lanes), BF16)] * 2,
+            halves * reps * size * lanes, got[c], terms_of(c, 0), name=f"split{c}",
+        )
+        sums.append((swap_mixed(send, x_mask, y_mask), stay))
+    parts = []
+    for c, size in enumerate(sizes):
+        stay, send = call(
+            functools.partial(half_kernel, count_z), [((fars, size, lanes), BF16)] * 2,
+            2 * fars * size * lanes, *sums[c], name=f"half{c}",
+        )
+        parts += [swap_mixed(send, y_mask, x_mask), stay]
+    (back,) = call(back_kernel, [((step, channels), BF16)], product, after(pg, parts[2]), wc, name="back")
+    lo, hi = call(
+        input_kernel, [((rows - step, channels), BF16), ((step, channels), F32)], product * 4,
+        after(pg, sums[0][0]), wc, c_in, name="input",
+    )
+    outs = call(
+        functools.partial(far_kernel, count_z), [((height, lanes), BF16)] * fars,
+        fars * height * lanes, *parts, name="far",
+    )
     arrived = lax.ppermute(back, "tm", [((i + 1) % tms, i) for i in range(tms)])
-
-    plane = ((count_z, height, lanes), BF16)
-    parts = call(
-        functools.partial(split_kernel, halves, count_z),
-        [plane] * (2 * halves),
-        term[0][0] * reps * height * lanes,
-        got, mine, name="split",
-    )
-    plane_masks = [(d // 2) * 2 * reps + d % 2 for d in range(2 * halves)]
-    line_masks = [2 * d for d in range(count_z)]
-    planes = [swap(p, m) if m else p for p, m in zip(parts[: 2 * halves], plane_masks)]
-    (grad_in,) = call(
-        input_kernel, [((rows, channels), BF16)], product * 4, after(pg, planes[1]), wc, c, arrived, name="input",
-    )
-    parts = call(
-        functools.partial(plane_kernel, halves, count_z),
-        [(plane[0][1:], BF16)] * count_z, height * lanes * 16, *planes, name="plane",
-    )
-    firsts = list(parts)
-    for d in list(range(2, count_z)) + [1]:
-        firsts[d] = swap(firsts[d], line_masks[d])
+    parts = [swap(p, m) if m else p for p, m in zip(outs, far_masks)]
+    parts = parts[:1:-1] + parts[:2]
+    (grad_in,) = call(rows_kernel, [((rows, channels), BF16)], rows * channels, lo, hi, arrived, name="rows")
     scale = float(rows * devices) ** (-0.5)
     conv, res = call(
         functools.partial(final_kernel, scale),
-        [((h, lanes), F32), ((low, lanes), F32)], height * lanes * 8, *firsts[2:], *firsts[:2], name="final",
+        [((h, lanes), F32), ((low, lanes), F32)], height * lanes * 8, after(parts[0], grad_in), *parts[1:], name="final",
     )
     return grad_in[None], conv, res.T
 

time: 42.2 us -> 39.9 us (0.945)
  waiting for transfers between devices: 20.5 us -> 14.8 us
  starting transfers between devices: 10.1 us -> 13 us
  Pallas kernels: 9.07 us -> 9.54 us
    ppermute x7 -> x5, waiting for transfers between devices: 18.5 us -> 3.41 us  [swap(): lax.ppermute(array, ('tm', 'rep'), [(i, i ^ mask) for i in range(devices)])]
    ppermute x0 -> x4, waiting for transfers between devices: none -> 9.31 us  [swap_mixed(): lax.ppermute(array, ('tm', 'rep'), [(i, i ^ (second_mask if core_of(i) el...]
    ppermute x0 -> x4, starting transfers between devices: none -> 6.93 us  [swap_mixed(): lax.ppermute(array, ('tm', 'rep'), [(i, i ^ (second_mask if core_of(i) el...]
    ppermute x7 -> x5, starting transfers between devices: 8.76 us -> 5.53 us  [swap(): lax.ppermute(array, ('tm', 'rep'), [(i, i ^ mask) for i in range(devices)])]
    ppermute x1, starting transfers between devices: 0.87 us -> 0.06 us  [body(): arrived = lax.ppermute(back, 'tm', [((i + 1) % tms, i) for i in range(tms)])]
    pallas_call x8 -> x14, Pallas kernels: 9.07 us -> 9.54 us  [call(): pl.pallas_call(kernel, out_shape=out_shape, in_specs=[spec(i, a) for i, a...]
  transfers between devices with their start and end apart: 9 -> 11, of which waited for: 8 -> 7; matrix products, arithmetic and copies ran while one was open for 0% -> 0% of each run, Pallas kernels for 16% -> 19%
where the time goes in v3:
time: 39.9 us; the launch traced here: 39.7 us
  waiting for transfers between devices  14.8 us (37%)
  starting transfers between devices  13 us (33%)
  Pallas kernels  9.54 us (24%)
  between operations  1.39 us (3%)
  local copies, waits for them, and re-layouts  0.97 us (2%)
    pallas_call x14, Pallas kernels, call(): pl.pallas_call(kernel, out_shape=out_shape, in_specs=[spec(i, a) for i, a...  9.54 us
    ppermute x4, waiting for transfers between devices, swap_mixed(): lax.ppermute(array, ('tm', 'rep'), [(i, i ^ (second_mask if core_of(i) el...  9.31 us
    ppermute x4, starting transfers between devices, swap_mixed(): lax.ppermute(array, ('tm', 'rep'), [(i, i ^ (second_mask if core_of(i) el...  6.93 us
    ppermute x5, starting transfers between devices, swap(): lax.ppermute(array, ('tm', 'rep'), [(i, i ^ mask) for i in range(devices)])  5.53 us
    ppermute x5, waiting for transfers between devices, swap(): lax.ppermute(array, ('tm', 'rep'), [(i, i ^ mask) for i in range(devices)])  3.41 us
    ppermute x1, waiting for transfers between devices, body(): lax.ppermute(x[rows - step:], 'tm', [(i, (i + 1) % tms) for i in range(tm...  2.04 us
    slice x1, local copies, waits for them, and re-layouts, body(): x[rows - step:]  0.97 us
  transfers between devices with their start and end apart: 11, of which 7 were waited for; matrix products, arithmetic and copies ran while one was open for 0% of the time, Pallas kernels for 19%

profile of v3, /device:TPU:0, one launch (start us, length us, event | category | flops | bytes accessed | tf_op | source)
XLA Modules:
  0.0 39.7 jit_solution(1951873194803784676)
XLA Ops:
  0.6 1.0 %slice_bitcast_fusion = bf16[256,512]{1,0:T(8,128)(2,1)S(1)} fusion(bf16[1,512,512]{2,1,0:T(8,128)(2,1)} %param.5), kind=kLoop, calls=%fused_computation | loop fusion | bytes 524288 | tf_op jit(solution)/shard_map/slice | solution.py:251
  1.6 0.5 %collective-permute-start = (bf16[256,512]{1,0:T(8,128)(2,1)S(1)}, bf16[256,512]{1,0:T(8,128)(2,1)S(1)}, u32[]{:S(2)}, u32[]{:S(2)}) collective-permute-start(bf16[256,512]{1,0:T(8,128)(2,1)S(1)} %slice_bitcast_fusion), channel_id=1, source_target_pairs={{0,8},{8,16},{16,24},{24,0},{1,9},{9,17},{17,25},{25,1},{2,10},{10... | collective-permute-start | bytes 786440 | tf_op jit(solution)/shard_map/ppermute | solution.py:251
  2.8 3.3 %local.1 = (bf16[2,256,512]{2,1,0:T(8,128)(2,1)S(1)}, bf16[512,512]{1,0:T(8,128)(2,1)S(1)}, f32[256,1024]{1,0:T(8,128)S(1)}, f32[256,512]{1,0:T(8,128)S(1)}, bf1...) custom-call(s32[1]{0:T(128)S(6)} %copy.12.lengths_ref, ...), custom_call_target="tpu_custom_call" | custom-call | flops 1073741824 | bytes 10485764 | tf_op jit(solution)/shard_map/local/pallas_call | solution.py:219
  6.0 2.0 %collective-permute-done.halo_ref = bf16[256,512]{1,0:T(8,128)(2,1)S(1)} collective-permute-done((bf16[256,512]{1,0:T(8,128)(2,1)S(1)}, bf16[256,512]{1,0:T(8,128)(2,1)S(1)}, u32[]{:S(2)}, u32[]{:S(2)}) %collective-permute-start) | collective-permute-done | bytes 262176 | tf_op jit(solution)/shard_map/ppermute | solution.py:251
  8.1 1.1 %partner.1 = (bf16[512,1024]{1,0:T(8,128)(2,1)S(1)}, bf16[4,512,128]{2,1,0:T(8,128)(2,1)S(1)}, bf16[2,256,256]{2,1,0:T(8,128)(2,1)S(1)}, bf16[2,8,160,128]{3,2,1,0:T(8,128)(2,1)S(1)}) custom-call(s32[1]{0:T(128)S(6)} %copy.12.lengths_ref, bf16[256,512]{1,0:T(8,128)(2,1)S(1)} %collective-permute-done.halo_ref, ...), custom_call_target="tpu_custom_call", output_to_operand_aliasing={{0}: (7, {}), {1}: (8, {})} | custom-call | flops 805306368 | bytes 9043972 | tf_op jit(solution)/shard_map/partner/pallas_call | solution.py:219
  9.2 0.6 %collective-permute-start.3 = (bf16[2,8,160,128]{3,2,1,0:T(8,128)(2,1)S(1)}, bf16[2,8,160,128]{3,2,1,0:T(8,128)(2,1)S(1)}, u32[]{:S(2)}, u32[]{:S(2)}) collective-permute-start(bf16[2,8,160,128]{3,2,1,0:T(8,128)(2,1)S(1)} %get-tuple-element.49), channel_id=1, source_target_pairs={{0,8},{1,9},{2,10},{3,11},{4,12},{5,13},{6,14},{7,15},{8,0},{9,1},... | collective-permute-start | bytes 1966088 | tf_op jit(solution)/shard_map/ppermute | solution.py:249
  9.9 0.5 %terms01.1 = bf16[2,8,160,128]{3,2,1,0:T(8,128)(2,1)S(1)} custom-call(bf16[2,256,512]{2,1,0:T(8,128)(2,1)S(1)} %get-tuple-element.35.xt_ref, bf16[2,256,256]{2,1,0:T(8,128)(2,1)S(1)} %get-tuple-element.42.ht_ref, bf16[512,512]{1,0:T(8,128)(2,1)S(1)} %get-tuple-element.36.ct_ref, bf16[512,1024]{1,0:T(8,128)(2,1)S(1)} %get-tuple-element.53.pg_ref, ...), custom_call_target="tpu_custom_call" | custom-call | flops 536870912 | bytes 3538944 | tf_op jit(solution)/shard_map/terms01/pallas_call | solution.py:219
  10.4 0.1 collective-permute-start.1
  10.5 0.5 %terms10.1.kept_ref = bf16[2,8,160,128]{3,2,1,0:T(8,128)(2,1)S(1)} custom-call(bf16[2,256,512]{2,1,0:T(8,128)(2,1)S(1)} %get-tuple-element.35.xt_ref, bf16[2,256,256]{2,1,0:T(8,128)(2,1)S(1)} %get-tuple-element.42.ht_ref, bf16[512,512]{1,0:T(8,128)(2,1)S(1)} %get-tuple-element.36.ct_ref, bf16[512,1024]{1,0:T(8,128)(2,1)S(1)} %get-tuple-element.53.pg_ref, ...), custom_call_target="tpu_custom_call" | custom-call | flops 536870912 | bytes 3538944 | tf_op jit(solution)/shard_map/terms10/pallas_call | solution.py:219
  11.0 0.6 %collective-permute-done.3.got_ref = bf16[2,8,160,128]{3,2,1,0:T(8,128)(2,1)S(1)} collective-permute-done((bf16[2,8,160,128]{3,2,1,0:T(8,128)(2,1)S(1)}, bf16[2,8,160,128]{3,2,1,0:T(8,128)(2,1)S(1)}, u32[]{:S(2)}, u32[]{:S(2)}) %collective-permute-start.3) | collective-permute-done | bytes 655392 | tf_op jit(solution)/shard_map/ppermute | solution.py:249
  11.6 0.2 split1.1
  11.8 2.2 %collective-permute-start.4 = (bf16[8,160,128]{2,1,0:T(8,128)(2,1)S(1)}, bf16[8,160,128]{2,1,0:T(8,128)(2,1)S(1)}, u32[]{:S(2)}, u32[]{:S(2)}) collective-permute-start(bf16[8,160,128]{2,1,0:T(8,128)(2,1)S(1)} %get-tuple-element.50), channel_id=1, source_target_pairs={{0,16},{1,17},{2,18},{3,19},{4,20},{5,21},{6,22},{7,23},{8,9},{9,8... | collective-permute-start | bytes 983048 | tf_op jit(solution)/shard_map/ppermute | solution.py:266
  13.9 0.5 %terms00.1.kept_ref = bf16[2,8,160,128]{3,2,1,0:T(8,128)(2,1)S(1)} custom-call(bf16[2,256,512]{2,1,0:T(8,128)(2,1)S(1)} %get-tuple-element.35.xt_ref, bf16[2,256,256]{2,1,0:T(8,128)(2,1)S(1)} %get-tuple-element.42.ht_ref, bf16[512,512]{1,0:T(8,128)(2,1)S(1)} %get-tuple-element.36.ct_ref, bf16[512,1024]{1,0:T(8,128)(2,1)S(1)} %get-tuple-element.53.pg_ref, ...), custom_call_target="tpu_custom_call" | custom-call | flops 536870912 | bytes 3538944 | tf_op jit(solution)/shard_map/terms00/pallas_call | solution.py:219
  14.4 0.0 collective-permute-done.1.got_ref
  14.4 0.2 split0.1
  14.6 0.2 collective-permute-start.2
  14.9 4.1 %collective-permute-done.4.got_ref = bf16[8,160,128]{2,1,0:T(8,128)(2,1)S(1)} collective-permute-done((bf16[8,160,128]{2,1,0:T(8,128)(2,1)S(1)}, bf16[8,160,128]{2,1,0:T(8,128)(2,1)S(1)}, u32[]{:S(2)}, u32[]{:S(2)}) %collective-permute-start.4) | collective-permute-done | bytes 327712 | tf_op jit(solution)/shard_map/ppermute | solution.py:266
  19.0 0.1 half1.1
  19.1 2.1 %collective-permute-start.5 = (bf16[4,160,128]{2,1,0:T(8,128)(2,1)S(1)}, bf16[4,160,128]{2,1,0:T(8,128)(2,1)S(1)}, u32[]{:S(2)}, u32[]{:S(2)}) collective-permute-start(bf16[4,160,128]{2,1,0:T(8,128)(2,1)S(1)} %get-tuple-element.52), channel_id=1, source_target_pairs={{0,1},{1,0},{2,3},{3,2},{4,5},{5,4},{6,7},{7,6},{8,24},{9,25},{10,... | collective-permute-start | bytes 491528 | tf_op jit(solution)/shard_map/ppermute | solution.py:266
  21.2 2.4 %collective-permute-done.2.got_ref = bf16[8,160,128]{2,1,0:T(8,128)(2,1)S(1)} collective-permute-done((bf16[8,160,128]{2,1,0:T(8,128)(2,1)S(1)}, bf16[8,160,128]{2,1,0:T(8,128)(2,1)S(1)}, u32[]{:S(2)}, u32[]{:S(2)}) %collective-permute-start.2) | collective-permute-done | bytes 327712 | tf_op jit(solution)/shard_map/ppermute | solution.py:266
  23.6 0.1 half0.1
  23.7 2.4 %collective-permute-start.7 = (bf16[4,160,128]{2,1,0:T(8,128)(2,1)S(1)}, bf16[4,160,128]{2,1,0:T(8,128)(2,1)S(1)}, u32[]{:S(2)}, u32[]{:S(2)}) collective-permute-start(bf16[4,160,128]{2,1,0:T(8,128)(2,1)S(1)} %get-tuple-element.55), channel_id=1, source_target_pairs={{0,1},{1,0},{2,3},{3,2},{4,5},{5,4},{6,7},{7,6},{8,24},{9,25},{10,... | collective-permute-start | bytes 491528 | tf_op jit(solution)/shard_map/ppermute | solution.py:266
  26.1 0.0 collective-permute-done.5.refs_2_
  26.1 0.5 %back.1 = bf16[256,512]{1,0:T(8,128)(2,1)S(1)} custom-call(bf16[512,1024]{1,0:T(8,128)(2,1)S(1)} %get-tuple-element.53.pg_ref, bf16[1024,1024]{1,0:T(8,128)(2,1)S(1)} %get-tuple-element.34.wc_ref), custom_call_target="tpu_custom_call" | custom-call | flops 268435456 | bytes 3407872 | tf_op jit(solution)/shard_map/back/pallas_call | solution.py:219
  26.6 0.1 collective-permute-start.6
  26.6 2.8 %collective-permute-done.7.refs_0_ = bf16[4,160,128]{2,1,0:T(8,128)(2,1)S(1)} collective-permute-done((bf16[4,160,128]{2,1,0:T(8,128)(2,1)S(1)}, bf16[4,160,128]{2,1,0:T(8,128)(2,1)S(1)}, u32[]{:S(2)}, u32[]{:S(2)}) %collective-permute-start.7) | collective-permute-done | bytes 163872 | tf_op jit(solution)/shard_map/ppermute | solution.py:266
  29.4 0.1 far.1
  29.5 4.2 %collective-permute-start.8 = (bf16[320,128]{1,0:T(8,128)(2,1)S(1)}, bf16[320,128]{1,0:T(8,128)(2,1)S(1)}, u32[]{:S(2)}, u32[]{:S(2)}) collective-permute-start(bf16[320,128]{1,0:T(8,128)(2,1)S(1)} %get-tuple-element.58), channel_id=1, source_target_pairs={{0,6},{1,7},{2,4},{3,5},{4,2},{5,3},{6,0},{7,1},{8,14},{9,15},{10,... | collective-permute-start | bytes 245768 | tf_op jit(solution)/shard_map/ppermute | solution.py:249
  33.6 0.0 collective-permute-start.9
  33.7 0.6 %collective-permute-start.10 = (bf16[320,128]{1,0:T(8,128)(2,1)S(1)}, bf16[320,128]{1,0:T(8,128)(2,1)S(1)}, u32[]{:S(2)}, u32[]{:S(2)}) collective-permute-start(bf16[320,128]{1,0:T(8,128)(2,1)S(1)} %get-tuple-element.62), channel_id=1, source_target_pairs={{0,2},{1,3},{2,0},{3,1},{4,6},{5,7},{6,4},{7,5},{8,10},{9,11},{10,... | collective-permute-start | bytes 245768 | tf_op jit(solution)/shard_map/ppermute | solution.py:249
  34.3 1.0 %input.1 = (bf16[256,512]{1,0:T(8,128)(2,1)S(1)}, f32[256,512]{1,0:T(8,128)S(1)}) custom-call(bf16[512,1024]{1,0:T(8,128)(2,1)S(1)} %get-tuple-element.53.pg_ref, bf16[1024,1024]{1,0:T(8,128)(2,1)S(1)} %get-tuple-element.34.wc_ref, bf16[512,512]{1,0:T(8,128)(2,1)S(1)} %get-tuple-element.46.c_ref), custom_call_target="tpu_custom_call" | custom-call | flops 1073741824 | bytes 4456448 | tf_op jit(solution)/shard_map/input/pallas_call | solution.py:219
  35.3 0.0 collective-permute-done.6.arrived_ref
  35.3 0.9 %rows.1 = bf16[512,512]{1,0:T(8,128)(2,1)} custom-call(bf16[256,512]{1,0:T(8,128)(2,1)S(1)} %get-tuple-element.47.lo_ref, f32[256,512]{1,0:T(8,128)S(1)} %get-tuple-element.48.hi_ref, bf16[256,512]{1,0:T(8,128)(2,1)S(1)} %collective-permute-done.6.arrived_ref), custom_call_target="tpu_custom_call" | custom-call | flops 262144 | bytes 1572864 | tf_op jit(solution)/shard_map/rows/pallas_call | solution.py:219
  36.2 0.6 %collective-permute-done.8.refs_0_ = bf16[320,128]{1,0:T(8,128)(2,1)S(1)} collective-permute-done((bf16[320,128]{1,0:T(8,128)(2,1)S(1)}, bf16[320,128]{1,0:T(8,128)(2,1)S(1)}, u32[]{:S(2)}, u32[]{:S(2)}) %collective-permute-start.8) | collective-permute-done | bytes 81952 | tf_op jit(solution)/shard_map/ppermute | solution.py:249
  36.8 2.2 %collective-permute-done.9.refs_1_ = bf16[320,128]{1,0:T(8,128)(2,1)S(1)} collective-permute-done((bf16[320,128]{1,0:T(8,128)(2,1)S(1)}, bf16[320,128]{1,0:T(8,128)(2,1)S(1)}, u32[]{:S(2)}, u32[]{:S(2)}) %collective-permute-start.9) | collective-permute-done | bytes 81952 | tf_op jit(solution)/shard_map/ppermute | solution.py:249
  39.0 0.0 collective-permute-done.10.refs_3_
  39.0 0.7 %final.1 = (f32[256,128]{1,0:T(8,128)}, f32[64,128]{1,0:T(8,128)}) custom-call(bf16[320,128]{1,0:T(8,128)(2,1)S(1)} %collective-permute-done.8.refs_0_, bf16[320,128]{1,0:T(8,128)(2,1)S(1)} %collective-permute-done.9.refs_1_, bf16[320,128]{1,0:T(8,128)(2,1)S(1)} %get-tuple-element.61.refs_2_, bf16[320,128]{1,0:T(8,128)(2,1)S(1)} %collective-permute-done.10.refs_3_), custom_call_target="tpu_custom_call" | custom-call | flops 327680 | bytes 491520 | tf_op jit(solution)/shard_map/final/pallas_call | solution.py:219
Async XLA Ops:
  1.6 6.5 %collective-permute-start = (bf16[256,512]{1,0:T(8,128)(2,1)S(1)}, bf16[256,512]{1,0:T(8,128)(2,1)S(1)}, u32[]{:S(2)}, u32[]{:S(2)}) collective-permute-start(bf16[256,512]{1,0:T(8,128)(2,1)S(1)} %slice_bitcast_fusion), channel_id=1, source_target_pairs={{0,8},{8,16},{16,24},{24,0},{1,9},{9,17},{17,25},{25,1},{2,10},{10... | collective-permute-start | bytes 786440 | tf_op jit(solution)/shard_map/ppermute | solution.py:251
  9.2 2.4 %collective-permute-start.3 = (bf16[2,8,160,128]{3,2,1,0:T(8,128)(2,1)S(1)}, bf16[2,8,160,128]{3,2,1,0:T(8,128)(2,1)S(1)}, u32[]{:S(2)}, u32[]{:S(2)}) collective-permute-start(bf16[2,8,160,128]{3,2,1,0:T(8,128)(2,1)S(1)} %get-tuple-element.49), channel_id=1, source_target_pairs={{0,8},{1,9},{2,10},{3,11},{4,12},{5,13},{6,14},{7,15},{8,0},{9,1},... | collective-permute-start | bytes 1966088 | tf_op jit(solution)/shard_map/ppermute | solution.py:249
  10.4 4.0 %collective-permute-start.1 = (bf16[2,8,160,128]{3,2,1,0:T(8,128)(2,1)S(1)}, bf16[2,8,160,128]{3,2,1,0:T(8,128)(2,1)S(1)}, u32[]{:S(2)}, u32[]{:S(2)}) collective-permute-start(bf16[2,8,160,128]{3,2,1,0:T(8,128)(2,1)S(1)} %terms01.1), channel_id=1, source_target_pairs={{0,8},{1,9},{2,10},{3,11},{4,12},{5,13},{6,14},{7,15},{8,0},{9,1},... | collective-permute-start | bytes 1966088 | tf_op jit(solution)/shard_map/ppermute | solution.py:249
  11.8 7.2 %collective-permute-start.4 = (bf16[8,160,128]{2,1,0:T(8,128)(2,1)S(1)}, bf16[8,160,128]{2,1,0:T(8,128)(2,1)S(1)}, u32[]{:S(2)}, u32[]{:S(2)}) collective-permute-start(bf16[8,160,128]{2,1,0:T(8,128)(2,1)S(1)} %get-tuple-element.50), channel_id=1, source_target_pairs={{0,16},{1,17},{2,18},{3,19},{4,20},{5,21},{6,22},{7,23},{8,9},{9,8... | collective-permute-start | bytes 983048 | tf_op jit(solution)/shard_map/ppermute | solution.py:266
  14.6 9.0 %collective-permute-start.2 = (bf16[8,160,128]{2,1,0:T(8,128)(2,1)S(1)}, bf16[8,160,128]{2,1,0:T(8,128)(2,1)S(1)}, u32[]{:S(2)}, u32[]{:S(2)}) collective-permute-start(bf16[8,160,128]{2,1,0:T(8,128)(2,1)S(1)} %get-tuple-element.44), channel_id=1, source_target_pairs={{0,16},{1,17},{2,18},{3,19},{4,20},{5,21},{6,22},{7,23},{8,9},{9,8... | collective-permute-start | bytes 983048 | tf_op jit(solution)/shard_map/ppermute | solution.py:266
  19.1 7.0 %collective-permute-start.5 = (bf16[4,160,128]{2,1,0:T(8,128)(2,1)S(1)}, bf16[4,160,128]{2,1,0:T(8,128)(2,1)S(1)}, u32[]{:S(2)}, u32[]{:S(2)}) collective-permute-start(bf16[4,160,128]{2,1,0:T(8,128)(2,1)S(1)} %get-tuple-element.52), channel_id=1, source_target_pairs={{0,1},{1,0},{2,3},{3,2},{4,5},{5,4},{6,7},{7,6},{8,24},{9,25},{10,... | collective-permute-start | bytes 491528 | tf_op jit(solution)/shard_map/ppermute | solution.py:266
  23.7 5.7 %collective-permute-start.7 = (bf16[4,160,128]{2,1,0:T(8,128)(2,1)S(1)}, bf16[4,160,128]{2,1,0:T(8,128)(2,1)S(1)}, u32[]{:S(2)}, u32[]{:S(2)}) collective-permute-start(bf16[4,160,128]{2,1,0:T(8,128)(2,1)S(1)} %get-tuple-element.55), channel_id=1, source_target_pairs={{0,1},{1,0},{2,3},{3,2},{4,5},{5,4},{6,7},{7,6},{8,24},{9,25},{10,... | collective-permute-start | bytes 491528 | tf_op jit(solution)/shard_map/ppermute | solution.py:266
  26.6 8.7 %collective-permute-start.6 = (bf16[256,512]{1,0:T(8,128)(2,1)S(1)}, bf16[256,512]{1,0:T(8,128)(2,1)S(1)}, u32[]{:S(2)}, u32[]{:S(2)}) collective-permute-start(bf16[256,512]{1,0:T(8,128)(2,1)S(1)} %back.1), channel_id=1, source_target_pairs={{8,0},{16,8},{24,16},{0,24},{9,1},{17,9},{25,17},{1,25},{10,2},{18... | collective-permute-start | bytes 786440 | tf_op jit(solution)/shard_map/ppermute | solution.py:314
  29.5 7.4 %collective-permute-start.8 = (bf16[320,128]{1,0:T(8,128)(2,1)S(1)}, bf16[320,128]{1,0:T(8,128)(2,1)S(1)}, u32[]{:S(2)}, u32[]{:S(2)}) collective-permute-start(bf16[320,128]{1,0:T(8,128)(2,1)S(1)} %get-tuple-element.58), channel_id=1, source_target_pairs={{0,6},{1,7},{2,4},{3,5},{4,2},{5,3},{6,0},{7,1},{8,14},{9,15},{10,... | collective-permute-start | bytes 245768 | tf_op jit(solution)/shard_map/ppermute | solution.py:249
  33.6 5.3 %collective-permute-start.9 = (bf16[320,128]{1,0:T(8,128)(2,1)S(1)}, bf16[320,128]{1,0:T(8,128)(2,1)S(1)}, u32[]{:S(2)}, u32[]{:S(2)}) collective-permute-start(bf16[320,128]{1,0:T(8,128)(2,1)S(1)} %get-tuple-element.60), channel_id=1, source_target_pairs={{0,4},{1,5},{2,6},{3,7},{4,0},{5,1},{6,2},{7,3},{8,12},{9,13},{10,... | collective-permute-start | bytes 245768 | tf_op jit(solution)/shard_map/ppermute | solution.py:249
  33.7 5.3 %collective-permute-start.10 = (bf16[320,128]{1,0:T(8,128)(2,1)S(1)}, bf16[320,128]{1,0:T(8,128)(2,1)S(1)}, u32[]{:S(2)}, u32[]{:S(2)}) collective-permute-start(bf16[320,128]{1,0:T(8,128)(2,1)S(1)} %get-tuple-element.62), channel_id=1, source_target_pairs={{0,2},{1,3},{2,0},{3,1},{4,6},{5,7},{6,4},{7,5},{8,10},{9,11},{10,... | collective-permute-start | bytes 245768 | tf_op jit(solution)/shard_map/ppermute | solution.py:249

commit v4 on v3

--- a/solution.py
+++ b/solution.py
@@ -139,13 +139,19 @@
     back_ref[...] = dot_nt(pg_ref[:step, :], wc_ref[:channels, :]).astype(BF16)
 
 
-def input_kernel(pg_ref, wc_ref, c_ref, lo_ref, hi_ref):
+def input_gradient(pg_ref, wc_ref, c_ref, lo_ref, hi_ref):
     step = DILATION_STEP
     rows, channels = c_ref.shape
     current = dot_nt(pg_ref[...], wc_ref[channels:, :]) + c_ref[...].astype(F32)
     earlier = dot_nt(pg_ref[step:, :], wc_ref[:channels, :])
     lo_ref[...] = (current[: rows - step] + earlier).astype(BF16)
     hi_ref[...] = current[rows - step :]
+
+
+def input_kernel(pg_ref, wc_ref, c_ref, lo_in, hi_in, lo_ref, hi_ref):
+    @pl.when(lax.rem(lax.axis_index("tm"), 2) == 0)
+    def _():
+        input_gradient(pg_ref, wc_ref, c_ref, lo_ref, hi_ref)
 
 
 def rows_kernel(lo_ref, hi_ref, arrived_ref, out_ref):
@@ -178,6 +184,14 @@
         for far in range(out.shape[0]):
             j = 2 * far + (mine ^ s)
             out[far] = (got_ref[j].astype(F32) + kept_ref[j].astype(F32)).astype(BF16)
+
+
+def half_input_kernel(count_z, got_ref, kept_ref, pg_ref, wc_ref, c_ref, stay_ref, send_ref, lo_ref, hi_ref):
+    @pl.when(lax.rem(lax.axis_index("tm"), 2) == 1)
+    def _():
+        input_gradient(pg_ref, wc_ref, c_ref, lo_ref, hi_ref)
+
+    half_kernel(count_z, got_ref, kept_ref, stay_ref, send_ref)
 
 
 def far_kernel(count_z, *refs):
@@ -296,17 +310,21 @@
         )
         sums.append((swap_mixed(send, x_mask, y_mask), stay))
     parts = []
+    input_shapes = [((rows - step, channels), BF16), ((step, channels), F32)]
     for c, size in enumerate(sizes):
-        stay, send = call(
-            functools.partial(half_kernel, count_z), [((fars, size, lanes), BF16)] * 2,
-            2 * fars * size * lanes, *sums[c], name=f"half{c}",
-        )
+        if c == 1:
+            stay, send, lo, hi = call(
+                functools.partial(half_input_kernel, count_z), [((fars, size, lanes), BF16)] * 2 + input_shapes,
+                2 * fars * size * lanes, *sums[c], pg, wc, c_in, name=f"half{c}",
+            )
+        else:
+            stay, send = call(
+                functools.partial(half_kernel, count_z), [((fars, size, lanes), BF16)] * 2,
+                2 * fars * size * lanes, *sums[c], name=f"half{c}",
+            )
         parts += [swap_mixed(send, y_mask, x_mask), stay]
     (back,) = call(back_kernel, [((step, channels), BF16)], product, after(pg, parts[2]), wc, name="back")
-    lo, hi = call(
-        input_kernel, [((rows - step, channels), BF16), ((step, channels), F32)], product * 4,
-        after(pg, sums[0][0]), wc, c_in, name="input",
-    )
+    lo, hi = call(input_kernel, input_shapes, product * 4, pg, wc, c_in, lo, hi, name="input", aliases={3: 0, 4: 1})
     outs = call(
         functools.partial(far_kernel, count_z), [((height, lanes), BF16)] * fars,
         fars * height * lanes, *parts, name="far",

time: 39.9 us -> 38.8 us (0.972)
  waiting for transfers between devices: 14.8 us -> 12.9 us
  starting transfers between devices: 13 us -> 13.9 us
    ppermute x4, waiting for transfers between devices: 9.31 us -> 7.4 us  [swap_mixed(): lax.ppermute(array, ('tm', 'rep'), [(i, i ^ (second_mask if core_of(i) el...]
    ppermute x1, starting transfers between devices: 0.06 us -> 0.95 us  [body(): arrived = lax.ppermute(back, 'tm', [((i + 1) % tms, i) for i in range(tms)])]
  transfers between devices with their start and end apart: 11 -> 11, of which waited for: 7 -> 7; matrix products, arithmetic and copies ran while one was open for 0% -> 0% of each run, Pallas kernels for 19% -> 20%
where the time goes in v4:
time: 38.8 us; the launch traced here: 38.7 us
  starting transfers between devices  13.9 us (36%)
  waiting for transfers between devices  12.9 us (33%)
  Pallas kernels  9.54 us (25%)
  between operations  1.38 us (4%)
  local copies, waits for them, and re-layouts  0.97 us (2%)
    pallas_call x14, Pallas kernels, call(): pl.pallas_call(kernel, out_shape=out_shape, in_specs=[spec(i, a) for i, a...  9.54 us
    ppermute x4, waiting for transfers between devices, swap_mixed(): lax.ppermute(array, ('tm', 'rep'), [(i, i ^ (second_mask if core_of(i) el...  7.4 us
    ppermute x4, starting transfers between devices, swap_mixed(): lax.ppermute(array, ('tm', 'rep'), [(i, i ^ (second_mask if core_of(i) el...  6.93 us
    ppermute x5, starting transfers between devices, swap(): lax.ppermute(array, ('tm', 'rep'), [(i, i ^ mask) for i in range(devices)])  5.53 us
    ppermute x5, waiting for transfers between devices, swap(): lax.ppermute(array, ('tm', 'rep'), [(i, i ^ mask) for i in range(devices)])  3.41 us
    ppermute x1, waiting for transfers between devices, body(): lax.ppermute(x[rows - step:], 'tm', [(i, (i + 1) % tms) for i in range(tm...  2.04 us
    slice x1, local copies, waits for them, and re-layouts, body(): x[rows - step:]  0.97 us
    ppermute x1, starting transfers between devices, body(): arrived = lax.ppermute(back, 'tm', [((i + 1) % tms, i) for i in range(tms)])  0.95 us
  transfers between devices with their start and end apart: 11, of which 7 were waited for; matrix products, arithmetic and copies ran while one was open for 0% of the time, Pallas kernels for 20%

profile of v4, /device:TPU:0, one launch (start us, length us, event | category | flops | bytes accessed | tf_op | source)
XLA Modules:
  0.0 38.7 jit_solution(18065972964491005016)
XLA Ops:
  0.6 1.0 %slice_bitcast_fusion = bf16[256,512]{1,0:T(8,128)(2,1)S(1)} fusion(bf16[1,512,512]{2,1,0:T(8,128)(2,1)} %param.5), kind=kLoop, calls=%fused_computation | loop fusion | bytes 524288 | tf_op jit(solution)/shard_map/slice | solution.py:265
  1.6 0.5 %collective-permute-start = (bf16[256,512]{1,0:T(8,128)(2,1)S(1)}, bf16[256,512]{1,0:T(8,128)(2,1)S(1)}, u32[]{:S(2)}, u32[]{:S(2)}) collective-permute-start(bf16[256,512]{1,0:T(8,128)(2,1)S(1)} %slice_bitcast_fusion), channel_id=1, source_target_pairs={{0,8},{8,16},{16,24},{24,0},{1,9},{9,17},{17,25},{25,1},{2,10},{10... | collective-permute-start | bytes 786440 | tf_op jit(solution)/shard_map/ppermute | solution.py:265
  2.8 3.3 %local.1 = (bf16[2,256,512]{2,1,0:T(8,128)(2,1)S(1)}, bf16[512,512]{1,0:T(8,128)(2,1)S(1)}, f32[256,1024]{1,0:T(8,128)S(1)}, f32[256,512]{1,0:T(8,128)S(1)}, bf1...) custom-call(s32[1]{0:T(128)S(6)} %copy.16.lengths_ref, ...), custom_call_target="tpu_custom_call" | custom-call | flops 1073741824 | bytes 10485764 | tf_op jit(solution)/shard_map/local/pallas_call | solution.py:233
  6.0 2.0 %collective-permute-done.halo_ref = bf16[256,512]{1,0:T(8,128)(2,1)S(1)} collective-permute-done((bf16[256,512]{1,0:T(8,128)(2,1)S(1)}, bf16[256,512]{1,0:T(8,128)(2,1)S(1)}, u32[]{:S(2)}, u32[]{:S(2)}) %collective-permute-start) | collective-permute-done | bytes 262176 | tf_op jit(solution)/shard_map/ppermute | solution.py:265
  8.1 1.1 %partner.1 = (bf16[512,1024]{1,0:T(8,128)(2,1)S(1)}, bf16[4,512,128]{2,1,0:T(8,128)(2,1)S(1)}, bf16[2,256,256]{2,1,0:T(8,128)(2,1)S(1)}, bf16[2,8,160,128]{3,2,1,0:T(8,128)(2,1)S(1)}) custom-call(s32[1]{0:T(128)S(6)} %copy.16.lengths_ref, bf16[256,512]{1,0:T(8,128)(2,1)S(1)} %collective-permute-done.halo_ref, ...), custom_call_target="tpu_custom_call", output_to_operand_aliasing={{0}: (7, {}), {1}: (8, {})} | custom-call | flops 805306368 | bytes 9043972 | tf_op jit(solution)/shard_map/partner/pallas_call | solution.py:233
  9.2 0.6 %collective-permute-start.1 = (bf16[2,8,160,128]{3,2,1,0:T(8,128)(2,1)S(1)}, bf16[2,8,160,128]{3,2,1,0:T(8,128)(2,1)S(1)}, u32[]{:S(2)}, u32[]{:S(2)}) collective-permute-start(bf16[2,8,160,128]{3,2,1,0:T(8,128)(2,1)S(1)} %get-tuple-element.44), channel_id=1, source_target_pairs={{0,8},{1,9},{2,10},{3,11},{4,12},{5,13},{6,14},{7,15},{8,0},{9,1},... | collective-permute-start | bytes 1966088 | tf_op jit(solution)/shard_map/ppermute | solution.py:263
  9.9 0.5 %terms01.1 = bf16[2,8,160,128]{3,2,1,0:T(8,128)(2,1)S(1)} custom-call(bf16[2,256,512]{2,1,0:T(8,128)(2,1)S(1)} %get-tuple-element.36.xt_ref, bf16[2,256,256]{2,1,0:T(8,128)(2,1)S(1)} %get-tuple-element.45.ht_ref, bf16[512,512]{1,0:T(8,128)(2,1)S(1)} %get-tuple-element.37.ct_ref, bf16[512,1024]{1,0:T(8,128)(2,1)S(1)} %get-tuple-element.54.pg_ref, ...), custom_call_target="tpu_custom_call" | custom-call | flops 536870912 | bytes 3538944 | tf_op jit(solution)/shard_map/terms01/pallas_call | solution.py:233
  10.4 0.1 collective-permute-start.5
  10.5 0.5 %terms10.1.kept_ref = bf16[2,8,160,128]{3,2,1,0:T(8,128)(2,1)S(1)} custom-call(bf16[2,256,512]{2,1,0:T(8,128)(2,1)S(1)} %get-tuple-element.36.xt_ref, bf16[2,256,256]{2,1,0:T(8,128)(2,1)S(1)} %get-tuple-element.45.ht_ref, bf16[512,512]{1,0:T(8,128)(2,1)S(1)} %get-tuple-element.37.ct_ref, bf16[512,1024]{1,0:T(8,128)(2,1)S(1)} %get-tuple-element.54.pg_ref, ...), custom_call_target="tpu_custom_call" | custom-call | flops 536870912 | bytes 3538944 | tf_op jit(solution)/shard_map/terms10/pallas_call | solution.py:233
  11.0 0.6 %collective-permute-done.1.got_ref = bf16[2,8,160,128]{3,2,1,0:T(8,128)(2,1)S(1)} collective-permute-done((bf16[2,8,160,128]{3,2,1,0:T(8,128)(2,1)S(1)}, bf16[2,8,160,128]{3,2,1,0:T(8,128)(2,1)S(1)}, u32[]{:S(2)}, u32[]{:S(2)}) %collective-permute-start.1) | collective-permute-done | bytes 655392 | tf_op jit(solution)/shard_map/ppermute | solution.py:263
  11.6 0.2 split1.1
  11.8 2.2 %collective-permute-start.2 = (bf16[8,160,128]{2,1,0:T(8,128)(2,1)S(1)}, bf16[8,160,128]{2,1,0:T(8,128)(2,1)S(1)}, u32[]{:S(2)}, u32[]{:S(2)}) collective-permute-start(bf16[8,160,128]{2,1,0:T(8,128)(2,1)S(1)} %get-tuple-element.47), channel_id=1, source_target_pairs={{0,16},{1,17},{2,18},{3,19},{4,20},{5,21},{6,22},{7,23},{8,9},{9,8... | collective-permute-start | bytes 983048 | tf_op jit(solution)/shard_map/ppermute | solution.py:280
  13.9 0.5 %terms00.1.kept_ref = bf16[2,8,160,128]{3,2,1,0:T(8,128)(2,1)S(1)} custom-call(bf16[2,256,512]{2,1,0:T(8,128)(2,1)S(1)} %get-tuple-element.36.xt_ref, bf16[2,256,256]{2,1,0:T(8,128)(2,1)S(1)} %get-tuple-element.45.ht_ref, bf16[512,512]{1,0:T(8,128)(2,1)S(1)} %get-tuple-element.37.ct_ref, bf16[512,1024]{1,0:T(8,128)(2,1)S(1)} %get-tuple-element.54.pg_ref, ...), custom_call_target="tpu_custom_call" | custom-call | flops 536870912 | bytes 3538944 | tf_op jit(solution)/shard_map/terms00/pallas_call | solution.py:233
  14.4 0.0 collective-permute-done.5.got_ref
  14.4 0.2 split0.1
  14.6 0.2 collective-permute-start.6
  14.9 4.1 %collective-permute-done.2.got_ref = bf16[8,160,128]{2,1,0:T(8,128)(2,1)S(1)} collective-permute-done((bf16[8,160,128]{2,1,0:T(8,128)(2,1)S(1)}, bf16[8,160,128]{2,1,0:T(8,128)(2,1)S(1)}, u32[]{:S(2)}, u32[]{:S(2)}) %collective-permute-start.2) | collective-permute-done | bytes 327712 | tf_op jit(solution)/shard_map/ppermute | solution.py:280
  19.0 0.1 half1.1
  19.1 2.1 %collective-permute-start.3 = (bf16[4,160,128]{2,1,0:T(8,128)(2,1)S(1)}, bf16[4,160,128]{2,1,0:T(8,128)(2,1)S(1)}, u32[]{:S(2)}, u32[]{:S(2)}) collective-permute-start(bf16[4,160,128]{2,1,0:T(8,128)(2,1)S(1)} %get-tuple-element.53), channel_id=1, source_target_pairs={{0,1},{1,0},{2,3},{3,2},{4,5},{5,4},{6,7},{7,6},{8,24},{9,25},{10,... | collective-permute-start | bytes 491528 | tf_op jit(solution)/shard_map/ppermute | solution.py:280
  21.2 1.4 %collective-permute-done.6.got_ref = bf16[8,160,128]{2,1,0:T(8,128)(2,1)S(1)} collective-permute-done((bf16[8,160,128]{2,1,0:T(8,128)(2,1)S(1)}, bf16[8,160,128]{2,1,0:T(8,128)(2,1)S(1)}, u32[]{:S(2)}, u32[]{:S(2)}) %collective-permute-start.6) | collective-permute-done | bytes 327712 | tf_op jit(solution)/shard_map/ppermute | solution.py:280
  22.6 0.1 half0.1
  22.7 2.4 %collective-permute-start.7 = (bf16[4,160,128]{2,1,0:T(8,128)(2,1)S(1)}, bf16[4,160,128]{2,1,0:T(8,128)(2,1)S(1)}, u32[]{:S(2)}, u32[]{:S(2)}) collective-permute-start(bf16[4,160,128]{2,1,0:T(8,128)(2,1)S(1)} %get-tuple-element.57), channel_id=1, source_target_pairs={{0,1},{1,0},{2,3},{3,2},{4,5},{5,4},{6,7},{7,6},{8,24},{9,25},{10,... | collective-permute-start | bytes 491528 | tf_op jit(solution)/shard_map/ppermute | solution.py:280
  25.1 0.0 collective-permute-done.3.refs_2_
  25.1 0.5 %back.1 = bf16[256,512]{1,0:T(8,128)(2,1)S(1)} custom-call(bf16[512,1024]{1,0:T(8,128)(2,1)S(1)} %get-tuple-element.54.pg_ref, bf16[1024,1024]{1,0:T(8,128)(2,1)S(1)} %get-tuple-element.35.wc_ref), custom_call_target="tpu_custom_call" | custom-call | flops 268435456 | bytes 3407872 | tf_op jit(solution)/shard_map/back/pallas_call | solution.py:233
  25.6 0.9 %collective-permute-start.4 = (bf16[256,512]{1,0:T(8,128)(2,1)S(1)}, bf16[256,512]{1,0:T(8,128)(2,1)S(1)}, u32[]{:S(2)}, u32[]{:S(2)}) collective-permute-start(bf16[256,512]{1,0:T(8,128)(2,1)S(1)} %back.1), channel_id=1, source_target_pairs={{8,0},{16,8},{24,16},{0,24},{9,1},{17,9},{25,17},{1,25},{10,2},{18... | collective-permute-start | bytes 786440 | tf_op jit(solution)/shard_map/ppermute | solution.py:332
  26.5 1.9 %collective-permute-done.7.refs_0_ = bf16[4,160,128]{2,1,0:T(8,128)(2,1)S(1)} collective-permute-done((bf16[4,160,128]{2,1,0:T(8,128)(2,1)S(1)}, bf16[4,160,128]{2,1,0:T(8,128)(2,1)S(1)}, u32[]{:S(2)}, u32[]{:S(2)}) %collective-permute-start.7) | collective-permute-done | bytes 163872 | tf_op jit(solution)/shard_map/ppermute | solution.py:280
  28.4 0.1 far.1
  28.5 4.2 %collective-permute-start.8 = (bf16[320,128]{1,0:T(8,128)(2,1)S(1)}, bf16[320,128]{1,0:T(8,128)(2,1)S(1)}, u32[]{:S(2)}, u32[]{:S(2)}) collective-permute-start(bf16[320,128]{1,0:T(8,128)(2,1)S(1)} %get-tuple-element.60), channel_id=1, source_target_pairs={{0,6},{1,7},{2,4},{3,5},{4,2},{5,3},{6,0},{7,1},{8,14},{9,15},{10,... | collective-permute-start | bytes 245768 | tf_op jit(solution)/shard_map/ppermute | solution.py:263
  32.6 0.0 collective-permute-start.9
  32.6 0.6 %collective-permute-start.10 = (bf16[320,128]{1,0:T(8,128)(2,1)S(1)}, bf16[320,128]{1,0:T(8,128)(2,1)S(1)}, u32[]{:S(2)}, u32[]{:S(2)}) collective-permute-start(bf16[320,128]{1,0:T(8,128)(2,1)S(1)} %get-tuple-element.64), channel_id=1, source_target_pairs={{0,2},{1,3},{2,0},{3,1},{4,6},{5,7},{6,4},{7,5},{8,10},{9,11},{10,... | collective-permute-start | bytes 245768 | tf_op jit(solution)/shard_map/ppermute | solution.py:263
  33.3 1.0 %input.1 = (bf16[256,512]{1,0:T(8,128)(2,1)S(1)}, f32[256,512]{1,0:T(8,128)S(1)}) custom-call(bf16[512,1024]{1,0:T(8,128)(2,1)S(1)} %get-tuple-element.54.pg_ref, bf16[1024,1024]{1,0:T(8,128)(2,1)S(1)} %get-tuple-element.35.wc_ref, bf16[512,512]{1,0:T(8,128)(2,1)S(1)} %get-tuple-element.43.c_ref, ...), custom_call_target="tpu_custom_call", output_to_operand_aliasing={{0}: (3, {}), {1}: (4, {})} | custom-call | flops 1073741824 | bytes 5242880 | tf_op jit(solution)/shard_map/input/pallas_call | solution.py:233
  34.3 0.0 collective-permute-done.4.arrived_ref
  34.3 0.9 %rows.1 = bf16[512,512]{1,0:T(8,128)(2,1)} custom-call(bf16[256,512]{1,0:T(8,128)(2,1)S(1)} %get-tuple-element.51.lo_ref, f32[256,512]{1,0:T(8,128)S(1)} %get-tuple-element.52.hi_ref, bf16[256,512]{1,0:T(8,128)(2,1)S(1)} %collective-permute-done.4.arrived_ref), custom_call_target="tpu_custom_call" | custom-call | flops 262144 | bytes 1572864 | tf_op jit(solution)/shard_map/rows/pallas_call | solution.py:233
  35.2 0.2 collective-permute-done.8.refs_0_
  35.4 2.6 %collective-permute-done.9.refs_1_ = bf16[320,128]{1,0:T(8,128)(2,1)S(1)} collective-permute-done((bf16[320,128]{1,0:T(8,128)(2,1)S(1)}, bf16[320,128]{1,0:T(8,128)(2,1)S(1)}, u32[]{:S(2)}, u32[]{:S(2)}) %collective-permute-start.9) | collective-permute-done | bytes 81952 | tf_op jit(solution)/shard_map/ppermute | solution.py:263
  38.0 0.0 collective-permute-done.10.refs_3_
  38.0 0.7 %final.1 = (f32[256,128]{1,0:T(8,128)}, f32[64,128]{1,0:T(8,128)}) custom-call(bf16[320,128]{1,0:T(8,128)(2,1)S(1)} %collective-permute-done.8.refs_0_, bf16[320,128]{1,0:T(8,128)(2,1)S(1)} %collective-permute-done.9.refs_1_, bf16[320,128]{1,0:T(8,128)(2,1)S(1)} %get-tuple-element.63.refs_2_, bf16[320,128]{1,0:T(8,128)(2,1)S(1)} %collective-permute-done.10.refs_3_), custom_call_target="tpu_custom_call" | custom-call | flops 327680 | bytes 491520 | tf_op jit(solution)/shard_map/final/pallas_call | solution.py:233
Async XLA Ops:
  1.6 6.5 %collective-permute-start = (bf16[256,512]{1,0:T(8,128)(2,1)S(1)}, bf16[256,512]{1,0:T(8,128)(2,1)S(1)}, u32[]{:S(2)}, u32[]{:S(2)}) collective-permute-start(bf16[256,512]{1,0:T(8,128)(2,1)S(1)} %slice_bitcast_fusion), channel_id=1, source_target_pairs={{0,8},{8,16},{16,24},{24,0},{1,9},{9,17},{17,25},{25,1},{2,10},{10... | collective-permute-start | bytes 786440 | tf_op jit(solution)/shard_map/ppermute | solution.py:265
  9.2 2.4 %collective-permute-start.1 = (bf16[2,8,160,128]{3,2,1,0:T(8,128)(2,1)S(1)}, bf16[2,8,160,128]{3,2,1,0:T(8,128)(2,1)S(1)}, u32[]{:S(2)}, u32[]{:S(2)}) collective-permute-start(bf16[2,8,160,128]{3,2,1,0:T(8,128)(2,1)S(1)} %get-tuple-element.44), channel_id=1, source_target_pairs={{0,8},{1,9},{2,10},{3,11},{4,12},{5,13},{6,14},{7,15},{8,0},{9,1},... | collective-permute-start | bytes 1966088 | tf_op jit(solution)/shard_map/ppermute | solution.py:263
  10.4 4.0 %collective-permute-start.5 = (bf16[2,8,160,128]{3,2,1,0:T(8,128)(2,1)S(1)}, bf16[2,8,160,128]{3,2,1,0:T(8,128)(2,1)S(1)}, u32[]{:S(2)}, u32[]{:S(2)}) collective-permute-start(bf16[2,8,160,128]{3,2,1,0:T(8,128)(2,1)S(1)} %terms01.1), channel_id=1, source_target_pairs={{0,8},{1,9},{2,10},{3,11},{4,12},{5,13},{6,14},{7,15},{8,0},{9,1},... | collective-permute-start | bytes 1966088 | tf_op jit(solution)/shard_map/ppermute | solution.py:263
  11.8 7.2 %collective-permute-start.2 = (bf16[8,160,128]{2,1,0:T(8,128)(2,1)S(1)}, bf16[8,160,128]{2,1,0:T(8,128)(2,1)S(1)}, u32[]{:S(2)}, u32[]{:S(2)}) collective-permute-start(bf16[8,160,128]{2,1,0:T(8,128)(2,1)S(1)} %get-tuple-element.47), channel_id=1, source_target_pairs={{0,16},{1,17},{2,18},{3,19},{4,20},{5,21},{6,22},{7,23},{8,9},{9,8... | collective-permute-start | bytes 983048 | tf_op jit(solution)/shard_map/ppermute | solution.py:280
  14.6 8.0 %collective-permute-start.6 = (bf16[8,160,128]{2,1,0:T(8,128)(2,1)S(1)}, bf16[8,160,128]{2,1,0:T(8,128)(2,1)S(1)}, u32[]{:S(2)}, u32[]{:S(2)}) collective-permute-start(bf16[8,160,128]{2,1,0:T(8,128)(2,1)S(1)} %get-tuple-element.55), channel_id=1, source_target_pairs={{0,16},{1,17},{2,18},{3,19},{4,20},{5,21},{6,22},{7,23},{8,9},{9,8... | collective-permute-start | bytes 983048 | tf_op jit(solution)/shard_map/ppermute | solution.py:280
  19.1 6.0 %collective-permute-start.3 = (bf16[4,160,128]{2,1,0:T(8,128)(2,1)S(1)}, bf16[4,160,128]{2,1,0:T(8,128)(2,1)S(1)}, u32[]{:S(2)}, u32[]{:S(2)}) collective-permute-start(bf16[4,160,128]{2,1,0:T(8,128)(2,1)S(1)} %get-tuple-element.53), channel_id=1, source_target_pairs={{0,1},{1,0},{2,3},{3,2},{4,5},{5,4},{6,7},{7,6},{8,24},{9,25},{10,... | collective-permute-start | bytes 491528 | tf_op jit(solution)/shard_map/ppermute | solution.py:280
  22.7 5.7 %collective-permute-start.7 = (bf16[4,160,128]{2,1,0:T(8,128)(2,1)S(1)}, bf16[4,160,128]{2,1,0:T(8,128)(2,1)S(1)}, u32[]{:S(2)}, u32[]{:S(2)}) collective-permute-start(bf16[4,160,128]{2,1,0:T(8,128)(2,1)S(1)} %get-tuple-element.57), channel_id=1, source_target_pairs={{0,1},{1,0},{2,3},{3,2},{4,5},{5,4},{6,7},{7,6},{8,24},{9,25},{10,... | collective-permute-start | bytes 491528 | tf_op jit(solution)/shard_map/ppermute | solution.py:280
  25.6 8.7 %collective-permute-start.4 = (bf16[256,512]{1,0:T(8,128)(2,1)S(1)}, bf16[256,512]{1,0:T(8,128)(2,1)S(1)}, u32[]{:S(2)}, u32[]{:S(2)}) collective-permute-start(bf16[256,512]{1,0:T(8,128)(2,1)S(1)} %back.1), channel_id=1, source_target_pairs={{8,0},{16,8},{24,16},{0,24},{9,1},{17,9},{25,17},{1,25},{10,2},{18... | collective-permute-start | bytes 786440 | tf_op jit(solution)/shard_map/ppermute | solution.py:332
  28.5 6.9 %collective-permute-start.8 = (bf16[320,128]{1,0:T(8,128)(2,1)S(1)}, bf16[320,128]{1,0:T(8,128)(2,1)S(1)}, u32[]{:S(2)}, u32[]{:S(2)}) collective-permute-start(bf16[320,128]{1,0:T(8,128)(2,1)S(1)} %get-tuple-element.60), channel_id=1, source_target_pairs={{0,6},{1,7},{2,4},{3,5},{4,2},{5,3},{6,0},{7,1},{8,14},{9,15},{10,... | collective-permute-start | bytes 245768 | tf_op jit(solution)/shard_map/ppermute | solution.py:263
  32.6 5.3 %collective-permute-start.9 = (bf16[320,128]{1,0:T(8,128)(2,1)S(1)}, bf16[320,128]{1,0:T(8,128)(2,1)S(1)}, u32[]{:S(2)}, u32[]{:S(2)}) collective-permute-start(bf16[320,128]{1,0:T(8,128)(2,1)S(1)} %get-tuple-element.62), channel_id=1, source_target_pairs={{0,4},{1,5},{2,6},{3,7},{4,0},{5,1},{6,2},{7,3},{8,12},{9,13},{10,... | collective-permute-start | bytes 245768 | tf_op jit(solution)/shard_map/ppermute | solution.py:263
  32.6 5.3 %collective-permute-start.10 = (bf16[320,128]{1,0:T(8,128)(2,1)S(1)}, bf16[320,128]{1,0:T(8,128)(2,1)S(1)}, u32[]{:S(2)}, u32[]{:S(2)}) collective-permute-start(bf16[320,128]{1,0:T(8,128)(2,1)S(1)} %get-tuple-element.64), channel_id=1, source_target_pairs={{0,2},{1,3},{2,0},{3,1},{4,6},{5,7},{6,4},{7,5},{8,10},{9,11},{10,... | collective-permute-start | bytes 245768 | tf_op jit(solution)/shard_map/ppermute | solution.py:263

commit v5 on v4

--- a/solution.py
+++ b/solution.py
@@ -89,7 +89,7 @@
         picked = [2 * i + parity for i in range(blocks // 2)]
         earlier = [jnp.concatenate([ht_ref[i, some], xt_ref[i, some, : rows - back]], 1) for i in picked]
         left = jnp.concatenate(earlier + [xt_ref[i, some] for i in picked], 0)
-        wide = min(256, columns)
+        wide = min(512, columns)
         for j in range(0, columns, wide):
             term = dot(left, pg_ref[:, j : j + wide]).astype(BF16)
             for t in range(halves):
@@ -134,9 +134,15 @@
     block_products(first, parity, xt_ref, ht_ref, ct_ref, pg_ref, gb_ref, out_ref)
 
 
-def back_kernel(pg_ref, wc_ref, back_ref):
+def back_product(pg_ref, wc_ref, back_ref):
     step, channels = back_ref.shape
     back_ref[...] = dot_nt(pg_ref[:step, :], wc_ref[:channels, :]).astype(BF16)
+
+
+def back_kernel(pg_ref, wc_ref, back_in, back_ref):
+    @pl.when(lax.rem(lax.axis_index("tm"), 2) == 0)
+    def _():
+        back_product(pg_ref, wc_ref, back_ref)
 
 
 def input_gradient(pg_ref, wc_ref, c_ref, lo_ref, hi_ref):
@@ -186,10 +192,11 @@
             out[far] = (got_ref[j].astype(F32) + kept_ref[j].astype(F32)).astype(BF16)
 
 
-def half_input_kernel(count_z, got_ref, kept_ref, pg_ref, wc_ref, c_ref, stay_ref, send_ref, lo_ref, hi_ref):
+def half_input_kernel(count_z, got_ref, kept_ref, pg_ref, wc_ref, c_ref, stay_ref, send_ref, lo_ref, hi_ref, back_ref):
     @pl.when(lax.rem(lax.axis_index("tm"), 2) == 1)
     def _():
         input_gradient(pg_ref, wc_ref, c_ref, lo_ref, hi_ref)
+        back_product(pg_ref, wc_ref, back_ref)
 
     half_kernel(count_z, got_ref, kept_ref, stay_ref, send_ref)
 
@@ -313,8 +320,8 @@
     input_shapes = [((rows - step, channels), BF16), ((step, channels), F32)]
     for c, size in enumerate(sizes):
         if c == 1:
-            stay, send, lo, hi = call(
-                functools.partial(half_input_kernel, count_z), [((fars, size, lanes), BF16)] * 2 + input_shapes,
+            stay, send, lo, hi, back = call(
+                functools.partial(half_input_kernel, count_z), [((fars, size, lanes), BF16)] * 2 + input_shapes + [((step, channels), BF16)],
                 2 * fars * size * lanes, *sums[c], pg, wc, c_in, name=f"half{c}",
             )
         else:
@@ -323,7 +330,7 @@
                 2 * fars * size * lanes, *sums[c], name=f"half{c}",
             )
         parts += [swap_mixed(send, y_mask, x_mask), stay]
-    (back,) = call(back_kernel, [((step, channels), BF16)], product, after(pg, parts[2]), wc, name="back")
+    (back,) = call(back_kernel, [((step, channels), BF16)], product, after(pg, parts[2]), wc, back, name="back", aliases={2: 0})
     lo, hi = call(input_kernel, input_shapes, product * 4, pg, wc, c_in, lo, hi, name="input", aliases={3: 0, 4: 1})
     outs = call(
         functools.partial(far_kernel, count_z), [((height, lanes), BF16)] * fars,

time: 38.8 us -> 38.7 us (level)
  starting transfers between devices: 13.9 us -> 13.5 us
  transfers between devices with their start and end apart: 11 -> 11, of which waited for: 7 -> 6; matrix products, arithmetic and copies ran while one was open for 0% -> 0% of each run, Pallas kernels for 20% -> 20%
where the time goes in v5:
time: 38.7 us; the launch traced here: 38.5 us
  starting transfers between devices  13.5 us (35%)
  waiting for transfers between devices  13.2 us (34%)
  Pallas kernels  9.54 us (25%)
  between operations  1.38 us (4%)
  local copies, waits for them, and re-layouts  0.97 us (3%)
    pallas_call x14, Pallas kernels, call(): pl.pallas_call(kernel, out_shape=out_shape, in_specs=[spec(i, a) for i, a...  9.54 us
    ppermute x4, waiting for transfers between devices, swap_mixed(): lax.ppermute(array, ('tm', 'rep'), [(i, i ^ (second_mask if core_of(i) el...  7.56 us
    ppermute x4, starting transfers between devices, swap_mixed(): lax.ppermute(array, ('tm', 'rep'), [(i, i ^ (second_mask if core_of(i) el...  6.76 us
    ppermute x5, starting transfers between devices, swap(): lax.ppermute(array, ('tm', 'rep'), [(i, i ^ mask) for i in range(devices)])  5.53 us
    ppermute x5, waiting for transfers between devices, swap(): lax.ppermute(array, ('tm', 'rep'), [(i, i ^ mask) for i in range(devices)])  3.55 us
    ppermute x1, waiting for transfers between devices, body(): lax.ppermute(x[rows - step:], 'tm', [(i, (i + 1) % tms) for i in range(tm...  2.04 us
    slice x1, local copies, waits for them, and re-layouts, body(): x[rows - step:]  0.97 us
  transfers between devices with their start and end apart: 11, of which 6 were waited for; matrix products, arithmetic and copies ran while one was open for 0% of the time, Pallas kernels for 20%

profile of v5, /device:TPU:0, one launch (start us, length us, event | category | flops | bytes accessed | tf_op | source)
XLA Modules:
  0.0 38.5 jit_solution(3701793707525884421)
XLA Ops:
  0.6 1.0 %slice_bitcast_fusion = bf16[256,512]{1,0:T(8,128)(2,1)S(1)} fusion(bf16[1,512,512]{2,1,0:T(8,128)(2,1)} %param.5), kind=kLoop, calls=%fused_computation | loop fusion | bytes 524288 | tf_op jit(solution)/shard_map/slice | solution.py:272
  1.6 0.5 %collective-permute-start = (bf16[256,512]{1,0:T(8,128)(2,1)S(1)}, bf16[256,512]{1,0:T(8,128)(2,1)S(1)}, u32[]{:S(2)}, u32[]{:S(2)}) collective-permute-start(bf16[256,512]{1,0:T(8,128)(2,1)S(1)} %slice_bitcast_fusion), channel_id=1, source_target_pairs={{0,8},{8,16},{16,24},{24,0},{1,9},{9,17},{17,25},{25,1},{2,10},{10... | collective-permute-start | bytes 786440 | tf_op jit(solution)/shard_map/ppermute | solution.py:272
  2.8 3.3 %local.1 = (bf16[2,256,512]{2,1,0:T(8,128)(2,1)S(1)}, bf16[512,512]{1,0:T(8,128)(2,1)S(1)}, f32[256,1024]{1,0:T(8,128)S(1)}, f32[256,512]{1,0:T(8,128)S(1)}, bf1...) custom-call(s32[1]{0:T(128)S(6)} %copy.18.lengths_ref, ...), custom_call_target="tpu_custom_call" | custom-call | flops 1073741824 | bytes 10485764 | tf_op jit(solution)/shard_map/local/pallas_call | solution.py:240
  6.0 2.0 %collective-permute-done.halo_ref = bf16[256,512]{1,0:T(8,128)(2,1)S(1)} collective-permute-done((bf16[256,512]{1,0:T(8,128)(2,1)S(1)}, bf16[256,512]{1,0:T(8,128)(2,1)S(1)}, u32[]{:S(2)}, u32[]{:S(2)}) %collective-permute-start) | collective-permute-done | bytes 262176 | tf_op jit(solution)/shard_map/ppermute | solution.py:272
  8.1 1.1 %partner.1 = (bf16[512,1024]{1,0:T(8,128)(2,1)S(1)}, bf16[4,512,128]{2,1,0:T(8,128)(2,1)S(1)}, bf16[2,256,256]{2,1,0:T(8,128)(2,1)S(1)}, bf16[2,8,160,128]{3,2,1,0:T(8,128)(2,1)S(1)}) custom-call(s32[1]{0:T(128)S(6)} %copy.18.lengths_ref, bf16[256,512]{1,0:T(8,128)(2,1)S(1)} %collective-permute-done.halo_ref, ...), custom_call_target="tpu_custom_call", output_to_operand_aliasing={{0}: (7, {}), {1}: (8, {})} | custom-call | flops 805306368 | bytes 9043972 | tf_op jit(solution)/shard_map/partner/pallas_call | solution.py:240
  9.2 0.6 %collective-permute-start.1 = (bf16[2,8,160,128]{3,2,1,0:T(8,128)(2,1)S(1)}, bf16[2,8,160,128]{3,2,1,0:T(8,128)(2,1)S(1)}, u32[]{:S(2)}, u32[]{:S(2)}) collective-permute-start(bf16[2,8,160,128]{3,2,1,0:T(8,128)(2,1)S(1)} %get-tuple-element.45), channel_id=1, source_target_pairs={{0,8},{1,9},{2,10},{3,11},{4,12},{5,13},{6,14},{7,15},{8,0},{9,1},... | collective-permute-start | bytes 1966088 | tf_op jit(solution)/shard_map/ppermute | solution.py:270
  9.9 0.5 %terms01.1 = bf16[2,8,160,128]{3,2,1,0:T(8,128)(2,1)S(1)} custom-call(bf16[2,256,512]{2,1,0:T(8,128)(2,1)S(1)} %get-tuple-element.37.xt_ref, bf16[2,256,256]{2,1,0:T(8,128)(2,1)S(1)} %get-tuple-element.46.ht_ref, bf16[512,512]{1,0:T(8,128)(2,1)S(1)} %get-tuple-element.38.ct_ref, bf16[512,1024]{1,0:T(8,128)(2,1)S(1)} %get-tuple-element.55.pg_ref, ...), custom_call_target="tpu_custom_call" | custom-call | flops 536870912 | bytes 3538944 | tf_op jit(solution)/shard_map/terms01/pallas_call | solution.py:240
  10.4 0.1 collective-permute-start.5
  10.5 0.5 %terms10.1.kept_ref = bf16[2,8,160,128]{3,2,1,0:T(8,128)(2,1)S(1)} custom-call(bf16[2,256,512]{2,1,0:T(8,128)(2,1)S(1)} %get-tuple-element.37.xt_ref, bf16[2,256,256]{2,1,0:T(8,128)(2,1)S(1)} %get-tuple-element.46.ht_ref, bf16[512,512]{1,0:T(8,128)(2,1)S(1)} %get-tuple-element.38.ct_ref, bf16[512,1024]{1,0:T(8,128)(2,1)S(1)} %get-tuple-element.55.pg_ref, ...), custom_call_target="tpu_custom_call" | custom-call | flops 536870912 | bytes 3538944 | tf_op jit(solution)/shard_map/terms10/pallas_call | solution.py:240
  11.0 0.6 %collective-permute-done.1.got_ref = bf16[2,8,160,128]{3,2,1,0:T(8,128)(2,1)S(1)} collective-permute-done((bf16[2,8,160,128]{3,2,1,0:T(8,128)(2,1)S(1)}, bf16[2,8,160,128]{3,2,1,0:T(8,128)(2,1)S(1)}, u32[]{:S(2)}, u32[]{:S(2)}) %collective-permute-start.1) | collective-permute-done | bytes 655392 | tf_op jit(solution)/shard_map/ppermute | solution.py:270
  11.6 0.2 split1.1
  11.8 2.2 %collective-permute-start.2 = (bf16[8,160,128]{2,1,0:T(8,128)(2,1)S(1)}, bf16[8,160,128]{2,1,0:T(8,128)(2,1)S(1)}, u32[]{:S(2)}, u32[]{:S(2)}) collective-permute-start(bf16[8,160,128]{2,1,0:T(8,128)(2,1)S(1)} %get-tuple-element.48), channel_id=1, source_target_pairs={{0,16},{1,17},{2,18},{3,19},{4,20},{5,21},{6,22},{7,23},{8,9},{9,8... | collective-permute-start | bytes 983048 | tf_op jit(solution)/shard_map/ppermute | solution.py:287
  13.9 0.5 %terms00.1.kept_ref = bf16[2,8,160,128]{3,2,1,0:T(8,128)(2,1)S(1)} custom-call(bf16[2,256,512]{2,1,0:T(8,128)(2,1)S(1)} %get-tuple-element.37.xt_ref, bf16[2,256,256]{2,1,0:T(8,128)(2,1)S(1)} %get-tuple-element.46.ht_ref, bf16[512,512]{1,0:T(8,128)(2,1)S(1)} %get-tuple-element.38.ct_ref, bf16[512,1024]{1,0:T(8,128)(2,1)S(1)} %get-tuple-element.55.pg_ref, ...), custom_call_target="tpu_custom_call" | custom-call | flops 536870912 | bytes 3538944 | tf_op jit(solution)/shard_map/terms00/pallas_call | solution.py:240
  14.4 0.0 collective-permute-done.5.got_ref
  14.4 0.2 split0.1
  14.6 0.2 collective-permute-start.6
  14.9 4.1 %collective-permute-done.2.got_ref = bf16[8,160,128]{2,1,0:T(8,128)(2,1)S(1)} collective-permute-done((bf16[8,160,128]{2,1,0:T(8,128)(2,1)S(1)}, bf16[8,160,128]{2,1,0:T(8,128)(2,1)S(1)}, u32[]{:S(2)}, u32[]{:S(2)}) %collective-permute-start.2) | collective-permute-done | bytes 327712 | tf_op jit(solution)/shard_map/ppermute | solution.py:287
  19.0 0.1 half1.1
  19.1 2.1 %collective-permute-start.3 = (bf16[4,160,128]{2,1,0:T(8,128)(2,1)S(1)}, bf16[4,160,128]{2,1,0:T(8,128)(2,1)S(1)}, u32[]{:S(2)}, u32[]{:S(2)}) collective-permute-start(bf16[4,160,128]{2,1,0:T(8,128)(2,1)S(1)} %get-tuple-element.54), channel_id=1, source_target_pairs={{0,1},{1,0},{2,3},{3,2},{4,5},{5,4},{6,7},{7,6},{8,24},{9,25},{10,... | collective-permute-start | bytes 491528 | tf_op jit(solution)/shard_map/ppermute | solution.py:287
  21.2 1.3 %collective-permute-done.6.got_ref = bf16[8,160,128]{2,1,0:T(8,128)(2,1)S(1)} collective-permute-done((bf16[8,160,128]{2,1,0:T(8,128)(2,1)S(1)}, bf16[8,160,128]{2,1,0:T(8,128)(2,1)S(1)}, u32[]{:S(2)}, u32[]{:S(2)}) %collective-permute-start.6) | collective-permute-done | bytes 327712 | tf_op jit(solution)/shard_map/ppermute | solution.py:287
  22.5 0.1 half0.1
  22.6 2.2 %collective-permute-start.7 = (bf16[4,160,128]{2,1,0:T(8,128)(2,1)S(1)}, bf16[4,160,128]{2,1,0:T(8,128)(2,1)S(1)}, u32[]{:S(2)}, u32[]{:S(2)}) collective-permute-start(bf16[4,160,128]{2,1,0:T(8,128)(2,1)S(1)} %get-tuple-element.59), channel_id=1, source_target_pairs={{0,1},{1,0},{2,3},{3,2},{4,5},{5,4},{6,7},{7,6},{8,24},{9,25},{10,... | collective-permute-start | bytes 491528 | tf_op jit(solution)/shard_map/ppermute | solution.py:287
  24.8 0.0 collective-permute-done.3.refs_2_
  24.8 0.5 %back.1 = bf16[256,512]{1,0:T(8,128)(2,1)S(1)} custom-call(bf16[512,1024]{1,0:T(8,128)(2,1)S(1)} %get-tuple-element.55.pg_ref, bf16[1024,1024]{1,0:T(8,128)(2,1)S(1)} %get-tuple-element.36.wc_ref, bf16[256,512]{1,0:T(8,128)(2,1)S(1)} %get-tuple-element.56.back_in), custom_call_target="tpu_custom_call", output_to_operand_aliasing={{}: (2, {})} | custom-call | flops 268435456 | bytes 3670016 | tf_op jit(solution)/shard_map/back/pallas_call | solution.py:240
  25.3 0.7 %collective-permute-start.4 = (bf16[256,512]{1,0:T(8,128)(2,1)S(1)}, bf16[256,512]{1,0:T(8,128)(2,1)S(1)}, u32[]{:S(2)}, u32[]{:S(2)}) collective-permute-start(bf16[256,512]{1,0:T(8,128)(2,1)S(1)} %back.1), channel_id=1, source_target_pairs={{8,0},{16,8},{24,16},{0,24},{9,1},{17,9},{25,17},{1,25},{10,2},{18... | collective-permute-start | bytes 786440 | tf_op jit(solution)/shard_map/ppermute | solution.py:339
  26.0 2.1 %collective-permute-done.7.refs_0_ = bf16[4,160,128]{2,1,0:T(8,128)(2,1)S(1)} collective-permute-done((bf16[4,160,128]{2,1,0:T(8,128)(2,1)S(1)}, bf16[4,160,128]{2,1,0:T(8,128)(2,1)S(1)}, u32[]{:S(2)}, u32[]{:S(2)}) %collective-permute-start.7) | collective-permute-done | bytes 163872 | tf_op jit(solution)/shard_map/ppermute | solution.py:287
  28.1 0.1 far.1
  28.2 4.2 %collective-permute-start.8 = (bf16[320,128]{1,0:T(8,128)(2,1)S(1)}, bf16[320,128]{1,0:T(8,128)(2,1)S(1)}, u32[]{:S(2)}, u32[]{:S(2)}) collective-permute-start(bf16[320,128]{1,0:T(8,128)(2,1)S(1)} %get-tuple-element.62), channel_id=1, source_target_pairs={{0,6},{1,7},{2,4},{3,5},{4,2},{5,3},{6,0},{7,1},{8,14},{9,15},{10,... | collective-permute-start | bytes 245768 | tf_op jit(solution)/shard_map/ppermute | solution.py:270
  32.4 0.0 collective-permute-start.9
  32.4 0.6 %collective-permute-start.10 = (bf16[320,128]{1,0:T(8,128)(2,1)S(1)}, bf16[320,128]{1,0:T(8,128)(2,1)S(1)}, u32[]{:S(2)}, u32[]{:S(2)}) collective-permute-start(bf16[320,128]{1,0:T(8,128)(2,1)S(1)} %get-tuple-element.66), channel_id=1, source_target_pairs={{0,2},{1,3},{2,0},{3,1},{4,6},{5,7},{6,4},{7,5},{8,10},{9,11},{10,... | collective-permute-start | bytes 245768 | tf_op jit(solution)/shard_map/ppermute | solution.py:270
  33.0 1.0 %input.1 = (bf16[256,512]{1,0:T(8,128)(2,1)S(1)}, f32[256,512]{1,0:T(8,128)S(1)}) custom-call(bf16[512,1024]{1,0:T(8,128)(2,1)S(1)} %get-tuple-element.55.pg_ref, bf16[1024,1024]{1,0:T(8,128)(2,1)S(1)} %get-tuple-element.36.wc_ref, bf16[512,512]{1,0:T(8,128)(2,1)S(1)} %get-tuple-element.44.c_ref, ...), custom_call_target="tpu_custom_call", output_to_operand_aliasing={{0}: (3, {}), {1}: (4, {})} | custom-call | flops 1073741824 | bytes 5242880 | tf_op jit(solution)/shard_map/input/pallas_call | solution.py:240
  34.0 0.0 collective-permute-done.4.arrived_ref
  34.0 0.9 %rows.1 = bf16[512,512]{1,0:T(8,128)(2,1)} custom-call(bf16[256,512]{1,0:T(8,128)(2,1)S(1)} %get-tuple-element.52.lo_ref, f32[256,512]{1,0:T(8,128)S(1)} %get-tuple-element.53.hi_ref, bf16[256,512]{1,0:T(8,128)(2,1)S(1)} %collective-permute-done.4.arrived_ref), custom_call_target="tpu_custom_call" | custom-call | flops 262144 | bytes 1572864 | tf_op jit(solution)/shard_map/rows/pallas_call | solution.py:240
  34.9 0.0 collective-permute-done.8.refs_0_
  34.9 2.9 %collective-permute-done.9.refs_1_ = bf16[320,128]{1,0:T(8,128)(2,1)S(1)} collective-permute-done((bf16[320,128]{1,0:T(8,128)(2,1)S(1)}, bf16[320,128]{1,0:T(8,128)(2,1)S(1)}, u32[]{:S(2)}, u32[]{:S(2)}) %collective-permute-start.9) | collective-permute-done | bytes 81952 | tf_op jit(solution)/shard_map/ppermute | solution.py:270
  37.8 0.0 collective-permute-done.10.refs_3_
  37.8 0.7 %final.1 = (f32[256,128]{1,0:T(8,128)}, f32[64,128]{1,0:T(8,128)}) custom-call(bf16[320,128]{1,0:T(8,128)(2,1)S(1)} %collective-permute-done.8.refs_0_, bf16[320,128]{1,0:T(8,128)(2,1)S(1)} %collective-permute-done.9.refs_1_, bf16[320,128]{1,0:T(8,128)(2,1)S(1)} %get-tuple-element.65.refs_2_, bf16[320,128]{1,0:T(8,128)(2,1)S(1)} %collective-permute-done.10.refs_3_), custom_call_target="tpu_custom_call" | custom-call | flops 327680 | bytes 491520 | tf_op jit(solution)/shard_map/final/pallas_call | solution.py:240
Async XLA Ops:
  1.6 6.5 %collective-permute-start = (bf16[256,512]{1,0:T(8,128)(2,1)S(1)}, bf16[256,512]{1,0:T(8,128)(2,1)S(1)}, u32[]{:S(2)}, u32[]{:S(2)}) collective-permute-start(bf16[256,512]{1,0:T(8,128)(2,1)S(1)} %slice_bitcast_fusion), channel_id=1, source_target_pairs={{0,8},{8,16},{16,24},{24,0},{1,9},{9,17},{17,25},{25,1},{2,10},{10... | collective-permute-start | bytes 786440 | tf_op jit(solution)/shard_map/ppermute | solution.py:272
  9.2 2.4 %collective-permute-start.1 = (bf16[2,8,160,128]{3,2,1,0:T(8,128)(2,1)S(1)}, bf16[2,8,160,128]{3,2,1,0:T(8,128)(2,1)S(1)}, u32[]{:S(2)}, u32[]{:S(2)}) collective-permute-start(bf16[2,8,160,128]{3,2,1,0:T(8,128)(2,1)S(1)} %get-tuple-element.45), channel_id=1, source_target_pairs={{0,8},{1,9},{2,10},{3,11},{4,12},{5,13},{6,14},{7,15},{8,0},{9,1},... | collective-permute-start | bytes 1966088 | tf_op jit(solution)/shard_map/ppermute | solution.py:270
  10.4 4.0 %collective-permute-start.5 = (bf16[2,8,160,128]{3,2,1,0:T(8,128)(2,1)S(1)}, bf16[2,8,160,128]{3,2,1,0:T(8,128)(2,1)S(1)}, u32[]{:S(2)}, u32[]{:S(2)}) collective-permute-start(bf16[2,8,160,128]{3,2,1,0:T(8,128)(2,1)S(1)} %terms01.1), channel_id=1, source_target_pairs={{0,8},{1,9},{2,10},{3,11},{4,12},{5,13},{6,14},{7,15},{8,0},{9,1},... | collective-permute-start | bytes 1966088 | tf_op jit(solution)/shard_map/ppermute | solution.py:270
  11.8 7.2 %collective-permute-start.2 = (bf16[8,160,128]{2,1,0:T(8,128)(2,1)S(1)}, bf16[8,160,128]{2,1,0:T(8,128)(2,1)S(1)}, u32[]{:S(2)}, u32[]{:S(2)}) collective-permute-start(bf16[8,160,128]{2,1,0:T(8,128)(2,1)S(1)} %get-tuple-element.48), channel_id=1, source_target_pairs={{0,16},{1,17},{2,18},{3,19},{4,20},{5,21},{6,22},{7,23},{8,9},{9,8... | collective-permute-start | bytes 983048 | tf_op jit(solution)/shard_map/ppermute | solution.py:287
  14.6 7.9 %collective-permute-start.6 = (bf16[8,160,128]{2,1,0:T(8,128)(2,1)S(1)}, bf16[8,160,128]{2,1,0:T(8,128)(2,1)S(1)}, u32[]{:S(2)}, u32[]{:S(2)}) collective-permute-start(bf16[8,160,128]{2,1,0:T(8,128)(2,1)S(1)} %get-tuple-element.57), channel_id=1, source_target_pairs={{0,16},{1,17},{2,18},{3,19},{4,20},{5,21},{6,22},{7,23},{8,9},{9,8... | collective-permute-start | bytes 983048 | tf_op jit(solution)/shard_map/ppermute | solution.py:287
  19.1 5.8 %collective-permute-start.3 = (bf16[4,160,128]{2,1,0:T(8,128)(2,1)S(1)}, bf16[4,160,128]{2,1,0:T(8,128)(2,1)S(1)}, u32[]{:S(2)}, u32[]{:S(2)}) collective-permute-start(bf16[4,160,128]{2,1,0:T(8,128)(2,1)S(1)} %get-tuple-element.54), channel_id=1, source_target_pairs={{0,1},{1,0},{2,3},{3,2},{4,5},{5,4},{6,7},{7,6},{8,24},{9,25},{10,... | collective-permute-start | bytes 491528 | tf_op jit(solution)/shard_map/ppermute | solution.py:287
  22.6 5.5 %collective-permute-start.7 = (bf16[4,160,128]{2,1,0:T(8,128)(2,1)S(1)}, bf16[4,160,128]{2,1,0:T(8,128)(2,1)S(1)}, u32[]{:S(2)}, u32[]{:S(2)}) collective-permute-start(bf16[4,160,128]{2,1,0:T(8,128)(2,1)S(1)} %get-tuple-element.59), channel_id=1, source_target_pairs={{0,1},{1,0},{2,3},{3,2},{4,5},{5,4},{6,7},{7,6},{8,24},{9,25},{10,... | collective-permute-start | bytes 491528 | tf_op jit(solution)/shard_map/ppermute | solution.py:287
  25.3 8.7 %collective-permute-start.4 = (bf16[256,512]{1,0:T(8,128)(2,1)S(1)}, bf16[256,512]{1,0:T(8,128)(2,1)S(1)}, u32[]{:S(2)}, u32[]{:S(2)}) collective-permute-start(bf16[256,512]{1,0:T(8,128)(2,1)S(1)} %back.1), channel_id=1, source_target_pairs={{8,0},{16,8},{24,16},{0,24},{9,1},{17,9},{25,17},{1,25},{10,2},{18... | collective-permute-start | bytes 786440 | tf_op jit(solution)/shard_map/ppermute | solution.py:339
  28.2 6.7 %collective-permute-start.8 = (bf16[320,128]{1,0:T(8,128)(2,1)S(1)}, bf16[320,128]{1,0:T(8,128)(2,1)S(1)}, u32[]{:S(2)}, u32[]{:S(2)}) collective-permute-start(bf16[320,128]{1,0:T(8,128)(2,1)S(1)} %get-tuple-element.62), channel_id=1, source_target_pairs={{0,6},{1,7},{2,4},{3,5},{4,2},{5,3},{6,0},{7,1},{8,14},{9,15},{10,... | collective-permute-start | bytes 245768 | tf_op jit(solution)/shard_map/ppermute | solution.py:270
  32.4 5.5 %collective-permute-start.9 = (bf16[320,128]{1,0:T(8,128)(2,1)S(1)}, bf16[320,128]{1,0:T(8,128)(2,1)S(1)}, u32[]{:S(2)}, u32[]{:S(2)}) collective-permute-start(bf16[320,128]{1,0:T(8,128)(2,1)S(1)} %get-tuple-element.64), channel_id=1, source_target_pairs={{0,4},{1,5},{2,6},{3,7},{4,0},{5,1},{6,2},{7,3},{8,12},{9,13},{10,... | collective-permute-start | bytes 245768 | tf_op jit(solution)/shard_map/ppermute | solution.py:270
  32.4 5.5 %collective-permute-start.10 = (bf16[320,128]{1,0:T(8,128)(2,1)S(1)}, bf16[320,128]{1,0:T(8,128)(2,1)S(1)}, u32[]{:S(2)}, u32[]{:S(2)}) collective-permute-start(bf16[320,128]{1,0:T(8,128)(2,1)S(1)} %get-tuple-element.66), channel_id=1, source_target_pairs={{0,2},{1,3},{2,0},{3,1},{4,6},{5,7},{6,4},{7,5},{8,10},{9,11},{10,... | collective-permute-start | bytes 245768 | tf_op jit(solution)/shard_map/ppermute | solution.py:270

commit v6 on v5

--- a/solution.py
+++ b/solution.py
@@ -206,10 +206,10 @@
     chunks = len(refs) - far_count(refs)
     ins, outs = refs[:chunks], refs[chunks:]
     for d, out in enumerate(outs):
-        first = 0
+        first, to = 0, lax.rem(me + d, len(outs))
         for got_ref, kept_ref in zip(ins[::2], ins[1::2]):
             last = first + got_ref.shape[1]
-            out[first:last, :] = (got_ref[me ^ d].astype(F32) + kept_ref[me ^ d].astype(F32)).astype(BF16)
+            out[first:last, :] = (got_ref[to].astype(F32) + kept_ref[to].astype(F32)).astype(BF16)
             first = last
 
 
@@ -289,7 +289,6 @@
         )
 
     fars = halves // 2 * count_z
-    far_masks = [(d // count_z) * 4 * reps + (d % count_z) * 2 for d in range(fars)]
     core_mask, x_mask, y_mask = reps, 2 * reps, 1
     cut = (height * FIRST_CHUNK // 20) // 16 * 16
     sizes, starts = [cut, height - cut], [0, cut]
@@ -337,8 +336,16 @@
         fars * height * lanes, *parts, name="far",
     )
     arrived = lax.ppermute(back, "tm", [((i + 1) % tms, i) for i in range(tms)])
-    parts = [swap(p, m) if m else p for p, m in zip(outs, far_masks)]
-    parts = parts[:1:-1] + parts[:2]
+    def shifted(array, by):
+        pairs = []
+        for i in range(devices):
+            tm, rep = divmod(i, reps)
+            far = (tm // 4 * count_z + rep // 2 + by) % fars
+            pairs.append((i, (far // count_z * 4 + tm % 4) * reps + far % count_z * 2 + rep % 2))
+        return lax.ppermute(array, ("tm", "rep"), pairs)
+
+    parts = [shifted(p, d) if d else p for d, p in enumerate(outs)]
+    parts = parts[1:] + parts[:1]
     (grad_in,) = call(rows_kernel, [((rows, channels), BF16)], rows * channels, lo, hi, arrived, name="rows")
     scale = float(rows * devices) ** (-0.5)
     conv, res = call(

time: 38.7 us -> 38.8 us (level)
  starting transfers between devices: 13.5 us -> 14.7 us
  waiting for transfers between devices: 13.2 us -> 12 us
    ppermute x0 -> x3, starting transfers between devices: none -> 6.07 us  [shifted(): return lax.ppermute(array, ('tm', 'rep'), pairs)]
    ppermute x5 -> x2, starting transfers between devices: 5.53 us -> 0.73 us  [swap(): lax.ppermute(array, ('tm', 'rep'), [(i, i ^ mask) for i in range(devices)])]
    ppermute x5 -> x2, waiting for transfers between devices: 3.55 us -> 0.61 us  [swap(): lax.ppermute(array, ('tm', 'rep'), [(i, i ^ mask) for i in range(devices)])]
    ppermute x0 -> x3, waiting for transfers between devices: none -> 1.77 us  [shifted(): return lax.ppermute(array, ('tm', 'rep'), pairs)]
  transfers between devices with their start and end apart: 11 -> 11, of which waited for: 6 -> 7; matrix products, arithmetic and copies ran while one was open for 0% -> 0% of each run, Pallas kernels for 20% -> 20%
where the time goes in v6:
time: 38.8 us; the launch traced here: 38.6 us
  starting transfers between devices  14.7 us (38%)
  waiting for transfers between devices  12 us (31%)
  Pallas kernels  9.54 us (25%)
  between operations  1.38 us (4%)
  local copies, waits for them, and re-layouts  0.97 us (2%)
    pallas_call x14, Pallas kernels, call(): pl.pallas_call(kernel, out_shape=out_shape, in_specs=[spec(i, a) for i, a...  9.54 us
    ppermute x4, waiting for transfers between devices, swap_mixed(): lax.ppermute(array, ('tm', 'rep'), [(i, i ^ (second_mask if core_of(i) el...  7.56 us
    ppermute x4, starting transfers between devices, swap_mixed(): lax.ppermute(array, ('tm', 'rep'), [(i, i ^ (second_mask if core_of(i) el...  6.76 us
    ppermute x3, starting transfers between devices, shifted(): return lax.ppermute(array, ('tm', 'rep'), pairs)  6.07 us
    ppermute x1, waiting for transfers between devices, body(): lax.ppermute(x[rows - step:], 'tm', [(i, (i + 1) % tms) for i in range(tm...  2.04 us
    ppermute x3, waiting for transfers between devices, shifted(): return lax.ppermute(array, ('tm', 'rep'), pairs)  1.77 us
    slice x1, local copies, waits for them, and re-layouts, body(): x[rows - step:]  0.97 us
  transfers between devices with their start and end apart: 11, of which 7 were waited for; matrix products, arithmetic and copies ran while one was open for 0% of the time, Pallas kernels for 20%

profile of v6, /device:TPU:0, one launch (start us, length us, event | category | flops | bytes accessed | tf_op | source)
XLA Modules:
  0.0 38.6 jit_solution(10504379945374142443)
XLA Ops:
  0.6 1.0 %slice_bitcast_fusion = bf16[256,512]{1,0:T(8,128)(2,1)S(1)} fusion(bf16[1,512,512]{2,1,0:T(8,128)(2,1)} %param.5), kind=kLoop, calls=%fused_computation | loop fusion | bytes 524288 | tf_op jit(solution)/shard_map/slice | solution.py:272
  1.6 0.5 %collective-permute-start = (bf16[256,512]{1,0:T(8,128)(2,1)S(1)}, bf16[256,512]{1,0:T(8,128)(2,1)S(1)}, u32[]{:S(2)}, u32[]{:S(2)}) collective-permute-start(bf16[256,512]{1,0:T(8,128)(2,1)S(1)} %slice_bitcast_fusion), channel_id=1, source_target_pairs={{0,8},{8,16},{16,24},{24,0},{1,9},{9,17},{17,25},{25,1},{2,10},{10... | collective-permute-start | bytes 786440 | tf_op jit(solution)/shard_map/ppermute | solution.py:272
  2.8 3.3 %local.1 = (bf16[2,256,512]{2,1,0:T(8,128)(2,1)S(1)}, bf16[512,512]{1,0:T(8,128)(2,1)S(1)}, f32[256,1024]{1,0:T(8,128)S(1)}, f32[256,512]{1,0:T(8,128)S(1)}, bf1...) custom-call(s32[1]{0:T(128)S(6)} %copy.18.lengths_ref, ...), custom_call_target="tpu_custom_call" | custom-call | flops 1073741824 | bytes 10485764 | tf_op jit(solution)/shard_map/local/pallas_call | solution.py:240
  6.0 2.0 %collective-permute-done.halo_ref = bf16[256,512]{1,0:T(8,128)(2,1)S(1)} collective-permute-done((bf16[256,512]{1,0:T(8,128)(2,1)S(1)}, bf16[256,512]{1,0:T(8,128)(2,1)S(1)}, u32[]{:S(2)}, u32[]{:S(2)}) %collective-permute-start) | collective-permute-done | bytes 262176 | tf_op jit(solution)/shard_map/ppermute | solution.py:272
  8.1 1.1 %partner.1 = (bf16[512,1024]{1,0:T(8,128)(2,1)S(1)}, bf16[4,512,128]{2,1,0:T(8,128)(2,1)S(1)}, bf16[2,256,256]{2,1,0:T(8,128)(2,1)S(1)}, bf16[2,8,160,128]{3,2,1,0:T(8,128)(2,1)S(1)}) custom-call(s32[1]{0:T(128)S(6)} %copy.18.lengths_ref, bf16[256,512]{1,0:T(8,128)(2,1)S(1)} %collective-permute-done.halo_ref, ...), custom_call_target="tpu_custom_call", output_to_operand_aliasing={{0}: (7, {}), {1}: (8, {})} | custom-call | flops 805306368 | bytes 9043972 | tf_op jit(solution)/shard_map/partner/pallas_call | solution.py:240
  9.2 0.6 %collective-permute-start.1 = (bf16[2,8,160,128]{3,2,1,0:T(8,128)(2,1)S(1)}, bf16[2,8,160,128]{3,2,1,0:T(8,128)(2,1)S(1)}, u32[]{:S(2)}, u32[]{:S(2)}) collective-permute-start(bf16[2,8,160,128]{3,2,1,0:T(8,128)(2,1)S(1)} %get-tuple-element.45), channel_id=1, source_target_pairs={{0,8},{1,9},{2,10},{3,11},{4,12},{5,13},{6,14},{7,15},{8,0},{9,1},... | collective-permute-start | bytes 1966088 | tf_op jit(solution)/shard_map/ppermute | solution.py:270
  9.9 0.5 %terms01.1 = bf16[2,8,160,128]{3,2,1,0:T(8,128)(2,1)S(1)} custom-call(bf16[2,256,512]{2,1,0:T(8,128)(2,1)S(1)} %get-tuple-element.37.xt_ref, bf16[2,256,256]{2,1,0:T(8,128)(2,1)S(1)} %get-tuple-element.46.ht_ref, bf16[512,512]{1,0:T(8,128)(2,1)S(1)} %get-tuple-element.38.ct_ref, bf16[512,1024]{1,0:T(8,128)(2,1)S(1)} %get-tuple-element.55.pg_ref, ...), custom_call_target="tpu_custom_call" | custom-call | flops 536870912 | bytes 3538944 | tf_op jit(solution)/shard_map/terms01/pallas_call | solution.py:240
  10.4 0.1 collective-permute-start.5
  10.5 0.5 %terms10.1.kept_ref = bf16[2,8,160,128]{3,2,1,0:T(8,128)(2,1)S(1)} custom-call(bf16[2,256,512]{2,1,0:T(8,128)(2,1)S(1)} %get-tuple-element.37.xt_ref, bf16[2,256,256]{2,1,0:T(8,128)(2,1)S(1)} %get-tuple-element.46.ht_ref, bf16[512,512]{1,0:T(8,128)(2,1)S(1)} %get-tuple-element.38.ct_ref, bf16[512,1024]{1,0:T(8,128)(2,1)S(1)} %get-tuple-element.55.pg_ref, ...), custom_call_target="tpu_custom_call" | custom-call | flops 536870912 | bytes 3538944 | tf_op jit(solution)/shard_map/terms10/pallas_call | solution.py:240
  11.0 0.6 %collective-permute-done.1.got_ref = bf16[2,8,160,128]{3,2,1,0:T(8,128)(2,1)S(1)} collective-permute-done((bf16[2,8,160,128]{3,2,1,0:T(8,128)(2,1)S(1)}, bf16[2,8,160,128]{3,2,1,0:T(8,128)(2,1)S(1)}, u32[]{:S(2)}, u32[]{:S(2)}) %collective-permute-start.1) | collective-permute-done | bytes 655392 | tf_op jit(solution)/shard_map/ppermute | solution.py:270
  11.6 0.2 split1.1
  11.8 2.2 %collective-permute-start.2 = (bf16[8,160,128]{2,1,0:T(8,128)(2,1)S(1)}, bf16[8,160,128]{2,1,0:T(8,128)(2,1)S(1)}, u32[]{:S(2)}, u32[]{:S(2)}) collective-permute-start(bf16[8,160,128]{2,1,0:T(8,128)(2,1)S(1)} %get-tuple-element.48), channel_id=1, source_target_pairs={{0,16},{1,17},{2,18},{3,19},{4,20},{5,21},{6,22},{7,23},{8,9},{9,8... | collective-permute-start | bytes 983048 | tf_op jit(solution)/shard_map/ppermute | solution.py:287
  13.9 0.5 %terms00.1.kept_ref = bf16[2,8,160,128]{3,2,1,0:T(8,128)(2,1)S(1)} custom-call(bf16[2,256,512]{2,1,0:T(8,128)(2,1)S(1)} %get-tuple-element.37.xt_ref, bf16[2,256,256]{2,1,0:T(8,128)(2,1)S(1)} %get-tuple-element.46.ht_ref, bf16[512,512]{1,0:T(8,128)(2,1)S(1)} %get-tuple-element.38.ct_ref, bf16[512,1024]{1,0:T(8,128)(2,1)S(1)} %get-tuple-element.55.pg_ref, ...), custom_call_target="tpu_custom_call" | custom-call | flops 536870912 | bytes 3538944 | tf_op jit(solution)/shard_map/terms00/pallas_call | solution.py:240
  14.4 0.0 collective-permute-done.5.got_ref
  14.4 0.2 split0.1
  14.6 0.2 collective-permute-start.6
  14.9 4.1 %collective-permute-done.2.got_ref = bf16[8,160,128]{2,1,0:T(8,128)(2,1)S(1)} collective-permute-done((bf16[8,160,128]{2,1,0:T(8,128)(2,1)S(1)}, bf16[8,160,128]{2,1,0:T(8,128)(2,1)S(1)}, u32[]{:S(2)}, u32[]{:S(2)}) %collective-permute-start.2) | collective-permute-done | bytes 327712 | tf_op jit(solution)/shard_map/ppermute | solution.py:287
  19.0 0.1 half1.1
  19.1 2.1 %collective-permute-start.3 = (bf16[4,160,128]{2,1,0:T(8,128)(2,1)S(1)}, bf16[4,160,128]{2,1,0:T(8,128)(2,1)S(1)}, u32[]{:S(2)}, u32[]{:S(2)}) collective-permute-start(bf16[4,160,128]{2,1,0:T(8,128)(2,1)S(1)} %get-tuple-element.54), channel_id=1, source_target_pairs={{0,1},{1,0},{2,3},{3,2},{4,5},{5,4},{6,7},{7,6},{8,24},{9,25},{10,... | collective-permute-start | bytes 491528 | tf_op jit(solution)/shard_map/ppermute | solution.py:287
  21.2 1.3 %collective-permute-done.6.got_ref = bf16[8,160,128]{2,1,0:T(8,128)(2,1)S(1)} collective-permute-done((bf16[8,160,128]{2,1,0:T(8,128)(2,1)S(1)}, bf16[8,160,128]{2,1,0:T(8,128)(2,1)S(1)}, u32[]{:S(2)}, u32[]{:S(2)}) %collective-permute-start.6) | collective-permute-done | bytes 327712 | tf_op jit(solution)/shard_map/ppermute | solution.py:287
  22.5 0.1 half0.1
  22.6 2.2 %collective-permute-start.7 = (bf16[4,160,128]{2,1,0:T(8,128)(2,1)S(1)}, bf16[4,160,128]{2,1,0:T(8,128)(2,1)S(1)}, u32[]{:S(2)}, u32[]{:S(2)}) collective-permute-start(bf16[4,160,128]{2,1,0:T(8,128)(2,1)S(1)} %get-tuple-element.59), channel_id=1, source_target_pairs={{0,1},{1,0},{2,3},{3,2},{4,5},{5,4},{6,7},{7,6},{8,24},{9,25},{10,... | collective-permute-start | bytes 491528 | tf_op jit(solution)/shard_map/ppermute | solution.py:287
  24.8 0.0 collective-permute-done.3.refs_2_
  24.8 0.5 %back.1 = bf16[256,512]{1,0:T(8,128)(2,1)S(1)} custom-call(bf16[512,1024]{1,0:T(8,128)(2,1)S(1)} %get-tuple-element.55.pg_ref, bf16[1024,1024]{1,0:T(8,128)(2,1)S(1)} %get-tuple-element.36.wc_ref, bf16[256,512]{1,0:T(8,128)(2,1)S(1)} %get-tuple-element.56.back_in), custom_call_target="tpu_custom_call", output_to_operand_aliasing={{}: (2, {})} | custom-call | flops 268435456 | bytes 3670016 | tf_op jit(solution)/shard_map/back/pallas_call | solution.py:240
  25.3 0.7 %collective-permute-start.4 = (bf16[256,512]{1,0:T(8,128)(2,1)S(1)}, bf16[256,512]{1,0:T(8,128)(2,1)S(1)}, u32[]{:S(2)}, u32[]{:S(2)}) collective-permute-start(bf16[256,512]{1,0:T(8,128)(2,1)S(1)} %back.1), channel_id=1, source_target_pairs={{8,0},{16,8},{24,16},{0,24},{9,1},{17,9},{25,17},{1,25},{10,2},{18... | collective-permute-start | bytes 786440 | tf_op jit(solution)/shard_map/ppermute | solution.py:338
  26.0 2.1 %collective-permute-done.7.refs_0_ = bf16[4,160,128]{2,1,0:T(8,128)(2,1)S(1)} collective-permute-done((bf16[4,160,128]{2,1,0:T(8,128)(2,1)S(1)}, bf16[4,160,128]{2,1,0:T(8,128)(2,1)S(1)}, u32[]{:S(2)}, u32[]{:S(2)}) %collective-permute-start.7) | collective-permute-done | bytes 163872 | tf_op jit(solution)/shard_map/ppermute | solution.py:287
  28.1 0.1 far.1
  28.2 2.1 %collective-permute-start.8 = (bf16[320,128]{1,0:T(8,128)(2,1)S(1)}, bf16[320,128]{1,0:T(8,128)(2,1)S(1)}, u32[]{:S(2)}, u32[]{:S(2)}) collective-permute-start(bf16[320,128]{1,0:T(8,128)(2,1)S(1)} %get-tuple-element.62), channel_id=1, source_target_pairs={{0,2},{1,3},{2,4},{3,5},{4,6},{5,7},{6,0},{7,1},{8,10},{9,11},{10,... | collective-permute-start | bytes 245768 | tf_op jit(solution)/shard_map/ppermute | solution.py:345
  30.3 2.6 %collective-permute-start.9 = (bf16[320,128]{1,0:T(8,128)(2,1)S(1)}, bf16[320,128]{1,0:T(8,128)(2,1)S(1)}, u32[]{:S(2)}, u32[]{:S(2)}) collective-permute-start(bf16[320,128]{1,0:T(8,128)(2,1)S(1)} %get-tuple-element.64), channel_id=1, source_target_pairs={{0,4},{1,5},{2,6},{3,7},{4,0},{5,1},{6,2},{7,3},{8,12},{9,13},{10,... | collective-permute-start | bytes 245768 | tf_op jit(solution)/shard_map/ppermute | solution.py:345
  32.9 1.4 %collective-permute-start.10 = (bf16[320,128]{1,0:T(8,128)(2,1)S(1)}, bf16[320,128]{1,0:T(8,128)(2,1)S(1)}, u32[]{:S(2)}, u32[]{:S(2)}) collective-permute-start(bf16[320,128]{1,0:T(8,128)(2,1)S(1)} %get-tuple-element.65), channel_id=1, source_target_pairs={{0,6},{1,7},{2,0},{3,1},{4,2},{5,3},{6,4},{7,5},{8,14},{9,15},{10,... | collective-permute-start | bytes 245768 | tf_op jit(solution)/shard_map/ppermute | solution.py:345
  34.3 1.0 %input.1 = (bf16[256,512]{1,0:T(8,128)(2,1)S(1)}, f32[256,512]{1,0:T(8,128)S(1)}) custom-call(bf16[512,1024]{1,0:T(8,128)(2,1)S(1)} %get-tuple-element.55.pg_ref, bf16[1024,1024]{1,0:T(8,128)(2,1)S(1)} %get-tuple-element.36.wc_ref, bf16[512,512]{1,0:T(8,128)(2,1)S(1)} %get-tuple-element.44.c_ref, ...), custom_call_target="tpu_custom_call", output_to_operand_aliasing={{0}: (3, {}), {1}: (4, {})} | custom-call | flops 1073741824 | bytes 5242880 | tf_op jit(solution)/shard_map/input/pallas_call | solution.py:240
  35.3 0.0 collective-permute-done.4.arrived_ref
  35.3 0.9 %rows.1 = bf16[512,512]{1,0:T(8,128)(2,1)} custom-call(bf16[256,512]{1,0:T(8,128)(2,1)S(1)} %get-tuple-element.52.lo_ref, f32[256,512]{1,0:T(8,128)S(1)} %get-tuple-element.53.hi_ref, bf16[256,512]{1,0:T(8,128)(2,1)S(1)} %collective-permute-done.4.arrived_ref), custom_call_target="tpu_custom_call" | custom-call | flops 262144 | bytes 1572864 | tf_op jit(solution)/shard_map/rows/pallas_call | solution.py:240
  36.2 0.0 collective-permute-done.8.refs_0_
  36.2 1.3 %collective-permute-done.9.refs_1_ = bf16[320,128]{1,0:T(8,128)(2,1)S(1)} collective-permute-done((bf16[320,128]{1,0:T(8,128)(2,1)S(1)}, bf16[320,128]{1,0:T(8,128)(2,1)S(1)}, u32[]{:S(2)}, u32[]{:S(2)}) %collective-permute-start.9) | collective-permute-done | bytes 81952 | tf_op jit(solution)/shard_map/ppermute | solution.py:345
  37.5 0.5 %collective-permute-done.10.refs_2_ = bf16[320,128]{1,0:T(8,128)(2,1)S(1)} collective-permute-done((bf16[320,128]{1,0:T(8,128)(2,1)S(1)}, bf16[320,128]{1,0:T(8,128)(2,1)S(1)}, u32[]{:S(2)}, u32[]{:S(2)}) %collective-permute-start.10) | collective-permute-done | bytes 81952 | tf_op jit(solution)/shard_map/ppermute | solution.py:345
  37.9 0.7 %final.1 = (f32[256,128]{1,0:T(8,128)}, f32[64,128]{1,0:T(8,128)}) custom-call(bf16[320,128]{1,0:T(8,128)(2,1)S(1)} %collective-permute-done.8.refs_0_, bf16[320,128]{1,0:T(8,128)(2,1)S(1)} %collective-permute-done.9.refs_1_, bf16[320,128]{1,0:T(8,128)(2,1)S(1)} %collective-permute-done.10.refs_2_, bf16[320,128]{1,0:T(8,128)(2,1)S(1)} %get-tuple-element.66.refs_3_), custom_call_target="tpu_custom_call" | custom-call | flops 327680 | bytes 491520 | tf_op jit(solution)/shard_map/final/pallas_call | solution.py:240
Async XLA Ops:
  1.6 6.5 %collective-permute-start = (bf16[256,512]{1,0:T(8,128)(2,1)S(1)}, bf16[256,512]{1,0:T(8,128)(2,1)S(1)}, u32[]{:S(2)}, u32[]{:S(2)}) collective-permute-start(bf16[256,512]{1,0:T(8,128)(2,1)S(1)} %slice_bitcast_fusion), channel_id=1, source_target_pairs={{0,8},{8,16},{16,24},{24,0},{1,9},{9,17},{17,25},{25,1},{2,10},{10... | collective-permute-start | bytes 786440 | tf_op jit(solution)/shard_map/ppermute | solution.py:272
  9.2 2.4 %collective-permute-start.1 = (bf16[2,8,160,128]{3,2,1,0:T(8,128)(2,1)S(1)}, bf16[2,8,160,128]{3,2,1,0:T(8,128)(2,1)S(1)}, u32[]{:S(2)}, u32[]{:S(2)}) collective-permute-start(bf16[2,8,160,128]{3,2,1,0:T(8,128)(2,1)S(1)} %get-tuple-element.45), channel_id=1, source_target_pairs={{0,8},{1,9},{2,10},{3,11},{4,12},{5,13},{6,14},{7,15},{8,0},{9,1},... | collective-permute-start | bytes 1966088 | tf_op jit(solution)/shard_map/ppermute | solution.py:270
  10.4 4.0 %collective-permute-start.5 = (bf16[2,8,160,128]{3,2,1,0:T(8,128)(2,1)S(1)}, bf16[2,8,160,128]{3,2,1,0:T(8,128)(2,1)S(1)}, u32[]{:S(2)}, u32[]{:S(2)}) collective-permute-start(bf16[2,8,160,128]{3,2,1,0:T(8,128)(2,1)S(1)} %terms01.1), channel_id=1, source_target_pairs={{0,8},{1,9},{2,10},{3,11},{4,12},{5,13},{6,14},{7,15},{8,0},{9,1},... | collective-permute-start | bytes 1966088 | tf_op jit(solution)/shard_map/ppermute | solution.py:270
  11.8 7.2 %collective-permute-start.2 = (bf16[8,160,128]{2,1,0:T(8,128)(2,1)S(1)}, bf16[8,160,128]{2,1,0:T(8,128)(2,1)S(1)}, u32[]{:S(2)}, u32[]{:S(2)}) collective-permute-start(bf16[8,160,128]{2,1,0:T(8,128)(2,1)S(1)} %get-tuple-element.48), channel_id=1, source_target_pairs={{0,16},{1,17},{2,18},{3,19},{4,20},{5,21},{6,22},{7,23},{8,9},{9,8... | collective-permute-start | bytes 983048 | tf_op jit(solution)/shard_map/ppermute | solution.py:287
  14.6 7.9 %collective-permute-start.6 = (bf16[8,160,128]{2,1,0:T(8,128)(2,1)S(1)}, bf16[8,160,128]{2,1,0:T(8,128)(2,1)S(1)}, u32[]{:S(2)}, u32[]{:S(2)}) collective-permute-start(bf16[8,160,128]{2,1,0:T(8,128)(2,1)S(1)} %get-tuple-element.57), channel_id=1, source_target_pairs={{0,16},{1,17},{2,18},{3,19},{4,20},{5,21},{6,22},{7,23},{8,9},{9,8... | collective-permute-start | bytes 983048 | tf_op jit(solution)/shard_map/ppermute | solution.py:287
  19.1 5.8 %collective-permute-start.3 = (bf16[4,160,128]{2,1,0:T(8,128)(2,1)S(1)}, bf16[4,160,128]{2,1,0:T(8,128)(2,1)S(1)}, u32[]{:S(2)}, u32[]{:S(2)}) collective-permute-start(bf16[4,160,128]{2,1,0:T(8,128)(2,1)S(1)} %get-tuple-element.54), channel_id=1, source_target_pairs={{0,1},{1,0},{2,3},{3,2},{4,5},{5,4},{6,7},{7,6},{8,24},{9,25},{10,... | collective-permute-start | bytes 491528 | tf_op jit(solution)/shard_map/ppermute | solution.py:287
  22.6 5.5 %collective-permute-start.7 = (bf16[4,160,128]{2,1,0:T(8,128)(2,1)S(1)}, bf16[4,160,128]{2,1,0:T(8,128)(2,1)S(1)}, u32[]{:S(2)}, u32[]{:S(2)}) collective-permute-start(bf16[4,160,128]{2,1,0:T(8,128)(2,1)S(1)} %get-tuple-element.59), channel_id=1, source_target_pairs={{0,1},{1,0},{2,3},{3,2},{4,5},{5,4},{6,7},{7,6},{8,24},{9,25},{10,... | collective-permute-start | bytes 491528 | tf_op jit(solution)/shard_map/ppermute | solution.py:287
  25.3 10.0 %collective-permute-start.4 = (bf16[256,512]{1,0:T(8,128)(2,1)S(1)}, bf16[256,512]{1,0:T(8,128)(2,1)S(1)}, u32[]{:S(2)}, u32[]{:S(2)}) collective-permute-start(bf16[256,512]{1,0:T(8,128)(2,1)S(1)} %back.1), channel_id=1, source_target_pairs={{8,0},{16,8},{24,16},{0,24},{9,1},{17,9},{25,17},{1,25},{10,2},{18... | collective-permute-start | bytes 786440 | tf_op jit(solution)/shard_map/ppermute | solution.py:338
  28.2 8.0 %collective-permute-start.8 = (bf16[320,128]{1,0:T(8,128)(2,1)S(1)}, bf16[320,128]{1,0:T(8,128)(2,1)S(1)}, u32[]{:S(2)}, u32[]{:S(2)}) collective-permute-start(bf16[320,128]{1,0:T(8,128)(2,1)S(1)} %get-tuple-element.62), channel_id=1, source_target_pairs={{0,2},{1,3},{2,4},{3,5},{4,6},{5,7},{6,0},{7,1},{8,10},{9,11},{10,... | collective-permute-start | bytes 245768 | tf_op jit(solution)/shard_map/ppermute | solution.py:345
  30.3 7.1 %collective-permute-start.9 = (bf16[320,128]{1,0:T(8,128)(2,1)S(1)}, bf16[320,128]{1,0:T(8,128)(2,1)S(1)}, u32[]{:S(2)}, u32[]{:S(2)}) collective-permute-start(bf16[320,128]{1,0:T(8,128)(2,1)S(1)} %get-tuple-element.64), channel_id=1, source_target_pairs={{0,4},{1,5},{2,6},{3,7},{4,0},{5,1},{6,2},{7,3},{8,12},{9,13},{10,... | collective-permute-start | bytes 245768 | tf_op jit(solution)/shard_map/ppermute | solution.py:345
  32.9 5.0 %collective-permute-start.10 = (bf16[320,128]{1,0:T(8,128)(2,1)S(1)}, bf16[320,128]{1,0:T(8,128)(2,1)S(1)}, u32[]{:S(2)}, u32[]{:S(2)}) collective-permute-start(bf16[320,128]{1,0:T(8,128)(2,1)S(1)} %get-tuple-element.65), channel_id=1, source_target_pairs={{0,6},{1,7},{2,0},{3,1},{4,2},{5,3},{6,4},{7,5},{8,14},{9,15},{10,... | collective-permute-start | bytes 245768 | tf_op jit(solution)/shard_map/ppermute | solution.py:345
